TPU v7x, 32 devices: a whole 2x2x4 slice. The times are simulated.
32 devices in a mesh: wide: 8 (over z, x), narrow: 4 (over y, core).
Axes of the slice: x: 2, y: 2, z: 4, core: 2. Of those that a mesh axis runs over, the one named last changes fastest.
Arguments:
- tokens: bfloat16 [2, 2, 1152, 8192], P(None, None, 'narrow', 'wide')
- ada_weight: bfloat16 [1152, 6, 1152], P('wide', None, 'narrow'), may hold values from -0.1875 to 0.1875
- ada_bias: bfloat16 [6, 1152], P(None, 'narrow'), may hold values from -3 to 3
- class_table: bfloat16 [101, 1152], replicated, may hold values from -6 to 6
- query_weight: bfloat16 [1152, 1152], P('wide', 'narrow'), may hold values from -0.1875 to 0.1875
- key_weight: bfloat16 [1152, 1152], P('wide', 'narrow'), may hold values from -0.1875 to 0.1875
- value_weight: bfloat16 [1152, 1152], P('wide', 'narrow'), may hold values from -0.1875 to 0.1875
- out_weight: bfloat16 [1152, 1152], P('narrow', 'wide'), may hold values from -0.375 to 0.375
- up_weight: bfloat16 [1152, 4608], P('wide', 'narrow')
- up_bias: bfloat16 [4608], P('narrow'), may hold values from -3 to 3
- down_weight: bfloat16 [4608, 1152], P('narrow', 'wide'), may hold values from -0.09375 to 0.09375
- down_bias: bfloat16 [1152], P('narrow'), may hold values from -3 to 3
- cotangent: bfloat16 [2, 2, 1152, 8192], P(None, None, 'narrow', 'wide'), may hold values from -6 to 6
- clip_frames: int32 [2, 2], replicated, may hold values from 1 to 16, as said below
- time_ids: int32 [2, 2], replicated, may hold values from 0 to 999
- class_ids: int32 [2, 2], replicated, may hold values from 0 to 100
Outputs:
- output: bfloat16 [2, 2, 1152, 8192], P(None, None, 'narrow', 'wide')
- input_grad: float32 [2, 2, 1152, 8192], P(None, None, 'narrow', 'wide')
- ada_weight_grad: float32 [1152, 6, 1152], P('wide', None, 'narrow')
- ada_bias_grad: float32 [6, 1152], P(None, 'narrow')
- class_table_grad: float32 [101, 1152], replicated
- query_weight_grad: float32 [1152, 1152], P('wide', 'narrow')
- key_weight_grad: float32 [1152, 1152], P('wide', 'narrow')
- value_weight_grad: float32 [1152, 1152], P('wide', 'narrow')
- out_weight_grad: float32 [1152, 1152], P('narrow', 'wide')
- up_weight_grad: float32 [1152, 4608], P('wide', 'narrow')
- up_bias_grad: float32 [4608], P('narrow')
- down_weight_grad: float32 [4608, 1152], P('narrow', 'wide')
- down_bias_grad: float32 [1152], P('narrow')
Inputs may be any that keep to these rules, and one draw needn't show every extreme that they name: Frames of a sequence at or after its clip_frames are single images. Some sequence of the first micro-batch is a clip of all 16 frames and some sequence of the last micro-batch has clip_frames 1.
All inputs are finite; a program needn't handle non-finite values.
Results may differ from a plain program's by a relative error of at most 0.02.
Values may be sent and summed in bfloat16 or wider, within the bound.
No kernel may reach another device: no remote copies, remote signals or barrier semaphores. Data moves between devices by JAX's collectives and lax.ppermute only.
A program may use at most 256 MiB of HBM per device.

v0:
```python
import functools
import math

import jax
import jax.numpy as jnp
from jax import lax
from jax.experimental import pallas as pl
from jax.experimental.pallas import tpu as pltpu
from jax.sharding import PartitionSpec as P

HEAD_DIM = 72
FRAMES = 16
BLOCK = 128
MIB = 1024 * 1024
COSTS = {
    "project_qkv": 15,
    "attention_forward": 24,
    "project_out": 17,
    "project_up": 28,
    "project_down": 25,
    "down_weight_grad": 10,
    "up_weight_grad": 10,
    "first_weight_grad": 12,
    "hidden_backward": 21,
    "middle_backward": 30,
    "attended_backward": 9,
    "attention_backward": 33,
    "input_backward": 25,
}
COST_SCALE = 1e8

norm_epsilon = 1e-06
masked_score = -1e30
both = ("wide", "narrow")
low = jnp.bfloat16
high = jnp.float32


def time_embedding(time_ids, full_width):
    half_width = full_width // 2
    frequency = jnp.exp(-math.log(10000.0) * jnp.arange(half_width, dtype=jnp.float32) / half_width)
    angles = time_ids.astype(jnp.float32)[..., None] * frequency
    return jnp.concatenate([jnp.cos(angles), jnp.sin(angles)], axis=-1)


def place():
    deep, tall = lax.axis_size("wide") // 2, lax.axis_size("narrow") // 2
    wide_at, narrow_at = lax.axis_index("wide"), lax.axis_index("narrow")
    return deep, tall, wide_at // 2, wide_at % 2, narrow_at // 2, narrow_at % 2


def send(value, deep_by=0, side_by=0, tall_by=0, core_by=0):
    deep, tall = lax.axis_size("wide") // 2, lax.axis_size("narrow") // 2
    pairs = []
    for z in range(deep):
        for x in range(2):
            for y in range(tall):
                for c in range(2):
                    source = ((z * 2 + x) * tall + y) * 2 + c
                    target = (
                        ((z + deep_by) % deep * 2 + (x + side_by) % 2) * tall + (y + tall_by) % tall
                    ) * 2 + (c + core_by) % 2
                    pairs.append((source, target))
    return lax.ppermute(value, both, pairs)


def after(value, *earlier):
    return lax.optimization_barrier((value, earlier))[0]


def sync(*values):
    arrays = []
    for value in values:
        if isinstance(value, GradSum):
            arrays += [array for array, _ in value.terms]
        elif isinstance(value, (list, tuple)):
            arrays += value
        else:
            arrays.append(value)
    arrays = iter(lax.optimization_barrier(tuple(arrays)))
    results = []
    for value in values:
        if isinstance(value, GradSum):
            value.terms = [(next(arrays), cuts) for _, cuts in value.terms]
            results.append(value)
        elif isinstance(value, (list, tuple)):
            results.append([next(arrays) for _ in value])
        else:
            results.append(next(arrays))
    return results


class Gather:
    def __init__(self, piece):
        self.deep = lax.axis_size("wide") // 2
        self.tall = lax.axis_size("narrow") // 2
        self.ring = [piece]
        self.rows = piece.shape[0]

    def step(self):
        self.ring.append(send(self.ring[-1], deep_by=1))

    def front_side(self):
        self.front = jnp.concatenate(self.ring[: self.deep // 2], axis=0)
        self.front_got = [send(self.front, side_by=1)]

    def rear_tall(self):
        self.rear = jnp.concatenate(self.ring[self.deep // 2 :], axis=0)
        self.rear_got = [send(self.rear, tall_by=k) for k in range(1, self.tall)]

    def second(self):
        self.front = jnp.concatenate([self.front] + self.front_got, axis=0)
        self.rear = jnp.concatenate([self.rear] + self.rear_got, axis=0)
        self.arrays = [self.rear, send(self.rear, side_by=1), self.front]
        self.arrays += [send(self.front, tall_by=k) for k in range(1, self.tall)]
        self.cores = [None] * len(self.arrays)

    def core(self, *at):
        for k in at:
            self.cores[k] = send(self.arrays[k], core_by=1)

    def result(self):
        count = len(self.arrays)
        near = self.deep // 2 * self.rows
        far = self.deep * self.rows - near
        panels = []
        for c in range(2):
            for y in range(self.tall):
                panels.append(
                    [
                        (c * count + 2 + y, (), 0, 0, near),
                        (c * count, (), y * far, near, far),
                        (c * count + 2 + y, (), near, near + far, near),
                        (c * count + 1, (), y * far, 2 * near + far, far),
                    ]
                )
        return self.arrays + self.cores, panels


class LateGather:
    def __init__(self, piece):
        self.deep = lax.axis_size("wide") // 2
        self.tall = lax.axis_size("narrow") // 2
        self.piece = piece
        self.cores = []

    def side(self):
        self.line = [self.piece, send(self.piece, side_by=1)]

    def along_tall(self):
        line = jnp.stack(self.line)
        self.plane = [line] + [send(line, tall_by=k) for k in range(1, self.tall)]

    def step(self):
        if not hasattr(self, "ring"):
            self.ring = [jnp.stack(self.plane)]
        self.ring.append(send(self.ring[-1], deep_by=1))

    def core(self, *at):
        self.cores += [send(self.ring[k], core_by=1) for k in at]

    def result(self):
        tall, deep, rows = self.tall, self.deep, self.piece.shape[0]
        arrays = self.ring + self.cores
        if rows % 16:
            whole = [
                jnp.concatenate([arrays[c * deep + k][y, x] for x in range(2) for k in range(deep)])
                for c in range(2)
                for y in range(tall)
            ]
            return whole, [[(at, (), 0, 0, 2 * deep * rows)] for at in range(2 * tall)]
        panels = [
            [
                (c * deep + k, (y, x), 0, (x * deep + k) * rows, rows)
                for x in range(2)
                for k in range(deep)
            ]
            for c in range(2)
            for y in range(tall)
        ]
        return arrays, panels


def device_order():
    deep, tall, z, x, y, c = place()
    order = []
    for core in range(2):
        for k in range(tall):
            n = (y - k) % tall * 2 + (c - core) % 2
            for side in range(2):
                for far in range(deep):
                    w = (z - far) % deep * 2 + (x - side) % 2
                    order.append(w * 2 * tall + n)
    return jnp.stack(order).astype(jnp.int32)


class GradSum:
    def __init__(self, other):
        self.sizes = {"x": 2, "y": lax.axis_size("narrow") // 2, "z": lax.axis_size("wide") // 2}
        self.got = send(other, core_by=-1)

    def near(self, near):
        _, tall, rows, columns = near.shape
        deep = self.sizes["z"]
        shape = (2, tall, deep, rows // deep, columns)
        self.terms = [(near.reshape(shape), ()), (self.got.reshape(shape), ())]
        self.axes = "xyz"

    def copy(self, cuts):
        one = GradSum.__new__(GradSum)
        one.sizes, one.axes = dict(self.sizes), self.axes
        one.terms = [(array, earlier + cuts) for array, earlier in self.terms]
        return one

    def split(self, *ends):
        parts = []
        for start, end in zip((0, *ends), (*ends, self.sizes["z"])):
            part = self.copy((self.at("z", slice(start, end)),))
            part.sizes["z"] = end - start
            parts.append(part)
        return parts

    def at(self, axis, k):
        return (slice(None),) * self.axes.index(axis) + (k,)

    def hold(self, *earlier):
        self.terms = [(after(array, *earlier), cuts) for array, cuts in self.terms]
        return self

    def total(self, *cuts):
        total = 0.0
        for array, earlier in self.terms:
            for one in earlier + cuts:
                array = array[one]
            total = total + array.astype(high)
        return total

    def sums(self, axis):
        return [self.total(self.at(axis, k)).astype(low) for k in range(1, self.sizes[axis])]

    def along(self, axis, sums, *earlier):
        by = {"x": "side_by", "y": "tall_by", "z": "deep_by"}[axis]
        gots = [send(after(v, *earlier), **{by: -k}) for k, v in enumerate(sums, 1)]
        self.receive(axis, gots)
        return gots

    def receive(self, axis, gots):
        own = self.at(axis, 0)
        self.terms = [(array, cuts + (own,)) for array, cuts in self.terms] + [(v, ()) for v in gots]
        self.axes = self.axes.replace(axis, "")


def deep_sums(parts):
    return [
        part.total(part.at("z", k)).astype(low) for part in parts for k in range(part.sizes["z"])
    ][1:]


def along_deep(parts, sums, *earlier):
    first = parts[0]
    gots = [send(after(v, *earlier), deep_by=-k) for k, v in enumerate(sums, 1)]
    first.receive("z", gots)
    return gots


def swap_narrow(parts):
    return lax.all_to_all(parts, "narrow", 0, 0, tiled=True)


class NarrowSwap:
    def __init__(self, parts):
        self.tall = lax.axis_size("narrow") // 2
        self.parts = parts
        _, _, _, _, self.y, self.c = place()
        self.own = [self.pick(0, core) for core in range(2)]

    def pick(self, k, core):
        target = (self.y + k) % self.tall * 2 + (self.c + core) % 2
        part = self.parts.shape[2] // (2 * self.tall)
        return lax.dynamic_slice_in_dim(self.parts, target * part, part, axis=2)[None]

    def step(self, core):
        return [send(self.pick(k, core), tall_by=k) for k in range(1, self.tall)]

    def pieces(self, same, other):
        other = send(jnp.concatenate([self.own[1]] + other, axis=0), core_by=1)
        return [self.own[0]] + same, other


def orders():
    deep, tall, z, x, y, c = place()
    wide_count, narrow_count = 2 * deep, 2 * tall
    ratio = wide_count // narrow_count

    def stands(n, h):
        w = n * ratio + h
        return (x - w % 2) % 2 * deep + (z - w // 2) % deep

    there = [stands(n, h) for n in range(narrow_count) for h in range(ratio)]
    came, goes = [], []
    for core_by in range(2):
        for tall_by in range(tall):
            source = (y - tall_by) % tall * 2 + (c - core_by) % 2
            target = (y + tall_by) % tall * 2 + (c + core_by) % 2
            came += [stands(source, h) for h in range(ratio)]
            goes += [stands(target, h) for h in range(ratio)]
    return [jnp.stack(v).astype(jnp.int32) for v in (there, came, goes)]


def sum_wide(value):
    deep = lax.axis_size("wide") // 2
    value = value + send(value, side_by=1)
    step = 1
    while step < deep:
        value = value + send(value, deep_by=step)
        step *= 2
    return value


def sum_narrow(value):
    tall = lax.axis_size("narrow") // 2
    value = value + send(value, core_by=1)
    step = 1
    while step < tall:
        value = value + send(value, tall_by=step)
        step *= 2
    return value


def gather_narrow(value):
    tall = lax.axis_size("narrow") // 2
    own = jnp.stack([value] + [send(value, tall_by=k) for k in range(1, tall)])
    return jnp.concatenate([own, send(own, core_by=1)])


def scatter_narrow(value):
    tall = lax.axis_size("narrow") // 2
    value = value.reshape(2, tall, *value.shape[1:])
    total = value[0] + send(value[1], core_by=1)
    return sum([total[0]] + [send(total[k], tall_by=k) for k in range(1, tall)])


def contract(left, right, left_dim, right_dim):
    return lax.dot_general(
        left, right, (((left_dim,), (right_dim,)), ((), ())), preferred_element_type=jnp.float32
    )


def call(kernel, name, grid, ins, outs, scratch=(), prefetch=(), vmem=60):
    in_specs = []
    for array, block, index in ins:
        if block == "any":
            in_specs.append(pl.BlockSpec(memory_space=pl.ANY))
        elif block is None:
            in_specs.append(pl.BlockSpec(array.shape, lambda *_, r=array.ndim: (0,) * r))
        else:
            in_specs.append(pl.BlockSpec(block, index))
    out_specs = []
    for shape, _, block, index in outs:
        if block is None:
            out_specs.append(pl.BlockSpec(shape, lambda *_, r=len(shape): (0,) * r))
        else:
            out_specs.append(pl.BlockSpec(block, index))
    return pl.pallas_call(
        kernel,
        grid_spec=pltpu.PrefetchScalarGridSpec(
            num_scalar_prefetch=len(prefetch),
            grid=grid,
            in_specs=in_specs,
            out_specs=out_specs,
            scratch_shapes=list(scratch),
        ),
        out_shape=[jax.ShapeDtypeStruct(shape, kind) for shape, kind, _, _ in outs],
        compiler_params=pltpu.CompilerParams(vmem_limit_bytes=vmem * MIB),
        cost_estimate=pl.CostEstimate(
            flops=int(COSTS.get(name, 4) * COST_SCALE), bytes_accessed=0, transcendentals=0
        ),
        name=name,
    )(*prefetch, *[array for array, _, _ in ins])


class Weights:
    def __init__(self, gathered, start=0, stop=None):
        self.arrays, self.panels = gathered
        self.columns = self.arrays[0].shape[-1]
        self.start, self.stop = start, self.columns if stop is None else stop
        self.rows = sum(size for *_, size in self.panels[0])
        self.prefetch = []

    def ins(self):
        return [(array, "any", None) for array in self.arrays]

    def scratch(self, wide=False):
        count, columns = len(self.panels), self.stop - self.start
        self.wide = wide and columns % BLOCK == 0
        return [
            pltpu.VMEM(
                (self.rows, count * columns) if self.wide else (count, self.rows, columns), low
            ),
            pltpu.SemaphoreType.DMA((count, len(self.panels[0]))),
        ]

    def source(self, refs, panel, piece):
        array, lead, begin, row, size = self.panels[panel][piece]
        source = refs[array].at[(*lead, pl.ds(begin, size), slice(self.start, self.stop))]
        return source, row, size

    def copies(self, refs, held, sems, panel):
        copies = []
        columns = self.stop - self.start
        for piece in range(len(self.panels[0])):
            source, row, size = self.source(refs, panel, piece)
            if self.wide:
                target = held.at[pl.ds(row, size), pl.ds(panel * columns, columns)]
            else:
                target = held.at[panel, pl.ds(row, size)]
            copies.append(pltpu.make_async_copy(source, target, sems.at[panel, piece]))
        return copies

    def start_all(self, refs, held, sems, at):
        @pl.when(at == 0)
        def _():
            for panel in range(len(self.panels)):
                for copy in self.copies(refs, held, sems, panel):
                    copy.start()

    def wait(self, refs, held, sems, at, panel, step=0):
        @pl.when(at == step)
        def _():
            for copy in self.copies(refs, held, sems, panel):
                copy.wait()

    def panel(self, refs, held, sems, at):
        self.start_all(refs, held, sems, at)
        for panel in range(len(self.panels)):
            self.wait(refs, held, sems, at, panel, panel)
        return held.at[at]


class GatheredWeights(Weights):
    def __init__(self, gathered, order, panel_count):
        devices, rows, columns = gathered.shape
        blocks = devices // panel_count
        if rows % 16:
            whole = jnp.take(gathered, order, axis=0).reshape(panel_count, blocks * rows, columns)
            super().__init__(([whole], [[(0, (p,), 0, 0, blocks * rows)] for p in range(panel_count)]))
            return
        panels = [
            [(p * blocks + b, (), 0, b * rows, rows) for b in range(blocks)]
            for p in range(panel_count)
        ]
        super().__init__(([gathered], panels))
        self.prefetch = [order]

    def source(self, refs, panel, piece):
        if not self.prefetch:
            return super().source(refs, panel, piece)
        at, _, _, row, size = self.panels[panel][piece]
        return refs[1].at[refs[0][at]], row, size


class Shape:
    def __init__(self, seqs, part, width, panels):
        self.seqs, self.part, self.width, self.panels = seqs, part, width, panels
        self.tokens = seqs * part
        self.block = part if part % BLOCK == 0 else self.tokens
        self.blocks = self.tokens // self.block
        self.share = self.block // part
        local = width // panels
        self.local = local
        self.qkv_rows = min(-(-3 * local // BLOCK) * BLOCK, 4 * local)
        self.out_from = 3 * local // BLOCK * BLOCK
        self.out_rows = 4 * local - self.out_from
        self.out_skip = 3 * local - self.out_from


def pick(table, at):
    lane = lax.broadcasted_iota(jnp.int32, table.shape, 1)
    return jnp.sum(jnp.where(lane == at, table, 0.0), axis=1, keepdims=True)


def spread(shape, table, slot, block):
    picked = [pick(table, slot * shape.seqs + block * shape.share + j) for j in range(shape.share)]
    if shape.share == 1:
        return picked[0]
    return jnp.concatenate(
        [jnp.broadcast_to(one, (one.shape[0], shape.part)) for one in picked], axis=1
    )


def seq_sums(shape, values):
    return [
        jnp.sum(values[:, j * shape.part : (j + 1) * shape.part], axis=1, keepdims=True)
        for j in range(shape.share)
    ]


def normed_rows(values):
    width = values.shape[0]
    center = jnp.sum(values, axis=0, keepdims=True) * (1.0 / width)
    shifted = values - center
    variance = jnp.sum(shifted * shifted, axis=0, keepdims=True) * (1.0 / width)
    inverse = lax.rsqrt(variance + norm_epsilon)
    return shifted * inverse, inverse


def norm_backward(grad_hat, normed, inverse):
    width = normed.shape[0]
    totals = jnp.sum(grad_hat, axis=0, keepdims=True) * (1.0 / width)
    crossed = jnp.sum(grad_hat * normed, axis=0, keepdims=True) * (1.0 / width)
    return inverse * (grad_hat - totals - normed * crossed)


def put_pieces(shape, at_ref, piece_refs, held):
    rows = held.shape[1]
    ratio = shape.local // rows
    for n in range(shape.panels):
        for h in range(ratio):
            for j in range(shape.share):
                ref, lead = (piece_refs[0], n) if len(piece_refs) == 1 else (piece_refs[n], 0)
                held[at_ref[n * ratio + h], :, j * shape.part : (j + 1) * shape.part] = ref[
                    lead, j, h * rows : (h + 1) * rows
                ].astype(high)


def take_pieces(shape, at_ref, held, pieces_ref):
    rows = held.shape[1]
    ratio = shape.local // rows
    for n in range(shape.panels):
        for h in range(ratio):
            for j in range(shape.share):
                pieces_ref[n, j, h * rows : (h + 1) * rows, :] = held[
                    at_ref[n * ratio + h], :, j * shape.part : (j + 1) * shape.part
                ].astype(pieces_ref.dtype)


def pieces_in(shape, pieces):
    if isinstance(pieces, list):
        block = (1, shape.share, shape.local, shape.part)
        return [(piece, block, lambda b, *_: (0, b, 0, 0)) for piece in pieces]
    return [pieces_by_device(shape, pieces)]


def pieces_by_device(shape, pieces):
    return (
        pieces,
        (shape.panels, shape.share, shape.local, shape.part),
        lambda b, *_: (0, b, 0, 0),
    )


def token_out(shape, kind):
    return (
        (shape.width, shape.tokens),
        kind,
        (shape.width, shape.block),
        lambda b, *_: (0, b),
    )


def prepare_tokens(shape, there, pieces, table, wide_count):
    def kernel(at_ref, *refs):
        *piece_refs, table_ref, whole_ref, input_ref, held = refs
        block = pl.program_id(0)
        put_pieces(shape, at_ref, piece_refs, held)
        values = held[...].reshape(shape.width, shape.block)
        normed, _ = normed_rows(values)
        table = table_ref[...]
        whole_ref[...] = values.astype(low)
        input_ref[...] = (
            normed * (1.0 + spread(shape, table, 1, block)) + spread(shape, table, 0, block)
        ).astype(low)

    return call(
        kernel,
        "prepare_tokens",
        (shape.blocks,),
        pieces_in(shape, pieces) + [(table, None, None)],
        [token_out(shape, low), token_out(shape, low)],
        [pltpu.VMEM((wide_count, shape.width // wide_count, shape.block), high)],
        [there],
    )


def prepare_upstream(shape, there, pieces, table, wide_count):
    def kernel(at_ref, pieces_ref, table_ref, whole_ref, grad_ref, bias_ref, held):
        block = pl.program_id(0)
        put_pieces(shape, at_ref, [pieces_ref], held)
        values = held[...].reshape(shape.width, shape.block)
        whole_ref[...] = values.astype(low)
        grad_low = (values * spread(shape, table_ref[...], 5, block)).astype(low)
        grad_ref[...] = grad_low
        total = jnp.sum(grad_low.astype(high), axis=1, keepdims=True)

        @pl.when(block == 0)
        def _():
            bias_ref[...] = total

        @pl.when(block > 0)
        def _():
            bias_ref[...] += total

    return call(
        kernel,
        "prepare_upstream",
        (shape.blocks,),
        pieces_in(shape, pieces) + [(table, None, None)],
        [token_out(shape, low), token_out(shape, low), ((shape.width, 1), high, None, None)],
        [pltpu.VMEM((wide_count, shape.width // wide_count, shape.block), high)],
        [there],
    )


def lay_small(shape, came, small, wide_count):
    rows = shape.width // wide_count
    ratio = shape.local // rows
    first = 6 * shape.seqs + 1
    count = small.shape[1]
    ups = count - first

    def kernel(at_ref, small_ref, table_ref, bias_ref, held):
        for p in range(shape.panels):
            turned = small_ref[p].T
            for h in range(ratio):
                held[at_ref[p * ratio + h]] = turned[h * rows : (h + 1) * rows]
            bias_ref[p] = jnp.concatenate(
                [turned[:, first + k : first + k + 1] for k in range(ups)], axis=0
            )
        table_ref[...] = held[...].reshape(shape.width, count)

    return call(
        kernel,
        "lay_small",
        (1,),
        [(small, None, None)],
        [
            ((shape.width, count), high, None, None),
            ((shape.panels, ups * shape.local, 1), high, None, None),
        ],
        [pltpu.VMEM((wide_count, rows, count), high)],
        [came],
    )


def lay_small_grads(shape, goes, late, middle, gate_two, down_bias, up_bias, wide_count):
    rows = shape.width // wide_count
    ratio = shape.local // rows
    seqs = shape.seqs
    ups = up_bias.shape[1] // shape.local
    count = 6 * seqs + 1 + ups

    def kernel(at_ref, late_ref, middle_ref, gate_ref, down_ref, up_ref, small_ref, held):
        table = jnp.concatenate(
            [late_ref[...], middle_ref[...], gate_ref[...], down_ref[...]], axis=1
        )
        held[...] = table.reshape(wide_count, rows, 6 * seqs + 1)
        for p in range(shape.panels):
            parts = [held[at_ref[p * ratio + h]] for h in range(ratio)]
            column = jnp.concatenate(parts, axis=0) if ratio > 1 else parts[0]
            bias = up_ref[p]
            column = jnp.concatenate(
                [column] + [bias[k * shape.local : (k + 1) * shape.local] for k in range(ups)],
                axis=1,
            )
            small_ref[p] = column.T

    return call(
        kernel,
        "lay_small_grads",
        (1,),
        [(v, None, None) for v in (late, middle, gate_two, down_bias, up_bias)],
        [((shape.panels, count, shape.local), high, None, None)],
        [pltpu.VMEM((wide_count, rows, 6 * seqs + 1), high)],
        [goes],
    )[0]


def cut_tokens(shape, local):
    def kernel(local_ref, out_ref):
        for n in range(shape.panels):
            out_ref[n, 0] = local_ref[0, :, n * shape.part : (n + 1) * shape.part]

    return call(
        kernel,
        "cut_tokens",
        (shape.seqs,),
        [(local, (1, *local.shape[1:]), lambda s, *_: (s, 0, 0))],
        [
            (
                (shape.panels, shape.seqs, shape.local, shape.part),
                low,
                (shape.panels, 1, shape.local, shape.part),
                lambda s, *_: (0, s, 0, 0),
            )
        ],
    )[0]


def join_tokens(shape, pieces, kind):
    def kernel(pieces_ref, out_ref):
        for n in range(shape.panels):
            out_ref[0, :, n * shape.part : (n + 1) * shape.part] = pieces_ref[n, 0].astype(kind)

    return call(
        kernel,
        "join_tokens",
        (shape.seqs,),
        [
            (
                pieces,
                (shape.panels, 1, shape.local, shape.part),
                lambda s, *_: (0, s, 0, 0),
            )
        ],
        [
            (
                (shape.seqs, shape.local, shape.panels * shape.part),
                kind,
                (1, shape.local, shape.panels * shape.part),
                lambda s, *_: (s, 0, 0),
            )
        ],
    )[0]


def by_panel(shape, rows, kind):
    return (
        (shape.panels, rows, shape.tokens),
        kind,
        (1, rows, shape.tokens),
        lambda n, *_: (n, 0, 0),
    )


def panel_in(array):
    return (array, (1, *array.shape[1:]), lambda n, *_: (n, 0, 0))


def project_qkv(shape, weights, source):
    order = weights.prefetch
    count = len(weights.arrays)

    def kernel(*refs):
        refs, order_refs = refs[len(order) :], refs[: len(order)]
        weight_refs, (source_ref, out_ref, held, sems) = refs[:count], refs[count:]
        panel = weights.panel((*order_refs, *weight_refs), held, sems, pl.program_id(0))
        out_ref[0] = contract(panel[...], source_ref[...], 0, 0).astype(low)

    return call(
        kernel,
        "project_qkv",
        (shape.panels,),
        weights.ins() + [(source, None, None)],
        [by_panel(shape, shape.qkv_rows, low)],
        weights.scratch(),
        prefetch=order,
    )[0]


def head_rows(block, head):
    return block[head * HEAD_DIM : (head + 1) * HEAD_DIM].astype(low)


def attention_forward(shape, qkv, in_clip):
    width = shape.local
    heads = width // HEAD_DIM
    blocks = shape.tokens // BLOCK
    score_scale = 1.0 / math.sqrt(HEAD_DIM)

    def kernel(qkv_ref, row_ref, column_ref, out_ref, probs_ref):
        rows_at = lax.broadcasted_iota(jnp.int32, (BLOCK, BLOCK), 0)
        columns_at = lax.broadcasted_iota(jnp.int32, (BLOCK, BLOCK), 1)
        allowed = (rows_at // FRAMES == columns_at // FRAMES) & (
            ((column_ref[...] > 0) & (row_ref[...] > 0)) | (rows_at == columns_at)
        )
        queries = qkv_ref[0, :width].astype(high)
        key_rows = qkv_ref[0, width : 2 * width].astype(high)
        value_rows = qkv_ref[0, 2 * width : 3 * width].astype(high)
        parts = [jnp.zeros((shape.out_skip, BLOCK), high)]
        for head in range(heads):
            scores = (
                contract(head_rows(key_rows, head), head_rows(queries, head), 0, 0) * score_scale
            )
            scores = jnp.where(allowed, scores, masked_score)
            exp_scores = jnp.exp(scores - jnp.max(scores, axis=0, keepdims=True))
            probs = exp_scores * (1.0 / jnp.sum(exp_scores, axis=0, keepdims=True))
            probs_low = probs.astype(low)
            probs_ref[0, 0, head] = probs_low
            parts.append(contract(head_rows(value_rows, head), probs_low, 1, 0))
        out_ref[0] = jnp.concatenate(parts, axis=0).astype(low)

    return call(
        kernel,
        "attention_forward",
        (blocks, shape.panels),
        [
            (qkv, (1, qkv.shape[1], BLOCK), lambda b, n: (n, 0, b)),
            (in_clip[None, :], (1, BLOCK), lambda b, n: (0, b)),
            (in_clip[:, None], (BLOCK, 1), lambda b, n: (b, 0)),
        ],
        [
            (
                (shape.panels, shape.out_rows, shape.tokens),
                low,
                (1, shape.out_rows, BLOCK),
                lambda b, n: (n, 0, b),
            ),
            (
                (blocks, shape.panels, heads, BLOCK, BLOCK),
                low,
                (1, 1, heads, BLOCK, BLOCK),
                lambda b, n: (b, n, 0, 0, 0),
            ),
        ],
    )


def attention_backward(shape, qkv, probs, grad_attended):
    width = shape.local
    heads = width // HEAD_DIM
    blocks = shape.tokens // BLOCK
    score_scale = 1.0 / math.sqrt(HEAD_DIM)

    def kernel(qkv_ref, probs_ref, grad_ref, out_ref):
        queries = qkv_ref[0, :width].astype(high)
        key_rows = qkv_ref[0, width : 2 * width].astype(high)
        value_rows = qkv_ref[0, 2 * width : 3 * width].astype(high)
        grads = grad_ref[0].astype(high)[shape.out_skip :]
        query_parts, key_parts, value_parts = [], [], []
        for head in range(heads):
            probs_low = probs_ref[0, 0, head]
            grad_head = head_rows(grads, head)
            value_parts.append(contract(grad_head, probs_low, 1, 1))
            grad_probs = contract(head_rows(value_rows, head), grad_head, 0, 0)
            probs = probs_low.astype(high)
            crossed = jnp.sum(grad_probs * probs, axis=0, keepdims=True)
            grad_scores = (probs * (grad_probs - crossed)).astype(low)
            query_parts.append(contract(head_rows(key_rows, head), grad_scores, 1, 0) * score_scale)
            key_parts.append(contract(head_rows(queries, head), grad_scores, 1, 1) * score_scale)
        rest = [jnp.zeros((shape.qkv_rows - 3 * width, BLOCK), high)]
        out_ref[0] = jnp.concatenate(
            query_parts + key_parts + value_parts + rest, axis=0
        ).astype(low)

    return call(
        kernel,
        "attention_backward",
        (blocks, shape.panels),
        [
            (qkv, (1, qkv.shape[1], BLOCK), lambda b, n: (n, 0, b)),
            (probs, (1, 1, heads, BLOCK, BLOCK), lambda b, n: (b, n, 0, 0, 0)),
            (grad_attended, (1, shape.out_rows, BLOCK), lambda b, n: (n, 0, b)),
        ],
        [
            (
                (shape.panels, shape.qkv_rows, shape.tokens),
                low,
                (1, shape.qkv_rows, BLOCK),
                lambda b, n: (n, 0, b),
            )
        ],
    )[0]


def weighted(weights, refs, held, sems, source_ref):
    block = pl.program_id(0)
    count = len(weights.panels)
    weights.start_all(refs, held, sems, block)
    for panel in range(count):
        weights.wait(refs, held, sems, block, panel)
    if weights.wide:
        source = source_ref[...]
        return contract(held[...], source.reshape(-1, source.shape[2]), 1, 0)
    return sum(contract(held[panel], source_ref[panel], 1, 0) for panel in range(count))


def store_sums(shape, sums_ref, rows, slot, block, values):
    lane = lax.broadcasted_iota(jnp.int32, (values[0].shape[0], sums_ref.shape[1]), 1)
    kept = sums_ref[rows]
    for j, value in enumerate(values):
        kept = jnp.where(lane == slot * shape.seqs + block * shape.share + j, value, kept)
    sums_ref[rows] = kept


def row_chunks(shape):
    rows = shape.width // 8
    return [slice(k * rows, (k + 1) * rows) for k in range(8)]


def moments(shape, first, second):
    center = first * (1.0 / shape.width)
    return center, lax.rsqrt(second * (1.0 / shape.width) - center * center + norm_epsilon)


def down_rows(values):
    return jnp.sum(values, axis=0, keepdims=True)


def panel_blocks(shape, array):
    return (array, (*array.shape[:2], shape.block), lambda b, *_: (0, 0, b))


def token_blocks(shape, array):
    return (array, (shape.width, shape.block), lambda b, *_: (0, b))


def sums_out(shape, slots):
    return ((shape.width, slots * shape.seqs), high, None, None)


def total_scratch(shape):
    return [pltpu.VMEM((shape.width, shape.block), high)]


def pieces_out(shape):
    return (
        (shape.panels, shape.seqs, shape.local, shape.part),
        low,
        (shape.panels, shape.share, shape.local, shape.part),
        lambda b, *_: (0, b, 0, 0),
    )


def norm_grads(shape, grad_ref, values_ref, table_ref, slot, block, sums_ref, sums_slot):
    first, second = 0.0, 0.0
    for rows in row_chunks(shape):
        values = values_ref[rows].astype(high)
        first, second = first + down_rows(values), second + down_rows(values * values)
    center, inverse = moments(shape, first, second)
    totals, crossed = 0.0, 0.0
    for rows in row_chunks(shape):
        grad = grad_ref[rows]
        normed = (values_ref[rows].astype(high) - center) * inverse
        store_sums(shape, sums_ref, rows, sums_slot, block, seq_sums(shape, grad))
        store_sums(shape, sums_ref, rows, sums_slot + 1, block, seq_sums(shape, grad * normed))
        hat = grad * (1.0 + spread(shape, table_ref[rows], slot, block))
        totals, crossed = totals + down_rows(hat), crossed + down_rows(hat * normed)

    def third(rows):
        normed = (values_ref[rows].astype(high) - center) * inverse
        hat = grad_ref[rows] * (1.0 + spread(shape, table_ref[rows], slot, block))
        return inverse * (hat - totals * (1.0 / shape.width) - normed * (crossed * (1.0 / shape.width)))

    return third


def project_out(shape, weights, attended, residual, table):
    order = weights.prefetch
    count = len(weights.arrays)

    def kernel(*refs):
        refs, order_refs = refs[len(order) :], refs[: len(order)]
        weight_refs, rest = refs[:count], refs[count:]
        attended_ref, residual_ref, table_ref, middle_ref, branch_ref, input_ref = rest[:6]
        held, sems, total = rest[6:]
        block = pl.program_id(0)
        total[...] = weighted(weights, (*order_refs, *weight_refs), held, sems, attended_ref)
        first, second = 0.0, 0.0
        for rows in row_chunks(shape):
            branch = total[rows]
            middle = residual_ref[rows].astype(high) + branch * spread(
                shape, table_ref[rows], 2, block
            )
            middle_ref[rows] = middle
            branch_ref[rows] = branch.astype(low)
            first, second = first + down_rows(middle), second + down_rows(middle * middle)
        center, inverse = moments(shape, first, second)
        for rows in row_chunks(shape):
            table = table_ref[rows]
            normed = (middle_ref[rows] - center) * inverse
            input_ref[rows] = (
                normed * (1.0 + spread(shape, table, 4, block)) + spread(shape, table, 3, block)
            ).astype(low)

    return call(
        kernel,
        "project_out",
        (shape.blocks,),
        weights.ins()
        + [panel_blocks(shape, attended), token_blocks(shape, residual), (table, None, None)],
        [token_out(shape, high), token_out(shape, low), token_out(shape, low)],
        weights.scratch(True) + total_scratch(shape),
        prefetch=order,
    )


def gelu_and_slope(values):
    root = math.sqrt(2.0 / math.pi)
    square = values * values
    bent = jnp.tanh(root * values * (1.0 + 0.044715 * square))
    half = 0.5 * (1.0 + bent)
    slope = half + 0.5 * values * (1.0 - bent * bent) * (root + 3.0 * 0.044715 * root * square)
    return values * half, slope


def project_up(shape, weights, source, bias):
    order = weights.prefetch
    count = len(weights.arrays)
    inner = weights.stop

    def kernel(*refs):
        refs, order_refs = refs[len(order) :], refs[: len(order)]
        weight_refs, rest = refs[:count], refs[count:]
        source_ref, bias_ref, hidden_ref, slope_ref, held, sems = rest
        panel = weights.panel((*order_refs, *weight_refs), held, sems, pl.program_id(0))
        values = contract(panel[...], source_ref[...], 0, 0) + bias_ref[0]
        hidden, slope = gelu_and_slope(values)
        hidden_ref[0] = hidden.astype(low)
        slope_ref[0] = slope.astype(low)

    return call(
        kernel,
        "project_up",
        (shape.panels,),
        weights.ins() + [(source, None, None), panel_in(bias)],
        [by_panel(shape, inner, low), by_panel(shape, inner, low)],
        weights.scratch(),
        prefetch=order,
    )


def project_down(shape, there, weights, hidden, middle, upstream, table, wide_count):
    order = weights.prefetch
    count = len(weights.arrays)
    bias_at = 6 * shape.seqs
    depth = shape.width // wide_count

    def kernel(at_ref, *refs):
        refs, order_refs = refs[len(order) :], refs[: len(order)]
        weight_refs, rest = refs[:count], refs[count:]
        hidden_ref, middle_ref, upstream_ref, table_ref, out_ref, gate_ref = rest[:6]
        held, sems, total, block_held = rest[6:]
        block = pl.program_id(0)
        total[...] = weighted(weights, (*order_refs, *weight_refs), held, sems, hidden_ref)
        for k in range(wide_count):
            rows = slice(k * depth, (k + 1) * depth)
            table = table_ref[rows]
            mlp = total[rows] + pick(table, bias_at)
            block_held[k] = middle_ref[rows] + mlp * spread(shape, table, 5, block)
            store_sums(
                shape, gate_ref, rows, 0, block, seq_sums(shape, upstream_ref[rows].astype(high) * mlp)
            )
        take_pieces(shape, at_ref, block_held, out_ref)

    return call(
        kernel,
        "project_down",
        (shape.blocks,),
        weights.ins()
        + [panel_blocks(shape, hidden), token_blocks(shape, middle)]
        + [token_blocks(shape, upstream), (table, None, None)],
        [pieces_out(shape), sums_out(shape, 1)],
        weights.scratch(True)
        + [
            *total_scratch(shape),
            pltpu.VMEM((wide_count, depth, shape.block), high),
        ],
        [there, *order],
    )


def grad_outs(shape, columns):
    tall = shape.panels // 2
    half = shape.width // 2
    return [((2, tall, half, columns), low, (2, 1, half, columns), lambda n, *_: (0, n, 0, 0))]


def core_panels(shape, array, core):
    tall = shape.panels // 2
    return (array, (1, *array.shape[1:]), lambda n, *_: (n + core * tall, 0, 0))


def weight_grad(shape, name, source, grad, core):
    columns = grad.shape[1]
    half = shape.width // 2

    def kernel(source_ref, grad_ref, out_ref):
        product = contract(source_ref[...], grad_ref[0], 1, 1).astype(low)
        out_ref[...] = product.reshape(2, 1, half, columns)

    return call(
        kernel,
        name,
        (shape.panels // 2,),
        [(source, None, None), core_panels(shape, grad, core)],
        grad_outs(shape, columns),
    )[0]


def device_weight_grad(shape, name, source, grad, order, wide_count):
    columns = grad.shape[1]
    rows = shape.width // wide_count

    def kernel(order_ref, source_ref, grad_ref, out_ref):
        product = contract(source_ref[...], grad_ref[0], 1, 1).astype(low)
        panel = pl.program_id(0)
        for block in range(wide_count):
            device = order_ref[panel * wide_count + block]
            out_ref[0, device // shape.panels] = product[block * rows : (block + 1) * rows]

    out = call(
        kernel,
        name,
        (shape.panels,),
        [(source, None, None), panel_in(grad)],
        [
            (
                (shape.panels, wide_count, rows, columns),
                low,
                (1, wide_count, rows, columns),
                lambda n, order_ref: (order_ref[n * wide_count] % shape.panels, 0, 0, 0),
            )
        ],
        prefetch=[order],
    )[0]
    return out.reshape(shape.panels * wide_count, rows, columns)


def first_weight_grad(shape, source, grad_qkv, grad_branch, attended, core):
    columns = 4 * shape.local
    begin = shape.out_from
    half = shape.width // 2

    def kernel(source_ref, qkv_ref, branch_ref, attended_ref, out_ref, held):
        held[:, : shape.qkv_rows] = contract(source_ref[...], qkv_ref[0], 1, 1)
        late = contract(branch_ref[...], attended_ref[0], 1, 1)
        both_there = shape.qkv_rows - begin
        if both_there:
            held[:, begin : shape.qkv_rows] += late[:, :both_there]
        held[:, shape.qkv_rows :] = late[:, both_there:]
        out_ref[...] = held[...].astype(low).reshape(2, 1, half, columns)

    return call(
        kernel,
        "first_weight_grad",
        (shape.panels // 2,),
        [
            (source, None, None),
            core_panels(shape, grad_qkv, core),
            (grad_branch, None, None),
            core_panels(shape, attended, core),
        ],
        grad_outs(shape, columns),
        [pltpu.VMEM((shape.width, columns), high)],
    )[0]


def hidden_backward(shape, weights, grad_mlp, slope):
    order = weights.prefetch
    count = len(weights.arrays)
    inner = weights.stop

    def kernel(*refs):
        refs, order_refs = refs[len(order) :], refs[: len(order)]
        weight_refs, rest = refs[:count], refs[count:]
        grad_ref, slope_ref, out_ref, bias_ref, held, sems = rest
        panel = weights.panel((*order_refs, *weight_refs), held, sems, pl.program_id(0))
        values = contract(panel[...], grad_ref[...], 0, 0) * slope_ref[0].astype(high)
        values = values.astype(low)
        out_ref[0] = values
        bias_ref[0] = jnp.sum(values.astype(high), axis=1, keepdims=True)

    return call(
        kernel,
        "hidden_backward",
        (shape.panels,),
        weights.ins() + [(grad_mlp, None, None), panel_in(slope)],
        [
            by_panel(shape, inner, low),
            ((shape.panels, inner, 1), high, (1, inner, 1), lambda n, *_: (n, 0, 0)),
        ],
        weights.scratch(),
        prefetch=order,
    )


def middle_backward(shape, weights, grad_up, middle, upstream, branch, table):
    order = weights.prefetch
    count = len(weights.arrays)

    def kernel(*refs):
        refs, order_refs = refs[len(order) :], refs[: len(order)]
        weight_refs, rest = refs[:count], refs[count:]
        grad_ref, middle_ref, upstream_ref, branch_ref, table_ref = rest[:5]
        out_ref, low_ref, sums_ref, held, sems, total = rest[5:]
        block = pl.program_id(0)
        total[...] = weighted(weights, (*order_refs, *weight_refs), held, sems, grad_ref)
        third = norm_grads(
            shape, total, middle_ref, table_ref, 4, block, sums_ref, 1
        )
        for rows in row_chunks(shape):
            grad = upstream_ref[rows].astype(high) + third(rows)
            store_sums(
                shape, sums_ref, rows, 0, block, seq_sums(shape, grad * branch_ref[rows].astype(high))
            )
            out_ref[rows] = grad
            low_ref[rows] = (grad * spread(shape, table_ref[rows], 2, block)).astype(low)

    return call(
        kernel,
        "middle_backward",
        (shape.blocks,),
        weights.ins()
        + [panel_blocks(shape, grad_up)]
        + [token_blocks(shape, v) for v in (middle, upstream, branch)]
        + [(table, None, None)],
        [token_out(shape, high), token_out(shape, low), sums_out(shape, 3)],
        weights.scratch(True) + total_scratch(shape),
        prefetch=order,
    )


def attended_backward(shape, weights, grad_branch):
    order = weights.prefetch
    count = len(weights.arrays)

    def kernel(*refs):
        refs, order_refs = refs[len(order) :], refs[: len(order)]
        weight_refs, (grad_ref, out_ref, held, sems) = refs[:count], refs[count:]
        panel = weights.panel((*order_refs, *weight_refs), held, sems, pl.program_id(0))
        out_ref[0] = contract(panel[...], grad_ref[...], 0, 0).astype(low)

    return call(
        kernel,
        "attended_backward",
        (shape.panels,),
        weights.ins() + [(grad_branch, None, None)],
        [by_panel(shape, shape.out_rows, low)],
        weights.scratch(),
        prefetch=order,
    )[0]


def input_backward(shape, there, weights, grad_qkv, residual, grad_middle, table, wide_count):
    order = weights.prefetch
    count = len(weights.arrays)
    depth = shape.width // wide_count

    def kernel(at_ref, *refs):
        refs, order_refs = refs[len(order) :], refs[: len(order)]
        weight_refs, rest = refs[:count], refs[count:]
        qkv_ref, residual_ref, middle_ref, table_ref, out_ref, sums_ref = rest[:6]
        held, sems, total, block_held = rest[6:]
        block = pl.program_id(0)
        total[...] = weighted(weights, (*order_refs, *weight_refs), held, sems, qkv_ref)
        third = norm_grads(shape, total, residual_ref, table_ref, 1, block, sums_ref, 0)
        for k in range(wide_count):
            rows = slice(k * depth, (k + 1) * depth)
            block_held[k] = middle_ref[rows] + third(rows)
        take_pieces(shape, at_ref, block_held, out_ref)

    return call(
        kernel,
        "input_backward",
        (shape.blocks,),
        weights.ins()
        + [panel_blocks(shape, grad_qkv)]
        + [token_blocks(shape, v) for v in (residual, grad_middle)]
        + [(table, None, None)],
        [pieces_out(shape), sums_out(shape, 2)],
        weights.scratch(True)
        + [
            *total_scratch(shape),
            pltpu.VMEM((wide_count, depth, shape.block), high),
        ],
        [there, *order],
    )


def on_device(
    tokens,
    ada_weight,
    ada_bias,
    class_table,
    query_weight,
    key_weight,
    value_weight,
    out_weight,
    up_weight,
    up_bias,
    down_weight,
    down_bias,
    cotangent,
    clip_frames,
    time_ids,
    class_ids,
):
    micro_count, seq_count, local_width, seq_tokens = tokens.shape
    class_count, full_width = class_table.shape
    panels, wide_count = lax.axis_size("narrow"), lax.axis_size("wide")
    wide_at = lax.axis_index("wide")
    seqs = micro_count * seq_count
    shape = Shape(seqs, seq_tokens // panels, full_width, panels)
    own_rows = ada_weight.shape[0]
    deep = wide_count // 2
    highest = lax.Precision.HIGHEST
    local_shape = (seqs, local_width, seq_tokens)
    there, came, goes = orders()

    class_hot = (class_ids.reshape(seqs)[:, None] == jnp.arange(class_count)[None, :]).astype(low)
    condition = time_embedding(time_ids.reshape(seqs), full_width) + jnp.einsum(
        "sc,cd->sd", class_hot, class_table, preferred_element_type=high
    )
    sigmoid_cond = jax.nn.sigmoid(condition)
    cond_act = (condition * sigmoid_cond).astype(low)
    silu_slope = sigmoid_cond * (1.0 + condition * (1.0 - sigmoid_cond))
    own_cond = lax.dynamic_slice_in_dim(cond_act, wide_at * own_rows, own_rows, axis=1)
    own_slope = lax.dynamic_slice_in_dim(silu_slope, wide_at * own_rows, own_rows, axis=1)

    first_piece = jnp.concatenate([query_weight, key_weight, value_weight, out_weight.T], axis=1)
    first, down = Gather(first_piece), LateGather(down_weight.T)
    order = device_order()
    mod_part = jnp.einsum("sd,dje->jse", own_cond, ada_weight, preferred_element_type=high)
    mod_part = mod_part.reshape(6 * seqs, local_width)
    hops = [{"side_by": 1}]
    while 2 ** len(hops) <= deep:
        hops.append({"deep_by": 2 ** (len(hops) - 1)})

    first.step()
    token_swap = NarrowSwap(tokens.reshape(local_shape))
    token_same = token_swap.step(0)
    mod_part = mod_part + send(mod_part, **hops[0])
    down.side()
    first.ring, token_same, mod_part, down.line, token_swap.parts = sync(
        first.ring, token_same, mod_part, down.line, token_swap.parts
    )

    first.step()
    token_other = token_swap.step(1)
    mod_part = mod_part + send(mod_part, **hops[1])
    first.ring, token_other, mod_part, down.line = sync(
        first.ring, token_other, mod_part, down.line
    )

    for at in range(2, max(deep - 1, len(hops))):
        if at < len(hops):
            mod_part = mod_part + send(mod_part, **hops[at])
        if at < deep - 1:
            first.step()
        if at == 2:
            token_near, token_far = token_swap.pieces(token_same, token_other)
        if at == max(deep - 1, len(hops)) - 1:
            first.front_side()
            first.front, first.front_got = sync(first.front, first.front_got)
        first.ring, mod_part = sync(first.ring, mod_part)

    first.rear_tall()
    mod_own = (
        mod_part.reshape(6, seqs, local_width) + ada_bias.astype(high)[:, None, :]
    ).reshape(6 * seqs, local_width)
    small = gather_narrow(
        jnp.concatenate(
            [
                mod_own,
                down_bias.astype(high)[None, :],
                up_bias.astype(high).reshape(-1, local_width),
            ]
        )
    )
    first.rear, first.rear_got, first.front, first.front_got, token_far, small = sync(
        first.rear, first.rear_got, first.front, first.front_got, token_far, small
    )

    first.second()
    first.core(0, 2)
    up_full = lax.all_gather(after(up_weight, small), both, axis=0, tiled=False)
    table, up_bias_full = lay_small(shape, came, small, wide_count)
    token_parts = token_near + [token_far[k : k + 1] for k in range(panels // 2)]
    frame_at = jnp.arange(shape.part) % FRAMES
    in_clip = (frame_at[None, :] < clip_frames.reshape(seqs)[:, None]).astype(jnp.int32).reshape(-1)
    residual, input_one = prepare_tokens(shape, came, token_parts, table, wide_count)
    first.arrays, input_one, down.line = sync(first.arrays, input_one, down.line)

    first.core(*[k for k in range(len(first.arrays)) if k not in (0, 2)])
    qkv_weights = Weights(first.result(), 0, shape.qkv_rows)
    out_weights = Weights(first.result(), shape.out_from)
    down.along_tall()
    upstream_cut = cut_tokens(shape, after(cotangent.reshape(local_shape), input_one))
    upstream_parts = swap_narrow(upstream_cut)
    qkv = project_qkv(shape, qkv_weights, after(input_one, upstream_cut))
    qkv, down.plane = sync(qkv, down.plane)

    down.step()
    attended, probs = attention_forward(shape, qkv, in_clip)
    (attended,) = sync(attended)

    middle, branch, input_two = project_out(shape, out_weights, attended, residual, table)
    middle, input_two, down.ring, upstream_parts = sync(
        middle, input_two, down.ring, upstream_parts
    )

    upstream, grad_mlp, down_bias_part = prepare_upstream(
        shape, there, upstream_parts, table, wide_count
    )
    down.step()
    down.core(0, 1)
    up_all = GatheredWeights(up_full, order, panels)
    hidden, slope = project_up(shape, up_all, after(input_two, grad_mlp), up_bias_full)
    hidden, slope, down.cores, down.ring = sync(hidden, slope, down.cores, down.ring)

    for k in range(3, deep):
        down.step()
    down.core(*range(2, deep - 1))
    down_grads = device_weight_grad(
        shape, "down_weight_grad", grad_mlp, hidden, order, wide_count
    )
    down_grad = lax.psum_scatter(
        down_grads, ("narrow", "wide"), scatter_dimension=0, tiled=False
    ).astype(high)
    down_grads, down.ring = sync(down_grads, down.ring)
    down.core(deep - 1)
    down_all = Weights(down.result())
    output_parts, gate_two_part = project_down(
        shape, there, down_all, after(hidden, down_grads), middle, upstream, table, wide_count
    )
    output_parts, gate_two_part = sync(output_parts, gate_two_part)

    output_got = swap_narrow(output_parts)
    grad_up, up_bias_part = hidden_backward(
        shape, down_all, after(grad_mlp, gate_two_part), slope
    )
    other = weight_grad(shape, "up_weight_grad", input_two, grad_up, 1)
    other, output_got = sync(other, output_got)

    up_sum = GradSum(other)
    near = weight_grad(shape, "up_weight_grad", after(input_two, other), grad_up, 0)
    near, up_sum.got = sync(near, up_sum.got)
    up_sum.near(near)
    half = deep // 2
    up_parts = up_sum.split(half)
    sums = up_parts[0].sums("y")
    up_parts[0].along("y", sums)
    grad_middle, grad_branch, middle_sums = middle_backward(
        shape, up_all, after(grad_up, near, *sums), middle, upstream, branch, table
    )
    *_, grad_branch = sync(*up_parts, grad_branch)

    tall_sums, side_sums = up_parts[1].sums("y"), up_parts[0].sums("x")
    up_parts[1].along("y", tall_sums)
    up_parts[0].along("x", side_sums)
    grad_attended = attended_backward(
        shape, out_weights, after(grad_branch, *tall_sums, *side_sums)
    )
    grad_qkv = attention_backward(shape, qkv, probs, grad_attended)
    *_, grad_qkv = sync(*up_parts, grad_qkv)

    side_sums = up_parts[1].sums("x")
    up_parts[1].along("x", side_sums)
    grad_qkv = after(grad_qkv, *side_sums)
    other = first_weight_grad(shape, input_one, grad_qkv, grad_branch, attended, 1)
    *_, other = sync(up_parts[0], other)

    first_sum = GradSum(other)
    near = first_weight_grad(shape, after(input_one, other), grad_qkv, grad_branch, attended, 0)
    near, first_sum.got, _ = sync(near, first_sum.got, up_parts[1])
    first_sum.near(near)
    first_parts = first_sum.split(half)
    side_sums, tall_sums = first_parts[0].sums("x"), first_parts[1].sums("y")
    first_parts[0].along("x", side_sums)
    first_parts[1].along("y", tall_sums)
    up_sums = deep_sums(up_parts)
    along_deep(up_parts, up_sums)
    input_parts, input_sums = input_backward(
        shape,
        there,
        qkv_weights,
        after(grad_qkv, *side_sums, *tall_sums, *up_sums),
        residual,
        grad_middle,
        table,
        wide_count,
    )
    *_, input_parts, input_sums = sync(*first_parts, up_parts[0], input_parts, input_sums)

    tall_sums, side_sums = first_parts[0].sums("y"), first_parts[1].sums("x")
    first_parts[0].along("y", tall_sums)
    first_parts[1].along("x", side_sums)
    small_grad = lay_small_grads(
        shape,
        goes,
        input_sums,
        middle_sums,
        after(gate_two_part, *side_sums, *tall_sums),
        down_bias_part,
        up_bias_part,
        wide_count,
    )
    small_grad = small_grad.reshape(2, panels // 2, *small_grad.shape[1:])
    small_grad = small_grad[0] + send(small_grad[1], core_by=1)
    by = 1
    while by < deep:
        small_grad = small_grad + send(small_grad, deep_by=by)
        by *= 2
    *_, small_grad = sync(*first_parts, small_grad)
    sums = deep_sums(first_parts)
    first_got = along_deep(first_parts, sums)
    output = join_tokens(shape, after(output_got, small_grad), low)
    small_grad = after(small_grad, *sums)
    small_grad = small_grad + send(small_grad, side_by=1)
    small_grad = after(small_grad, first_got[0], output)
    small_grad = sum(
        [small_grad[0]] + [send(small_grad[k], tall_by=k) for k in range(1, panels // 2)]
    )
    own_mod = small_grad[: 6 * seqs].reshape(6, seqs, local_width)
    down_bias_grad = small_grad[6 * seqs]
    up_bias_grad = small_grad[6 * seqs + 1 :].reshape(-1)
    ada_grad = jnp.einsum("sd,jse->dje", own_cond.astype(high), own_mod, precision=highest)
    ada_bias_grad = jnp.sum(own_mod, axis=1)
    own_mod = after(own_mod, *first_got[1:2])
    cond_local = sum_narrow(
        own_slope * jnp.einsum("jse,dje->sd", own_mod, ada_weight.astype(high), precision=highest)
    )
    input_got = swap_narrow(after(input_parts, cond_local))
    cond_local = after(cond_local, *first_got)
    cond_grad = sum_wide(
        lax.dynamic_update_slice_in_dim(
            jnp.zeros((seqs, full_width), high), cond_local, wide_at * own_rows, axis=1
        )
    )
    input_grad = join_tokens(shape, after(input_got, cond_grad), high)
    up_grad = up_parts[0].total()
    first_grad = first_parts[0].total()
    table_grad = jnp.einsum("sc,sd->cd", class_hot.astype(high), cond_grad, precision=highest)
    return (
        output.reshape(tokens.shape),
        input_grad.reshape(tokens.shape),
        ada_grad,
        ada_bias_grad,
        table_grad,
        first_grad[:, :local_width],
        first_grad[:, local_width : 2 * local_width],
        first_grad[:, 2 * local_width : 3 * local_width],
        first_grad[:, 3 * local_width :].T,
        up_grad,
        up_bias_grad,
        down_grad.T,
        down_bias_grad,
    )


def solution(mesh):
    return jax.shard_map(
        on_device,
        mesh=mesh,
        in_specs=(
            P(None, None, "narrow", "wide"),
            P("wide", None, "narrow"),
            P(None, "narrow"),
            P(),
            P("wide", "narrow"),
            P("wide", "narrow"),
            P("wide", "narrow"),
            P("narrow", "wide"),
            P("wide", "narrow"),
            P("narrow"),
            P("narrow", "wide"),
            P("narrow"),
            P(None, None, "narrow", "wide"),
            P(),
            P(),
            P(),
        ),
        out_specs=(
            P(None, None, "narrow", "wide"),
            P(None, None, "narrow", "wide"),
            P("wide", None, "narrow"),
            P(None, "narrow"),
            P(),
            P("wide", "narrow"),
            P("wide", "narrow"),
            P("wide", "narrow"),
            P("narrow", "wide"),
            P("wide", "narrow"),
            P("narrow"),
            P("narrow", "wide"),
            P("narrow"),
        ),
        check_vma=False,
    )
```

profile of v0, /device:TPU:0, one launch (start us, length us, event | category | flops | bytes accessed | tf_op | source)
XLA Modules:
  0.0 611.8 jit_solution(14339253407365089558)
XLA Ops:
  8.6 3.1 collective-permute-start
  19.5 3.4 collective-permute-done.2
  23.0 7.1 %collective-permute-done.1.refs_1_ = bf16[1,4,288,256]{3,2,1,0:T(8,128)(2,1)S(1)} collective-permute-done((bf16[1,4,288,256]{3,2,1,0:T(8,128)(2,1)S(1)}, bf16[1,4,288,256]{3,2,1,0:T(8,128)(2,1)S(1)}, u32[]{:S(2)}, u32[]{:S(2)}) %collective-permute-start.1) | collective-permute-done | bytes 589856 | tf_op jit(solution)/shard_map/ppermute | solution.py:64
  36.1 7.2 %collective-permute-done.6 = f32[24,288]{1,0:T(8,128)S(1)} collective-permute-done((f32[24,288]{1,0:T(8,128)S(1)}, f32[24,288]{1,0:T(8,128)S(1)}, u32[]{:S(2)}, u32[]{:S(2)}) %collective-permute-start.6) | collective-permute-done | bytes 27680 | tf_op jit(solution)/shard_map/ppermute | solution.py:64
  50.2 6.9 %collective-permute-done.8 = f32[24,288]{1,0:T(8,128)S(1)} collective-permute-done((f32[24,288]{1,0:T(8,128)S(1)}, f32[24,288]{1,0:T(8,128)S(1)}, u32[]{:S(2)}, u32[]{:S(2)}) %collective-permute-start.8) | collective-permute-done | bytes 27680 | tf_op jit(solution)/shard_map/ppermute | solution.py:64
  59.5 11.9 %collective-permute-done.12 = f32[29,288]{1,0:T(8,128)S(1)} collective-permute-done((f32[29,288]{1,0:T(8,128)S(1)}, f32[29,288]{1,0:T(8,128)S(1)}, u32[]{:S(2)}, u32[]{:S(2)}) %collective-permute-start.12) | collective-permute-done | bytes 33440 | tf_op jit(solution)/shard_map/ppermute | solution.py:64
  78.1 4.4 lay_small.1
  84.8 7.0 %prepare_tokens.1 = (bf16[1152,1024]{1,0:T(8,128)(2,1)}, bf16[1152,1024]{1,0:T(8,128)(2,1)}) custom-call(s32[8]{0:T(128)} %stack.214.at_ref, bf16[1,4,288,256]{3,2,1,0:T(8,128)(2,1)} %get-tuple-element.309.refs_0_, bf16[1,4,288,256]{3,2,1,0:T(8,128)(2,1)} %copy-done.21, bf16[1,4,288,256]{3,2,1,0:T(8,128)(2,1)} %get-tuple-element.313.refs_2_, ...), custom_call_target="tpu_custom_call" | custom-call | flops 400000000 | tf_op jit(solution)/shard_map/prepare_tokens/pallas_call | solution.py:364
  91.8 21.2 %collective-permute-done.15.refs_3_ = bf16[576,1152]{1,0:T(8,128)(2,1)} collective-permute-done((bf16[576,1152]{1,0:T(8,128)(2,1)S(1)}, bf16[576,1152]{1,0:T(8,128)(2,1)}, u32[]{:S(2)}, u32[]{:S(2)}) %collective-permute-start.15) | collective-permute-done | bytes 1327136 | tf_op jit(solution)/shard_map/ppermute | solution.py:64
  113.0 4.0 collective-permute-done.14.refs_1_
  120.9 3.9 cut_tokens.1
  124.8 4.5 all-to-all-start
  129.4 15.6 %project_qkv.1.qkv_ref = bf16[4,896,1024]{2,1,0:T(8,128)(2,1)} custom-call(bf16[576,1152]{1,0:T(8,128)(2,1)} %copy-done.2, bf16[576,1152]{1,0:T(8,128)(2,1)} %collective-permute-done.14.refs_1_, bf16[576,1152]{1,0:T(8,128)(2,1)} %copy-done.1, bf16[576,1152]{1,0:T(8,128)(2,1)} %collective-permute-done.15.refs_3_, ...), custom_call_target="tpu_custom_call" | custom-call | flops 1500000000 | tf_op jit(solution)/shard_map/project_qkv/pallas_call | solution.py:364
  147.7 24.8 %attention_forward.1 = (bf16[4,384,1024]{2,1,0:T(8,128)(2,1)}, bf16[8,4,4,128,128]{4,3,2,1,0:T(8,128)(2,1)}) custom-call(bf16[4,896,1024]{2,1,0:T(8,128)(2,1)} %project_qkv.1.qkv_ref, s32[1,1024]{1,0:T(1,128)} %bitcast.238, s32[1024,1]{1,0:T(8,128)} %bitcast.230), custom_call_target="tpu_custom_call" | custom-call | flops 2400000000 | tf_op jit(solution)/shard_map/attention_forward/pallas_call | solution.py:364
  172.6 11.6 %project_out.1 = (f32[1152,1024]{1,0:T(8,128)}, bf16[1152,1024]{1,0:T(8,128)(2,1)}, bf16[1152,1024]{1,0:T(8,128)(2,1)}) custom-call(bf16[576,1152]{1,0:T(8,128)(2,1)} %copy-done.2, bf16[576,1152]{1,0:T(8,128)(2,1)} %collective-permute-done.14.refs_1_, bf16[576,1152]{1,0:T(8,128)(2,1)} %copy-done.1, bf16[576,1152]{1,0:T(8,128)(2,1)} %collective-permute-done.15.refs_3_, ...), custom_call_target="tpu_custom_call" | custom-call | flops 1700000000 | tf_op jit(solution)/shard_map/project_out/pallas_call | solution.py:364
  184.1 9.7 %collective-permute-done.21.refs_1_ = bf16[2,2,144,1152]{3,2,1,0:T(8,128)(2,1)S(1)} collective-permute-done((bf16[2,2,144,1152]{3,2,1,0:T(8,128)(2,1)S(1)}, bf16[2,2,144,1152]{3,2,1,0:T(8,128)(2,1)S(1)}, u32[]{:S(2)}, u32[]{:S(2)}) %collective-permute-start.21) | collective-permute-done | bytes 1327136 | tf_op jit(solution)/shard_map/ppermute | solution.py:64
  196.2 6.4 %prepare_upstream.1 = (bf16[1152,1024]{1,0:T(8,128)(2,1)}, bf16[1152,1024]{1,0:T(8,128)(2,1)}, f32[1152,1]{1,0:T(8,128)}) custom-call(s32[8]{0:T(128)} %stack.262.at_ref, bf16[4,4,288,256]{3,2,1,0:T(8,128)(2,1)} %all-to-all-done.pieces_ref, f32[1152,29]{1,0:T(8,128)} %get-tuple-element.182.refs_4_.refs_10_.table_ref.refs_11_.refs_6_), custom_call_target="tpu_custom_call" | custom-call | flops 400000000 | tf_op jit(solution)/shard_map/prepare_upstream/pallas_call | solution.py:364
  202.5 29.1 %project_up.1 = (bf16[4,1152,1024]{2,1,0:T(8,128)(2,1)}, bf16[4,1152,1024]{2,1,0:T(8,128)(2,1)}) custom-call(s32[32]{0:T(128)} %stack.253.refs_0_.order_ref, bf16[32,144,1152]{2,1,0:T(8,128)(2,1)} %bitcast.209, bf16[1152,1024]{1,0:T(8,128)(2,1)} %get-tuple-element.231.refs_2_.source_ref, f32[4,1152,1]{2,1,0:T(8,128)} %get-tuple-element.207.refs_3_), custom_call_target="tpu_custom_call" | custom-call | flops 2800000000 | tf_op jit(solution)/shard_map/project_up/pallas_call | solution.py:364
  231.9 17.8 %down_weight_grad.1 = bf16[4,8,144,1152]{3,2,1,0:T(8,128)(2,1)} custom-call(s32[32]{0:T(128)} %stack.253.refs_0_.order_ref, bf16[1152,1024]{1,0:T(8,128)(2,1)} %get-tuple-element.225.source_ref.refs_8_, bf16[4,1152,1024]{2,1,0:T(8,128)(2,1)} %get-tuple-element.212.grad_ref.refs_8_), custom_call_target="tpu_custom_call" | custom-call | flops 1000000000 | tf_op jit(solution)/shard_map/down_weight_grad/pallas_call | solution.py:364
  249.8 15.3 %collective-permute-done.25.refs_3_ = bf16[2,2,144,1152]{3,2,1,0:T(8,128)(2,1)S(1)} collective-permute-done((bf16[2,2,144,1152]{3,2,1,0:T(8,128)(2,1)}, bf16[2,2,144,1152]{3,2,1,0:T(8,128)(2,1)S(1)}, u32[]{:S(2)}, u32[]{:S(2)}) %collective-permute-start.25) | collective-permute-done | bytes 1327136 | tf_op jit(solution)/shard_map/ppermute | solution.py:64
  269.2 21.2 %project_down.1 = (bf16[4,4,288,256]{3,2,1,0:T(8,128)(2,1)}, f32[1152,4]{1,0:T(8,128)}) custom-call(s32[8]{0:T(128)} %stack.262.at_ref, bf16[2,2,144,1152]{3,2,1,0:T(8,128)(2,1)} %copy-done.3, bf16[2,2,144,1152]{3,2,1,0:T(8,128)(2,1)} %copy-done.6, bf16[2,2,144,1152]{3,2,1,0:T(8,128)(2,1)} %collective-permute-done.24.refs_2_, ...), custom_call_target="tpu_custom_call" | custom-call | flops 2500000000 | tf_op jit(solution)/shard_map/project_down/pallas_call | solution.py:364
  290.5 3.6 all-to-all-start.1
  294.3 20.2 %hidden_backward.1 = (bf16[4,1152,1024]{2,1,0:T(8,128)(2,1)}, f32[4,1152,1]{2,1,0:T(8,128)}) custom-call(bf16[2,2,144,1152]{3,2,1,0:T(8,128)(2,1)} %copy-done.3, bf16[2,2,144,1152]{3,2,1,0:T(8,128)(2,1)} %copy-done.6, bf16[2,2,144,1152]{3,2,1,0:T(8,128)(2,1)} %collective-permute-done.24.refs_2_, bf16[2,2,144,1152]{3,2,1,0:T(8,128)(2,1)} %copy-done.7, ...), custom_call_target="tpu_custom_call" | custom-call | flops 2100000000 | tf_op jit(solution)/shard_map/hidden_backward/pallas_call | solution.py:364
  314.6 10.5 %up_weight_grad.2 = bf16[2,2,576,1152]{3,2,1,0:T(8,128)(2,1)} custom-call(bf16[1152,1024]{1,0:T(8,128)(2,1)} %get-tuple-element.231.refs_2_.source_ref, bf16[4,1152,1024]{2,1,0:T(8,128)(2,1)} %get-tuple-element.234.grad_ref.refs_2_), custom_call_target="tpu_custom_call" | custom-call | flops 1000000000 | tf_op jit(solution)/shard_map/up_weight_grad/pallas_call | solution.py:364
  325.5 10.8 %up_weight_grad.3 = bf16[2,2,576,1152]{3,2,1,0:T(8,128)(2,1)} custom-call(bf16[1152,1024]{1,0:T(8,128)(2,1)} %get-tuple-element.231.refs_2_.source_ref, bf16[4,1152,1024]{2,1,0:T(8,128)(2,1)} %get-tuple-element.234.grad_ref.refs_2_), custom_call_target="tpu_custom_call" | custom-call | flops 1000000000 | tf_op jit(solution)/shard_map/up_weight_grad/pallas_call | solution.py:364
  340.4 27.4 %middle_backward.1 = (f32[1152,1024]{1,0:T(8,128)}, bf16[1152,1024]{1,0:T(8,128)(2,1)}, f32[1152,12]{1,0:T(8,128)}) custom-call(s32[32]{0:T(128)} %stack.253.refs_0_.order_ref, bf16[32,144,1152]{2,1,0:T(8,128)(2,1)} %bitcast.210, bf16[4,1152,1024]{2,1,0:T(8,128)(2,1)} %get-tuple-element.234.grad_ref.refs_2_, ...), custom_call_target="tpu_custom_call" | custom-call | flops 3000000000 | tf_op jit(solution)/shard_map/middle_backward/pallas_call | solution.py:364
  369.9 3.7 fusion.1
  378.2 9.4 %attended_backward.1.grad_ref = bf16[4,384,1024]{2,1,0:T(8,128)(2,1)} custom-call(bf16[576,1152]{1,0:T(8,128)(2,1)} %copy-done.2, bf16[576,1152]{1,0:T(8,128)(2,1)} %collective-permute-done.14.refs_1_, bf16[576,1152]{1,0:T(8,128)(2,1)} %copy-done.1, bf16[576,1152]{1,0:T(8,128)(2,1)} %collective-permute-done.15.refs_3_, ...), custom_call_target="tpu_custom_call" | custom-call | flops 900000000 | tf_op jit(solution)/shard_map/attended_backward/pallas_call | solution.py:364
  387.6 34.0 %attention_backward.1.qkv_ref.refs_8_ = bf16[4,896,1024]{2,1,0:T(8,128)(2,1)} custom-call(bf16[4,896,1024]{2,1,0:T(8,128)(2,1)} %project_qkv.1.qkv_ref, bf16[8,4,4,128,128]{4,3,2,1,0:T(8,128)(2,1)} %get-tuple-element.242.probs_ref, bf16[4,384,1024]{2,1,0:T(8,128)(2,1)} %attended_backward.1.grad_ref), custom_call_target="tpu_custom_call" | custom-call | flops 3300000000 | tf_op jit(solution)/shard_map/attention_backward/pallas_call | solution.py:364
  424.5 12.7 %first_weight_grad.2 = bf16[2,2,576,1152]{3,2,1,0:T(8,128)(2,1)} custom-call(bf16[1152,1024]{1,0:T(8,128)(2,1)} %get-tuple-element.255.refs_8_.source_ref, bf16[4,896,1024]{2,1,0:T(8,128)(2,1)} %attention_backward.1.qkv_ref.refs_8_, bf16[1152,1024]{1,0:T(8,128)(2,1)} %get-tuple-element.244.refs_8_.branch_ref, ...), custom_call_target="tpu_custom_call" | custom-call | flops 1200000000 | tf_op jit(solution)/shard_map/first_weight_grad/pallas_call | solution.py:364
  438.8 12.5 %first_weight_grad.3 = bf16[2,2,576,1152]{3,2,1,0:T(8,128)(2,1)} custom-call(bf16[1152,1024]{1,0:T(8,128)(2,1)} %get-tuple-element.255.refs_8_.source_ref, bf16[4,896,1024]{2,1,0:T(8,128)(2,1)} %attention_backward.1.qkv_ref.refs_8_, bf16[1152,1024]{1,0:T(8,128)(2,1)} %get-tuple-element.244.refs_8_.branch_ref, ...), custom_call_target="tpu_custom_call" | custom-call | flops 1200000000 | tf_op jit(solution)/shard_map/first_weight_grad/pallas_call | solution.py:364
  451.2 8.2 %collective-permute-done.33 = bf16[2,144,1152]{2,1,0:T(8,128)(2,1)S(1)} collective-permute-done((bf16[2,144,1152]{2,1,0:T(8,128)(2,1)}, bf16[2,144,1152]{2,1,0:T(8,128)(2,1)S(1)}, u32[]{:S(2)}, u32[]{:S(2)}) %collective-permute-start.33) | collective-permute-done | bytes 663584 | tf_op jit(solution)/shard_map/ppermute | solution.py:64
  459.4 3.3 fusion.3
  462.8 3.1 fusion.2
  474.2 22.0 %input_backward.1 = (bf16[4,4,288,256]{3,2,1,0:T(8,128)(2,1)}, f32[1152,8]{1,0:T(8,128)}) custom-call(s32[8]{0:T(128)} %stack.262.at_ref, bf16[576,1152]{1,0:T(8,128)(2,1)} %copy-done.2, bf16[576,1152]{1,0:T(8,128)(2,1)} %collective-permute-done.14.refs_1_, bf16[576,1152]{1,0:T(8,128)(2,1)} %copy-done.1, bf16[576,1152]{1,0:T(8,128)(2,1)} %collective-permute-done.15.refs_3_, ...), custom_call_target="tpu_custom_call" | custom-call | flops 2500000000 | tf_op jit(solution)/shard_map/input_backward/pallas_call | solution.py:364
  496.3 9.7 %collective-permute-done.37 = bf16[144,1152]{1,0:T(8,128)(2,1)S(1)} collective-permute-done((bf16[144,1152]{1,0:T(8,128)(2,1)S(1)}, bf16[144,1152]{1,0:T(8,128)(2,1)S(1)}, u32[]{:S(2)}, u32[]{:S(2)}) %collective-permute-start.37) | collective-permute-done | bytes 331808 | tf_op jit(solution)/shard_map/ppermute | solution.py:64
  506.0 3.1 fusion.5
  514.4 5.0 lay_small_grads.1
  524.9 4.3 collective-permute-done.42
  531.7 4.6 collective-permute-done.43
  544.2 3.9 join_tokens.2
  550.3 3.5 collective-permute-done.46
  553.9 6.3 %collective-permute-done.47 = bf16[144,1152]{1,0:T(8,128)(2,1)S(1)} collective-permute-done((bf16[144,1152]{1,0:T(8,128)(2,1)S(1)}, bf16[144,1152]{1,0:T(8,128)(2,1)S(1)}, u32[]{:S(2)}, u32[]{:S(2)}) %collective-permute-start.47) | collective-permute-done | bytes 331808 | tf_op jit(solution)/shard_map/ppermute | solution.py:64
  566.5 3.8 all-to-all-start.2
  573.1 4.4 collective-permute-done.50
  586.1 3.7 collective-permute-done.52
  595.7 3.0 all-to-all-done.2.pieces_ref
  600.2 4.4 join_tokens.3
  (256 shorter events, 118.9 us)
Async XLA Ops:
  7.2 195.3 %all-gather.3.cloned.1.call-start = ((), (), s32[]{:S(2)}) async-start(), calls=%async_computation.5 | async-start | bytes 10948608 | tf_op jit(solution)/shard_map/all_gather | solution.py:1366
  8.6 14.4 %collective-permute-start = (bf16[144,1152]{1,0:T(8,128)(2,1)S(1)}, bf16[144,1152]{1,0:T(8,128)(2,1)S(1)}, u32[]{:S(2)}, u32[]{:S(2)}) collective-permute-start(bf16[144,1152]{1,0:T(8,128)(2,1)S(1)} %concatenate.28), channel_id=1, source_target_pairs={{0,8},{1,9},{2,10},{3,11},{4,12},{5,13},{6,14},{7,15},{8,16},{9,17... | collective-permute-start | bytes 995336 | tf_op jit(solution)/shard_map/ppermute | solution.py:64
  11.7 11.3 %collective-permute-start.3 = (bf16[144,1152]{1,0:T(8,128)(2,1)}, bf16[144,1152]{1,0:T(8,128)(2,1)S(1)}, u32[]{:S(2)}, u32[]{:S(2)}) collective-permute-start(bf16[144,1152]{1,0:T(8,128)(2,1)} %bitcast.231), channel_id=1, source_target_pairs={{0,4},{1,5},{2,6},{3,7},{4,0},{5,1},{6,2},{7,3},{8,12},{9,13},{10,... | collective-permute-start | bytes 995336 | tf_op jit(solution)/shard_map/ppermute | solution.py:64
  15.6 14.5 %collective-permute-start.1 = (bf16[1,4,288,256]{3,2,1,0:T(8,128)(2,1)S(1)}, bf16[1,4,288,256]{3,2,1,0:T(8,128)(2,1)S(1)}, u32[]{:S(2)}, u32[]{:S(2)}) collective-permute-start(bf16[1,4,288,256]{3,2,1,0:T(8,128)(2,1)S(1)} %get-tuple-element.311), channel_id=1, source_target_pairs={{0,2},{1,3},{2,0},{3,1},{4,6},{5,7},{6,4},{7,5},{8,10},{9,11},{10,... | collective-permute-start | bytes 1769480 | tf_op jit(solution)/shard_map/ppermute | solution.py:64
  31.4 13.6 %collective-permute-start.5 = (bf16[1,4,288,256]{3,2,1,0:T(8,128)(2,1)S(1)}, bf16[1,4,288,256]{3,2,1,0:T(8,128)(2,1)S(1)}, u32[]{:S(2)}, u32[]{:S(2)}) collective-permute-start(bf16[1,4,288,256]{3,2,1,0:T(8,128)(2,1)S(1)} %dynamic-slice_bitcast_fusion.2), channel_id=1, source_target_pairs={{0,2},{1,3},{2,0},{3,1},{4,6},{5,7},{6,4},{7,5},{8,10},{9,11},{10,... | collective-permute-start | bytes 1769480 | tf_op jit(solution)/shard_map/ppermute | solution.py:64
  33.0 10.4 %collective-permute-start.4 = (bf16[144,1152]{1,0:T(8,128)(2,1)S(1)}, bf16[144,1152]{1,0:T(8,128)(2,1)S(1)}, u32[]{:S(2)}, u32[]{:S(2)}) collective-permute-start(bf16[144,1152]{1,0:T(8,128)(2,1)S(1)} %collective-permute-done), channel_id=1, source_target_pairs={{0,8},{1,9},{2,10},{3,11},{4,12},{5,13},{6,14},{7,15},{8,16},{9,17... | collective-permute-start | bytes 995336 | tf_op jit(solution)/shard_map/ppermute | solution.py:64
  34.5 8.8 %collective-permute-start.6 = (f32[24,288]{1,0:T(8,128)S(1)}, f32[24,288]{1,0:T(8,128)S(1)}, u32[]{:S(2)}, u32[]{:S(2)}) collective-permute-start(f32[24,288]{1,0:T(8,128)S(1)} %add.840), channel_id=1, source_target_pairs={{0,8},{1,9},{2,10},{3,11},{4,12},{5,13},{6,14},{7,15},{8,16},{9,17... | collective-permute-start | bytes 82952 | tf_op jit(solution)/shard_map/ppermute | solution.py:64
  45.0 12.0 %collective-permute-start.8 = (f32[24,288]{1,0:T(8,128)S(1)}, f32[24,288]{1,0:T(8,128)S(1)}, u32[]{:S(2)}, u32[]{:S(2)}) collective-permute-start(f32[24,288]{1,0:T(8,128)S(1)} %add.845), channel_id=1, source_target_pairs={{0,16},{1,17},{2,18},{3,19},{4,20},{5,21},{6,22},{7,23},{8,24},{9,... | collective-permute-start | bytes 82952 | tf_op jit(solution)/shard_map/ppermute | solution.py:64
  47.6 9.4 %collective-permute-start.7 = (bf16[144,1152]{1,0:T(8,128)(2,1)S(1)}, bf16[144,1152]{1,0:T(8,128)(2,1)S(1)}, u32[]{:S(2)}, u32[]{:S(2)}) collective-permute-start(bf16[144,1152]{1,0:T(8,128)(2,1)S(1)} %collective-permute-done.4), channel_id=1, source_target_pairs={{0,8},{1,9},{2,10},{3,11},{4,12},{5,13},{6,14},{7,15},{8,16},{9,17... | collective-permute-start | bytes 995336 | tf_op jit(solution)/shard_map/ppermute | solution.py:64
  49.3 24.2 %collective-permute-start.11 = (bf16[2,4,288,256]{3,2,1,0:T(8,128)(2,1)}, bf16[2,4,288,256]{3,2,1,0:T(8,128)(2,1)}, u32[]{:S(2)}, u32[]{:S(2)}) collective-permute-start(bf16[2,4,288,256]{3,2,1,0:T(8,128)(2,1)} %pad_maximum_fusion.1), channel_id=1, source_target_pairs={{0,1},{1,0},{2,3},{3,2},{4,5},{5,4},{6,7},{7,6},{8,9},{9,8},{10,11... | collective-permute-start | bytes 3538952 | tf_op jit(solution)/shard_map/ppermute | solution.py:64
  49.4 24.1 %collective-permute-start.10 = (bf16[288,1152]{1,0:T(8,128)(2,1)S(1)}, bf16[288,1152]{1,0:T(8,128)(2,1)S(1)}, u32[]{:S(2)}, u32[]{:S(2)}) collective-permute-start(bf16[288,1152]{1,0:T(8,128)(2,1)S(1)} %constant_dynamic-update-slice_fusion.2), channel_id=1, source_target_pairs={{0,4},{1,5},{2,6},{3,7},{4,0},{5,1},{6,2},{7,3},{8,12},{9,13},{10,... | collective-permute-start | bytes 1990664 | tf_op jit(solution)/shard_map/ppermute | solution.py:64
  57.2 16.3 %collective-permute-start.9 = (bf16[288,1152]{1,0:T(8,128)(2,1)S(1)}, bf16[288,1152]{1,0:T(8,128)(2,1)S(1)}, u32[]{:S(2)}, u32[]{:S(2)}) collective-permute-start(bf16[288,1152]{1,0:T(8,128)(2,1)S(1)} %constant_dynamic-update-slice_fusion), channel_id=1, source_target_pairs={{0,2},{1,3},{2,0},{3,1},{4,6},{5,7},{6,4},{7,5},{8,10},{9,11},{10,... | collective-permute-start | bytes 1990664 | tf_op jit(solution)/shard_map/ppermute | solution.py:64
  58.9 12.5 %collective-permute-start.12 = (f32[29,288]{1,0:T(8,128)S(1)}, f32[29,288]{1,0:T(8,128)S(1)}, u32[]{:S(2)}, u32[]{:S(2)}) collective-permute-start(f32[29,288]{1,0:T(8,128)S(1)} %get-tuple-element.319), channel_id=1, source_target_pairs={{0,2},{1,3},{2,0},{3,1},{4,6},{5,7},{6,4},{7,5},{8,10},{9,11},{10,... | collective-permute-start | bytes 100232 | tf_op jit(solution)/shard_map/ppermute | solution.py:64
  74.5 38.5 %collective-permute-start.15 = (bf16[576,1152]{1,0:T(8,128)(2,1)S(1)}, bf16[576,1152]{1,0:T(8,128)(2,1)}, u32[]{:S(2)}, u32[]{:S(2)}) collective-permute-start(bf16[576,1152]{1,0:T(8,128)(2,1)S(1)} %constant_dynamic-update-slice_fusion.6.refs_2_), channel_id=1, source_target_pairs={{0,2},{1,3},{2,0},{3,1},{4,6},{5,7},{6,4},{7,5},{8,10},{9,11},{10,... | collective-permute-start | bytes 3981320 | tf_op jit(solution)/shard_map/ppermute | solution.py:64
  76.3 40.7 %collective-permute-start.14 = (bf16[576,1152]{1,0:T(8,128)(2,1)S(1)}, bf16[576,1152]{1,0:T(8,128)(2,1)}, u32[]{:S(2)}, u32[]{:S(2)}) collective-permute-start(bf16[576,1152]{1,0:T(8,128)(2,1)S(1)} %constant_dynamic-update-slice_fusion.4.refs_0_), channel_id=1, source_target_pairs={{0,4},{1,5},{2,6},{3,7},{4,0},{5,1},{6,2},{7,3},{8,12},{9,13},{10,... | collective-permute-start | bytes 3981320 | tf_op jit(solution)/shard_map/ppermute | solution.py:64
  77.5 51.8 %collective-permute-start.18 = (bf16[576,1152]{1,0:T(8,128)(2,1)S(1)}, bf16[576,1152]{1,0:T(8,128)(2,1)}, u32[]{:S(2)}, u32[]{:S(2)}) collective-permute-start(bf16[576,1152]{1,0:T(8,128)(2,1)S(1)} %constant_dynamic-update-slice_fusion.6.refs_2_), channel_id=1, source_target_pairs={{0,1},{1,0},{2,3},{3,2},{4,5},{5,4},{6,7},{7,6},{8,9},{9,8},{10,11... | collective-permute-start | bytes 3981320 | tf_op jit(solution)/shard_map/ppermute | solution.py:64
  77.6 51.7 %collective-permute-start.16 = (bf16[576,1152]{1,0:T(8,128)(2,1)S(1)}, bf16[576,1152]{1,0:T(8,128)(2,1)}, u32[]{:S(2)}, u32[]{:S(2)}) collective-permute-start(bf16[576,1152]{1,0:T(8,128)(2,1)S(1)} %constant_dynamic-update-slice_fusion.4.refs_0_), channel_id=1, source_target_pairs={{0,1},{1,0},{2,3},{3,2},{4,5},{5,4},{6,7},{7,6},{8,9},{9,8},{10,11... | collective-permute-start | bytes 3981320 | tf_op jit(solution)/shard_map/ppermute | solution.py:64
  117.0 12.4 %collective-permute-start.17 = (bf16[576,1152]{1,0:T(8,128)(2,1)}, bf16[576,1152]{1,0:T(8,128)(2,1)}, u32[]{:S(2)}, u32[]{:S(2)}) collective-permute-start(bf16[576,1152]{1,0:T(8,128)(2,1)} %collective-permute-done.14.refs_1_), channel_id=1, source_target_pairs={{0,1},{1,0},{2,3},{3,2},{4,5},{5,4},{6,7},{7,6},{8,9},{9,8},{10,11... | collective-permute-start | bytes 3981320 | tf_op jit(solution)/shard_map/ppermute | solution.py:64
  117.0 12.4 %collective-permute-start.19 = (bf16[576,1152]{1,0:T(8,128)(2,1)}, bf16[576,1152]{1,0:T(8,128)(2,1)}, u32[]{:S(2)}, u32[]{:S(2)}) collective-permute-start(bf16[576,1152]{1,0:T(8,128)(2,1)} %collective-permute-done.15.refs_3_), channel_id=1, source_target_pairs={{0,1},{1,0},{2,3},{3,2},{4,5},{5,4},{6,7},{7,6},{8,9},{9,8},{10,11... | collective-permute-start | bytes 3981320 | tf_op jit(solution)/shard_map/ppermute | solution.py:64
  119.4 25.6 %collective-permute-start.20 = (bf16[2,144,1152]{2,1,0:T(8,128)(2,1)}, bf16[2,144,1152]{2,1,0:T(8,128)(2,1)}, u32[]{:S(2)}, u32[]{:S(2)}) collective-permute-start(bf16[2,144,1152]{2,1,0:T(8,128)(2,1)} %pad_maximum_fusion.2), channel_id=1, source_target_pairs={{0,2},{1,3},{2,0},{3,1},{4,6},{5,7},{6,4},{7,5},{8,10},{9,11},{10,... | collective-permute-start | bytes 1990664 | tf_op jit(solution)/shard_map/ppermute | solution.py:64
  124.8 59.3 %all-to-all-start = ((bf16[4,4,288,256]{3,2,1,0:T(8,128)(2,1)}), bf16[4,4,288,256]{3,2,1,0:T(8,128)(2,1)}, u32[]{:S(2)}, u32[]{:S(2)}) async-start(bf16[4,4,288,256]{3,2,1,0:T(8,128)(2,1)} %cut_tokens.1), calls=%async_computation | async-start | bytes 4718592 | tf_op jit(solution)/shard_map/all_to_all | solution.py:267
  146.4 47.5 %collective-permute-start.21 = (bf16[2,2,144,1152]{3,2,1,0:T(8,128)(2,1)S(1)}, bf16[2,2,144,1152]{3,2,1,0:T(8,128)(2,1)S(1)}, u32[]{:S(2)}, u32[]{:S(2)}) collective-permute-start(bf16[2,2,144,1152]{3,2,1,0:T(8,128)(2,1)S(1)} %pad_maximum_fusion.refs_0_), channel_id=1, source_target_pairs={{0,8},{1,9},{2,10},{3,11},{4,12},{5,13},{6,14},{7,15},{8,16},{9,17... | collective-permute-start | bytes 3981320 | tf_op jit(solution)/shard_map/ppermute | solution.py:64
  193.9 37.8 %collective-permute-start.22 = (bf16[2,2,144,1152]{3,2,1,0:T(8,128)(2,1)S(1)}, bf16[2,2,144,1152]{3,2,1,0:T(8,128)(2,1)}, u32[]{:S(2)}, u32[]{:S(2)}) collective-permute-start(bf16[2,2,144,1152]{3,2,1,0:T(8,128)(2,1)S(1)} %pad_maximum_fusion.refs_0_), channel_id=1, source_target_pairs={{0,1},{1,0},{2,3},{3,2},{4,5},{5,4},{6,7},{7,6},{8,9},{9,8},{10,11... | collective-permute-start | bytes 3981320 | tf_op jit(solution)/shard_map/ppermute | solution.py:64
  193.9 37.8 %collective-permute-start.24 = (bf16[2,2,144,1152]{3,2,1,0:T(8,128)(2,1)S(1)}, bf16[2,2,144,1152]{3,2,1,0:T(8,128)(2,1)}, u32[]{:S(2)}, u32[]{:S(2)}) collective-permute-start(bf16[2,2,144,1152]{3,2,1,0:T(8,128)(2,1)S(1)} %collective-permute-done.21.refs_1_), channel_id=1, source_target_pairs={{0,8},{1,9},{2,10},{3,11},{4,12},{5,13},{6,14},{7,15},{8,16},{9,17... | collective-permute-start | bytes 3981320 | tf_op jit(solution)/shard_map/ppermute | solution.py:64
  194.4 37.3 %collective-permute-start.23 = (bf16[2,2,144,1152]{3,2,1,0:T(8,128)(2,1)S(1)}, bf16[2,2,144,1152]{3,2,1,0:T(8,128)(2,1)}, u32[]{:S(2)}, u32[]{:S(2)}) collective-permute-start(bf16[2,2,144,1152]{3,2,1,0:T(8,128)(2,1)S(1)} %collective-permute-done.21.refs_1_), channel_id=1, source_target_pairs={{0,1},{1,0},{2,3},{3,2},{4,5},{5,4},{6,7},{7,6},{8,9},{9,8},{10,11... | collective-permute-start | bytes 3981320 | tf_op jit(solution)/shard_map/ppermute | solution.py:64
  231.7 33.4 %collective-permute-start.25 = (bf16[2,2,144,1152]{3,2,1,0:T(8,128)(2,1)}, bf16[2,2,144,1152]{3,2,1,0:T(8,128)(2,1)S(1)}, u32[]{:S(2)}, u32[]{:S(2)}) collective-permute-start(bf16[2,2,144,1152]{3,2,1,0:T(8,128)(2,1)} %collective-permute-done.24.refs_2_), channel_id=1, source_target_pairs={{0,8},{1,9},{2,10},{3,11},{4,12},{5,13},{6,14},{7,15},{8,16},{9,17... | collective-permute-start | bytes 3981320 | tf_op jit(solution)/shard_map/ppermute | solution.py:64
  231.8 33.3 %collective-permute-start.26 = (bf16[2,2,144,1152]{3,2,1,0:T(8,128)(2,1)}, bf16[2,2,144,1152]{3,2,1,0:T(8,128)(2,1)S(1)}, u32[]{:S(2)}, u32[]{:S(2)}) collective-permute-start(bf16[2,2,144,1152]{3,2,1,0:T(8,128)(2,1)} %collective-permute-done.24.refs_2_), channel_id=1, source_target_pairs={{0,1},{1,0},{2,3},{3,2},{4,5},{5,4},{6,7},{7,6},{8,9},{9,8},{10,11... | collective-permute-start | bytes 3981320 | tf_op jit(solution)/shard_map/ppermute | solution.py:64
  290.5 34.6 %all-to-all-start.1 = ((bf16[4,4,288,256]{3,2,1,0:T(8,128)(2,1)}), bf16[4,4,288,256]{3,2,1,0:T(8,128)(2,1)S(1)}, u32[]{:S(2)}, u32[]{:S(2)}) async-start(bf16[4,4,288,256]{3,2,1,0:T(8,128)(2,1)} %get-tuple-element.228), calls=%async_computation.1 | async-start | bytes 4718592 | tf_op jit(solution)/shard_map/all_to_all | solution.py:267
  294.1 268.5 %reduce-scatter.2.cloned.1.call-start = ((), (), s32[]{:S(2)}) async-start(), calls=%async_computation.4 | async-start | bytes 10948608 | tf_op jit(solution)/shard_map/reduce_scatter | solution.py:1407
  325.1 11.3 %collective-permute-start.28 = (bf16[2,2,576,1152]{3,2,1,0:T(8,128)(2,1)}, bf16[2,2,576,1152]{3,2,1,0:T(8,128)(2,1)}, u32[]{:S(2)}, u32[]{:S(2)}) collective-permute-start(bf16[2,2,576,1152]{3,2,1,0:T(8,128)(2,1)} %up_weight_grad.2), channel_id=1, source_target_pairs={{0,1},{1,0},{2,3},{3,2},{4,5},{5,4},{6,7},{7,6},{8,9},{9,8},{10,11... | collective-permute-start | bytes 15925256 | tf_op jit(solution)/shard_map/ppermute | solution.py:64
  338.4 31.6 %collective-permute-start.29 = (bf16[2,2,144,1152]{3,2,1,0:T(8,128)(2,1)S(1)}, bf16[2,2,144,1152]{3,2,1,0:T(8,128)(2,1)S(1)}, u32[]{:S(2)}, u32[]{:S(2)}) collective-permute-start(bf16[2,2,144,1152]{3,2,1,0:T(8,128)(2,1)S(1)} %fusion), channel_id=1, source_target_pairs={{0,2},{1,3},{2,0},{3,1},{4,6},{5,7},{6,4},{7,5},{8,10},{9,11},{10,... | collective-permute-start | bytes 3981320 | tf_op jit(solution)/shard_map/ppermute | solution.py:64
  373.6 47.9 %collective-permute-start.31 = (bf16[2,2,144,1152]{3,2,1,0:T(8,128)(2,1)}, bf16[2,2,144,1152]{3,2,1,0:T(8,128)(2,1)S(1)}, u32[]{:S(2)}, u32[]{:S(2)}) collective-permute-start(bf16[2,2,144,1152]{3,2,1,0:T(8,128)(2,1)} %fusion.1), channel_id=1, source_target_pairs={{0,2},{1,3},{2,0},{3,1},{4,6},{5,7},{6,4},{7,5},{8,10},{9,11},{10,... | collective-permute-start | bytes 3981320 | tf_op jit(solution)/shard_map/ppermute | solution.py:64
  377.7 43.8 %collective-permute-start.30 = (bf16[2,144,1152]{2,1,0:T(8,128)(2,1)}, bf16[2,144,1152]{2,1,0:T(8,128)(2,1)}, u32[]{:S(2)}, u32[]{:S(2)}) collective-permute-start(bf16[2,144,1152]{2,1,0:T(8,128)(2,1)} %fusion.7), channel_id=1, source_target_pairs={{0,4},{1,5},{2,6},{3,7},{4,0},{5,1},{6,2},{7,3},{8,12},{9,13},{10,... | collective-permute-start | bytes 1990664 | tf_op jit(solution)/shard_map/ppermute | solution.py:64
  437.2 22.3 %collective-permute-start.32 = (bf16[2,2,576,1152]{3,2,1,0:T(8,128)(2,1)}, bf16[2,2,576,1152]{3,2,1,0:T(8,128)(2,1)}, u32[]{:S(2)}, u32[]{:S(2)}) collective-permute-start(bf16[2,2,576,1152]{3,2,1,0:T(8,128)(2,1)} %first_weight_grad.2), channel_id=1, source_target_pairs={{0,1},{1,0},{2,3},{3,2},{4,5},{5,4},{6,7},{7,6},{8,9},{9,8},{10,11... | collective-permute-start | bytes 15925256 | tf_op jit(solution)/shard_map/ppermute | solution.py:64
  437.2 22.3 %collective-permute-start.33 = (bf16[2,144,1152]{2,1,0:T(8,128)(2,1)}, bf16[2,144,1152]{2,1,0:T(8,128)(2,1)S(1)}, u32[]{:S(2)}, u32[]{:S(2)}) collective-permute-start(bf16[2,144,1152]{2,1,0:T(8,128)(2,1)} %fusion.6), channel_id=1, source_target_pairs={{0,4},{1,5},{2,6},{3,7},{4,0},{5,1},{6,2},{7,3},{8,12},{9,13},{10,... | collective-permute-start | bytes 1990664 | tf_op jit(solution)/shard_map/ppermute | solution.py:64
  465.9 40.1 %collective-permute-start.34 = (bf16[2,2,144,1152]{3,2,1,0:T(8,128)(2,1)}, bf16[2,2,144,1152]{3,2,1,0:T(8,128)(2,1)S(1)}, u32[]{:S(2)}, u32[]{:S(2)}) collective-permute-start(bf16[2,2,144,1152]{3,2,1,0:T(8,128)(2,1)} %fusion.2), channel_id=1, source_target_pairs={{0,4},{1,5},{2,6},{3,7},{4,0},{5,1},{6,2},{7,3},{8,12},{9,13},{10,... | collective-permute-start | bytes 3981320 | tf_op jit(solution)/shard_map/ppermute | solution.py:64
  467.5 38.5 %collective-permute-start.35 = (bf16[2,2,144,1152]{3,2,1,0:T(8,128)(2,1)}, bf16[2,2,144,1152]{3,2,1,0:T(8,128)(2,1)}, u32[]{:S(2)}, u32[]{:S(2)}) collective-permute-start(bf16[2,2,144,1152]{3,2,1,0:T(8,128)(2,1)} %fusion.3), channel_id=1, source_target_pairs={{0,2},{1,3},{2,0},{3,1},{4,6},{5,7},{6,4},{7,5},{8,10},{9,11},{10,... | collective-permute-start | bytes 3981320 | tf_op jit(solution)/shard_map/ppermute | solution.py:64
  470.0 26.3 %collective-permute-start.36 = (bf16[144,1152]{1,0:T(8,128)(2,1)}, bf16[144,1152]{1,0:T(8,128)(2,1)S(1)}, u32[]{:S(2)}, u32[]{:S(2)}) collective-permute-start(bf16[144,1152]{1,0:T(8,128)(2,1)} %fusion.20), channel_id=1, source_target_pairs={{0,24},{1,25},{2,26},{3,27},{4,28},{5,29},{6,30},{7,31},{8,0},{9,1... | collective-permute-start | bytes 995336 | tf_op jit(solution)/shard_map/ppermute | solution.py:64
  473.5 32.4 %collective-permute-start.37 = (bf16[144,1152]{1,0:T(8,128)(2,1)S(1)}, bf16[144,1152]{1,0:T(8,128)(2,1)S(1)}, u32[]{:S(2)}, u32[]{:S(2)}) collective-permute-start(bf16[144,1152]{1,0:T(8,128)(2,1)S(1)} %get-tuple-element.308), channel_id=1, source_target_pairs={{0,16},{1,17},{2,18},{3,19},{4,20},{5,21},{6,22},{7,23},{8,24},{9,... | collective-permute-start | bytes 995336 | tf_op jit(solution)/shard_map/ppermute | solution.py:64
  473.6 32.4 %collective-permute-start.38 = (bf16[144,1152]{1,0:T(8,128)(2,1)S(1)}, bf16[144,1152]{1,0:T(8,128)(2,1)S(1)}, u32[]{:S(2)}, u32[]{:S(2)}) collective-permute-start(bf16[144,1152]{1,0:T(8,128)(2,1)S(1)} %get-tuple-element.307), channel_id=1, source_target_pairs={{0,8},{1,9},{2,10},{3,11},{4,12},{5,13},{6,14},{7,15},{8,16},{9,17... | collective-permute-start | bytes 995336 | tf_op jit(solution)/shard_map/ppermute | solution.py:64
  511.7 24.6 %collective-permute-start.40 = (bf16[2,144,1152]{2,1,0:T(8,128)(2,1)}, bf16[2,144,1152]{2,1,0:T(8,128)(2,1)S(1)}, u32[]{:S(2)}, u32[]{:S(2)}) collective-permute-start(bf16[2,144,1152]{2,1,0:T(8,128)(2,1)} %fusion.4), channel_id=1, source_target_pairs={{0,4},{1,5},{2,6},{3,7},{4,0},{5,1},{6,2},{7,3},{8,12},{9,13},{10,... | collective-permute-start | bytes 1990664 | tf_op jit(solution)/shard_map/ppermute | solution.py:64
  512.3 24.0 %collective-permute-start.39 = (bf16[2,144,1152]{2,1,0:T(8,128)(2,1)}, bf16[2,144,1152]{2,1,0:T(8,128)(2,1)S(1)}, u32[]{:S(2)}, u32[]{:S(2)}) collective-permute-start(bf16[2,144,1152]{2,1,0:T(8,128)(2,1)} %fusion.5), channel_id=1, source_target_pairs={{0,2},{1,3},{2,0},{3,1},{4,6},{5,7},{6,4},{7,5},{8,10},{9,11},{10,... | collective-permute-start | bytes 1990664 | tf_op jit(solution)/shard_map/ppermute | solution.py:64
  522.5 6.7 %collective-permute-start.42 = (f32[2,29,288]{2,1,0:T(8,128)S(1)}, f32[2,29,288]{2,1,0:T(8,128)S(1)}, u32[]{:S(2)}, u32[]{:S(2)}) collective-permute-start(f32[2,29,288]{2,1,0:T(8,128)S(1)} %slice_add_fusion), channel_id=1, source_target_pairs={{0,8},{1,9},{2,10},{3,11},{4,12},{5,13},{6,14},{7,15},{8,16},{9,17... | collective-permute-start | bytes 200456 | tf_op jit(solution)/shard_map/ppermute | solution.py:64
  529.2 7.0 %collective-permute-start.43 = (f32[2,29,288]{2,1,0:T(8,128)S(1)}, f32[2,29,288]{2,1,0:T(8,128)S(1)}, u32[]{:S(2)}, u32[]{:S(2)}) collective-permute-start(f32[2,29,288]{2,1,0:T(8,128)S(1)} %add.1008), channel_id=1, source_target_pairs={{0,16},{1,17},{2,18},{3,19},{4,20},{5,21},{6,22},{7,23},{8,24},{9,... | collective-permute-start | bytes 200456 | tf_op jit(solution)/shard_map/ppermute | solution.py:64
  538.6 11.1 %collective-permute-start.45 = (bf16[144,1152]{1,0:T(8,128)(2,1)}, bf16[144,1152]{1,0:T(8,128)(2,1)S(1)}, u32[]{:S(2)}, u32[]{:S(2)}) collective-permute-start(bf16[144,1152]{1,0:T(8,128)(2,1)} %fusion.17), channel_id=1, source_target_pairs={{0,24},{1,25},{2,26},{3,27},{4,28},{5,29},{6,30},{7,31},{8,0},{9,1... | collective-permute-start | bytes 995336 | tf_op jit(solution)/shard_map/ppermute | solution.py:64
  544.2 16.0 %collective-permute-start.47 = (bf16[144,1152]{1,0:T(8,128)(2,1)S(1)}, bf16[144,1152]{1,0:T(8,128)(2,1)S(1)}, u32[]{:S(2)}, u32[]{:S(2)}) collective-permute-start(bf16[144,1152]{1,0:T(8,128)(2,1)S(1)} %get-tuple-element.306), channel_id=1, source_target_pairs={{0,16},{1,17},{2,18},{3,19},{4,20},{5,21},{6,22},{7,23},{8,24},{9,... | collective-permute-start | bytes 995336 | tf_op jit(solution)/shard_map/ppermute | solution.py:64
  564.5 13.0 %collective-permute-start.50 = (bf16[144,1152]{1,0:T(8,128)(2,1)}, bf16[144,1152]{1,0:T(8,128)(2,1)}, u32[]{:S(2)}, u32[]{:S(2)}) collective-permute-start(bf16[144,1152]{1,0:T(8,128)(2,1)} %get-tuple-element.305), channel_id=1, source_target_pairs={{0,8},{1,9},{2,10},{3,11},{4,12},{5,13},{6,14},{7,15},{8,16},{9,17... | collective-permute-start | bytes 995336 | tf_op jit(solution)/shard_map/ppermute | solution.py:64
  566.5 32.3 %all-to-all-start.2 = ((bf16[4,4,288,256]{3,2,1,0:T(8,128)(2,1)}), bf16[4,4,288,256]{3,2,1,0:T(8,128)(2,1)S(1)}, u32[]{:S(2)}, u32[]{:S(2)}) async-start(bf16[4,4,288,256]{3,2,1,0:T(8,128)(2,1)} %get-tuple-element.295), calls=%async_computation.2 | async-start | bytes 4718592 | tf_op jit(solution)/shard_map/all_to_all | solution.py:267
  (50 other events, 478.3 us)
Sparse Core Ops, SparseCore 0:
  74.5 123.8 all-gather.2
  340.6 161.0 reduce-scatter.1
where the time goes:
time: 622 us; the launch traced here: 612 us
  Pallas kernels  315 us (51%)
  waiting for transfers between devices  151 us (24%)
  starting transfers between devices  60.3 us (10%)
  other arithmetic  46 us (7%)
  local copies, waits for them, and re-layouts  20 us (3%)
  between operations  15.4 us (2%)
    pallas_call x22, Pallas kernels, call(): pl.pallas_call(kernel, grid_spec=pltpu.PrefetchScalarGridSpec(num_scalar_...  315 us
    ppermute x54, waiting for transfers between devices, send(): return lax.ppermute(value, both, pairs)  147 us
    ppermute x54, starting transfers between devices, send(): return lax.ppermute(value, both, pairs)  48.1 us
    convert_element_type x8, other arithmetic, sums(): self.total(self.at(axis, k)).astype(low)  23.2 us
  transfers between devices with their start and end apart: 59, of which 28 were waited for; matrix products, arithmetic and copies ran while one was open for 10% of the time, Pallas kernels for 47%

commit v1 on v0

--- a/solution.py
+++ b/solution.py
@@ -12,6 +12,8 @@
 FRAMES = 16
 BLOCK = 128
 MIB = 1024 * 1024
+FORWARD_SHARE = 8
+BACKWARD_SHARE = 4
 COSTS = {
     "project_qkv": 15,
     "attention_forward": 24,
@@ -767,15 +769,22 @@
     blocks = shape.tokens // BLOCK
     score_scale = 1.0 / math.sqrt(HEAD_DIM)
 
+    share = math.gcd(blocks, FORWARD_SHARE)
+
     def kernel(qkv_ref, row_ref, column_ref, out_ref, probs_ref):
+        for sub in range(share):
+            one_block(qkv_ref, row_ref, column_ref, out_ref, probs_ref, sub)
+
+    def one_block(qkv_ref, row_ref, column_ref, out_ref, probs_ref, sub):
+        at = slice(sub * BLOCK, (sub + 1) * BLOCK)
         rows_at = lax.broadcasted_iota(jnp.int32, (BLOCK, BLOCK), 0)
         columns_at = lax.broadcasted_iota(jnp.int32, (BLOCK, BLOCK), 1)
         allowed = (rows_at // FRAMES == columns_at // FRAMES) & (
-            ((column_ref[...] > 0) & (row_ref[...] > 0)) | (rows_at == columns_at)
+            ((column_ref[at] > 0) & (row_ref[:, at] > 0)) | (rows_at == columns_at)
         )
-        queries = qkv_ref[0, :width].astype(high)
-        key_rows = qkv_ref[0, width : 2 * width].astype(high)
-        value_rows = qkv_ref[0, 2 * width : 3 * width].astype(high)
+        queries = qkv_ref[0, :width, at].astype(high)
+        key_rows = qkv_ref[0, width : 2 * width, at].astype(high)
+        value_rows = qkv_ref[0, 2 * width : 3 * width, at].astype(high)
         parts = [jnp.zeros((shape.out_skip, BLOCK), high)]
         for head in range(heads):
             scores = (
@@ -785,30 +794,30 @@
             exp_scores = jnp.exp(scores - jnp.max(scores, axis=0, keepdims=True))
             probs = exp_scores * (1.0 / jnp.sum(exp_scores, axis=0, keepdims=True))
             probs_low = probs.astype(low)
-            probs_ref[0, 0, head] = probs_low
+            probs_ref[sub, 0, head] = probs_low
             parts.append(contract(head_rows(value_rows, head), probs_low, 1, 0))
-        out_ref[0] = jnp.concatenate(parts, axis=0).astype(low)
+        out_ref[0, :, at] = jnp.concatenate(parts, axis=0).astype(low)
 
     return call(
         kernel,
         "attention_forward",
-        (blocks, shape.panels),
+        (blocks // share, shape.panels),
         [
-            (qkv, (1, qkv.shape[1], BLOCK), lambda b, n: (n, 0, b)),
-            (in_clip[None, :], (1, BLOCK), lambda b, n: (0, b)),
-            (in_clip[:, None], (BLOCK, 1), lambda b, n: (b, 0)),
+            (qkv, (1, qkv.shape[1], share * BLOCK), lambda b, n: (n, 0, b)),
+            (in_clip[None, :], (1, share * BLOCK), lambda b, n: (0, b)),
+            (in_clip[:, None], (share * BLOCK, 1), lambda b, n: (b, 0)),
         ],
         [
             (
                 (shape.panels, shape.out_rows, shape.tokens),
                 low,
-                (1, shape.out_rows, BLOCK),
+                (1, shape.out_rows, share * BLOCK),
                 lambda b, n: (n, 0, b),
             ),
             (
                 (blocks, shape.panels, heads, BLOCK, BLOCK),
                 low,
-                (1, 1, heads, BLOCK, BLOCK),
+                (share, 1, heads, BLOCK, BLOCK),
                 lambda b, n: (b, n, 0, 0, 0),
             ),
         ],
@@ -821,14 +830,21 @@
     blocks = shape.tokens // BLOCK
     score_scale = 1.0 / math.sqrt(HEAD_DIM)
 
+    share = math.gcd(blocks, BACKWARD_SHARE)
+
     def kernel(qkv_ref, probs_ref, grad_ref, out_ref):
-        queries = qkv_ref[0, :width].astype(high)
-        key_rows = qkv_ref[0, width : 2 * width].astype(high)
-        value_rows = qkv_ref[0, 2 * width : 3 * width].astype(high)
-        grads = grad_ref[0].astype(high)[shape.out_skip :]
+        for sub in range(share):
+            one_block(qkv_ref, probs_ref, grad_ref, out_ref, sub)
+
+    def one_block(qkv_ref, probs_ref, grad_ref, out_ref, sub):
+        at = slice(sub * BLOCK, (sub + 1) * BLOCK)
+        queries = qkv_ref[0, :width, at].astype(high)
+        key_rows = qkv_ref[0, width : 2 * width, at].astype(high)
+        value_rows = qkv_ref[0, 2 * width : 3 * width, at].astype(high)
+        grads = grad_ref[0, :, at].astype(high)[shape.out_skip :]
         query_parts, key_parts, value_parts = [], [], []
         for head in range(heads):
-            probs_low = probs_ref[0, 0, head]
+            probs_low = probs_ref[sub, 0, head]
             grad_head = head_rows(grads, head)
             value_parts.append(contract(grad_head, probs_low, 1, 1))
             grad_probs = contract(head_rows(value_rows, head), grad_head, 0, 0)
@@ -838,24 +854,24 @@
             query_parts.append(contract(head_rows(key_rows, head), grad_scores, 1, 0) * score_scale)
             key_parts.append(contract(head_rows(queries, head), grad_scores, 1, 1) * score_scale)
         rest = [jnp.zeros((shape.qkv_rows - 3 * width, BLOCK), high)]
-        out_ref[0] = jnp.concatenate(
+        out_ref[0, :, at] = jnp.concatenate(
             query_parts + key_parts + value_parts + rest, axis=0
         ).astype(low)
 
     return call(
         kernel,
         "attention_backward",
-        (blocks, shape.panels),
+        (blocks // share, shape.panels),
         [
-            (qkv, (1, qkv.shape[1], BLOCK), lambda b, n: (n, 0, b)),
-            (probs, (1, 1, heads, BLOCK, BLOCK), lambda b, n: (b, n, 0, 0, 0)),
-            (grad_attended, (1, shape.out_rows, BLOCK), lambda b, n: (n, 0, b)),
+            (qkv, (1, qkv.shape[1], share * BLOCK), lambda b, n: (n, 0, b)),
+            (probs, (share, 1, heads, BLOCK, BLOCK), lambda b, n: (b, n, 0, 0, 0)),
+            (grad_attended, (1, shape.out_rows, share * BLOCK), lambda b, n: (n, 0, b)),
         ],
         [
             (
                 (shape.panels, shape.qkv_rows, shape.tokens),
                 low,
-                (1, shape.qkv_rows, BLOCK),
+                (1, shape.qkv_rows, share * BLOCK),
                 lambda b, n: (n, 0, b),
             )
         ],
@@ -1308,7 +1324,7 @@
     own_slope = lax.dynamic_slice_in_dim(silu_slope, wide_at * own_rows, own_rows, axis=1)
 
     first_piece = jnp.concatenate([query_weight, key_weight, value_weight, out_weight.T], axis=1)
-    first, down = Gather(first_piece), LateGather(down_weight.T)
+    first, up = Gather(first_piece), Gather(up_weight)
     order = device_order()
     mod_part = jnp.einsum("sd,dje->jse", own_cond, ada_weight, preferred_element_type=high)
     mod_part = mod_part.reshape(6 * seqs, local_width)
@@ -1320,17 +1336,14 @@
     token_swap = NarrowSwap(tokens.reshape(local_shape))
     token_same = token_swap.step(0)
     mod_part = mod_part + send(mod_part, **hops[0])
-    down.side()
-    first.ring, token_same, mod_part, down.line, token_swap.parts = sync(
-        first.ring, token_same, mod_part, down.line, token_swap.parts
+    first.ring, token_same, mod_part, token_swap.parts = sync(
+        first.ring, token_same, mod_part, token_swap.parts
     )
 
     first.step()
     token_other = token_swap.step(1)
     mod_part = mod_part + send(mod_part, **hops[1])
-    first.ring, token_other, mod_part, down.line = sync(
-        first.ring, token_other, mod_part, down.line
-    )
+    first.ring, token_other, mod_part = sync(first.ring, token_other, mod_part)
 
     for at in range(2, max(deep - 1, len(hops))):
         if at < len(hops):
@@ -1345,6 +1358,7 @@
         first.ring, mod_part = sync(first.ring, mod_part)
 
     first.rear_tall()
+    up.step()
     mod_own = (
         mod_part.reshape(6, seqs, local_width) + ada_bias.astype(high)[:, None, :]
     ).reshape(6 * seqs, local_width)
@@ -1357,59 +1371,59 @@
             ]
         )
     )
-    first.rear, first.rear_got, first.front, first.front_got, token_far, small = sync(
-        first.rear, first.rear_got, first.front, first.front_got, token_far, small
+    first.rear, first.rear_got, first.front, first.front_got, token_far, small, up.ring = sync(
+        first.rear, first.rear_got, first.front, first.front_got, token_far, small, up.ring
     )
 
     first.second()
     first.core(0, 2)
-    up_full = lax.all_gather(after(up_weight, small), both, axis=0, tiled=False)
+    for _ in range(2, deep):
+        up.step()
     table, up_bias_full = lay_small(shape, came, small, wide_count)
     token_parts = token_near + [token_far[k : k + 1] for k in range(panels // 2)]
     frame_at = jnp.arange(shape.part) % FRAMES
     in_clip = (frame_at[None, :] < clip_frames.reshape(seqs)[:, None]).astype(jnp.int32).reshape(-1)
     residual, input_one = prepare_tokens(shape, came, token_parts, table, wide_count)
-    first.arrays, input_one, down.line = sync(first.arrays, input_one, down.line)
+    upstream_cut = cut_tokens(shape, after(cotangent.reshape(local_shape), input_one))
+    first.arrays, input_one, up.ring, upstream_cut = sync(
+        first.arrays, input_one, up.ring, upstream_cut
+    )
 
     first.core(*[k for k in range(len(first.arrays)) if k not in (0, 2)])
     qkv_weights = Weights(first.result(), 0, shape.qkv_rows)
     out_weights = Weights(first.result(), shape.out_from)
-    down.along_tall()
-    upstream_cut = cut_tokens(shape, after(cotangent.reshape(local_shape), input_one))
+    up.front_side()
+    up.rear_tall()
+    qkv = project_qkv(shape, qkv_weights, input_one)
+    qkv, up.front, up.front_got, up.rear, up.rear_got = sync(
+        qkv, up.front, up.front_got, up.rear, up.rear_got
+    )
+
+    up.second()
+    up.core(0, 2)
+    down_full = lax.all_gather(after(down_weight.T, qkv), both, axis=0, tiled=False)
+    attended, probs = attention_forward(shape, qkv, in_clip)
+    attended, up.arrays = sync(attended, up.arrays)
+
+    up.core(*[k for k in range(len(up.arrays)) if k not in (0, 2)])
     upstream_parts = swap_narrow(upstream_cut)
-    qkv = project_qkv(shape, qkv_weights, after(input_one, upstream_cut))
-    qkv, down.plane = sync(qkv, down.plane)
-
-    down.step()
-    attended, probs = attention_forward(shape, qkv, in_clip)
-    (attended,) = sync(attended)
-
     middle, branch, input_two = project_out(shape, out_weights, attended, residual, table)
-    middle, input_two, down.ring, upstream_parts = sync(
-        middle, input_two, down.ring, upstream_parts
-    )
+    middle, input_two, up.cores = sync(middle, input_two, up.cores)
+
+    up_all = Weights(up.result())
+    hidden, slope = project_up(shape, up_all, input_two, up_bias_full)
+    hidden, slope, upstream_parts = sync(hidden, slope, upstream_parts)
 
     upstream, grad_mlp, down_bias_part = prepare_upstream(
         shape, there, upstream_parts, table, wide_count
     )
-    down.step()
-    down.core(0, 1)
-    up_all = GatheredWeights(up_full, order, panels)
-    hidden, slope = project_up(shape, up_all, after(input_two, grad_mlp), up_bias_full)
-    hidden, slope, down.cores, down.ring = sync(hidden, slope, down.cores, down.ring)
-
-    for k in range(3, deep):
-        down.step()
-    down.core(*range(2, deep - 1))
     down_grads = device_weight_grad(
         shape, "down_weight_grad", grad_mlp, hidden, order, wide_count
     )
     down_grad = lax.psum_scatter(
         down_grads, ("narrow", "wide"), scatter_dimension=0, tiled=False
     ).astype(high)
-    down_grads, down.ring = sync(down_grads, down.ring)
-    down.core(deep - 1)
-    down_all = Weights(down.result())
+    down_all = GatheredWeights(down_full, order, panels)
     output_parts, gate_two_part = project_down(
         shape, there, down_all, after(hidden, down_grads), middle, upstream, table, wide_count
     )
@@ -1448,29 +1462,32 @@
     up_parts[1].along("x", side_sums)
     grad_qkv = after(grad_qkv, *side_sums)
     other = first_weight_grad(shape, input_one, grad_qkv, grad_branch, attended, 1)
-    *_, other = sync(up_parts[0], other)
+    *_, other = sync(*up_parts, other)
 
     first_sum = GradSum(other)
-    near = first_weight_grad(shape, after(input_one, other), grad_qkv, grad_branch, attended, 0)
-    near, first_sum.got, _ = sync(near, first_sum.got, up_parts[1])
+    up_sums = deep_sums(up_parts)
+    along_deep(up_parts, up_sums)
+    near = first_weight_grad(
+        shape, after(input_one, other, *up_sums), grad_qkv, grad_branch, attended, 0
+    )
+    near, first_sum.got = sync(near, first_sum.got)
     first_sum.near(near)
     first_parts = first_sum.split(half)
     side_sums, tall_sums = first_parts[0].sums("x"), first_parts[1].sums("y")
     first_parts[0].along("x", side_sums)
     first_parts[1].along("y", tall_sums)
-    up_sums = deep_sums(up_parts)
-    along_deep(up_parts, up_sums)
     input_parts, input_sums = input_backward(
         shape,
         there,
         qkv_weights,
-        after(grad_qkv, *side_sums, *tall_sums, *up_sums),
+        after(grad_qkv, *side_sums, *tall_sums),
         residual,
         grad_middle,
         table,
         wide_count,
     )
     *_, input_parts, input_sums = sync(*first_parts, up_parts[0], input_parts, input_sums)
+    input_got = swap_narrow(input_parts)
 
     tall_sums, side_sums = first_parts[0].sums("y"), first_parts[1].sums("x")
     first_parts[0].along("y", tall_sums)
@@ -1497,7 +1514,7 @@
     output = join_tokens(shape, after(output_got, small_grad), low)
     small_grad = after(small_grad, *sums)
     small_grad = small_grad + send(small_grad, side_by=1)
-    small_grad = after(small_grad, first_got[0], output)
+    small_grad = after(small_grad, output, input_got)
     small_grad = sum(
         [small_grad[0]] + [send(small_grad[k], tall_by=k) for k in range(1, panels // 2)]
     )
@@ -1506,18 +1523,17 @@
     up_bias_grad = small_grad[6 * seqs + 1 :].reshape(-1)
     ada_grad = jnp.einsum("sd,jse->dje", own_cond.astype(high), own_mod, precision=highest)
     ada_bias_grad = jnp.sum(own_mod, axis=1)
-    own_mod = after(own_mod, *first_got[1:2])
+    input_grad = join_tokens(shape, after(input_got, own_mod), high)
+    own_mod = after(own_mod, *first_got[:1], input_grad)
     cond_local = sum_narrow(
         own_slope * jnp.einsum("jse,dje->sd", own_mod, ada_weight.astype(high), precision=highest)
     )
-    input_got = swap_narrow(after(input_parts, cond_local))
     cond_local = after(cond_local, *first_got)
     cond_grad = sum_wide(
         lax.dynamic_update_slice_in_dim(
             jnp.zeros((seqs, full_width), high), cond_local, wide_at * own_rows, axis=1
         )
     )
-    input_grad = join_tokens(shape, after(input_got, cond_grad), high)
     up_grad = up_parts[0].total()
     first_grad = first_parts[0].total()
     table_grad = jnp.einsum("sc,sd->cd", class_hot.astype(high), cond_grad, precision=highest)

time: 622 us -> 596 us (0.958)
  waiting for transfers between devices: 151 us -> 114 us
  starting transfers between devices: 60.3 us -> 81.1 us
  Pallas kernels: 315 us -> 301 us
  local copies, waits for them, and re-layouts: 20 us -> 29.3 us
    ppermute x54 -> x56, waiting for transfers between devices: 147 us -> 114 us  [send(): return lax.ppermute(value, both, pairs)]
    ppermute x54 -> x56, starting transfers between devices: 48.1 us -> 69.9 us  [send(): return lax.ppermute(value, both, pairs)]
    pallas_call x22, Pallas kernels: 315 us -> 301 us  [call(): pl.pallas_call(kernel, grid_spec=pltpu.PrefetchScalarGridSpec(num_scalar_...]
  transfers between devices with their start and end apart: 59 -> 61, of which waited for: 28 -> 24; matrix products, arithmetic and copies ran while one was open for 10% -> 11% of each run, Pallas kernels for 47% -> 48%
where the time goes in v1:
time: 596 us; the launch traced here: 587 us
  Pallas kernels  301 us (51%)
  waiting for transfers between devices  114 us (19%)
  starting transfers between devices  81.1 us (14%)
  other arithmetic  41.8 us (7%)
  local copies, waits for them, and re-layouts  29.3 us (5%)
  between operations  15.5 us (3%)
    pallas_call x22, Pallas kernels, call(): pl.pallas_call(kernel, grid_spec=pltpu.PrefetchScalarGridSpec(num_scalar_...  301 us
    ppermute x56, waiting for transfers between devices, send(): return lax.ppermute(value, both, pairs)  114 us
    ppermute x56, starting transfers between devices, send(): return lax.ppermute(value, both, pairs)  69.9 us
    convert_element_type x8, other arithmetic, sums(): self.total(self.at(axis, k)).astype(low)  22.1 us
  transfers between devices with their start and end apart: 61, of which 24 were waited for; matrix products, arithmetic and copies ran while one was open for 11% of the time, Pallas kernels for 48%

profile of v1, /device:TPU:0, one launch (start us, length us, event | category | flops | bytes accessed | tf_op | source)
XLA Modules:
  0.0 587.3 jit_solution(11882424557930231956)
XLA Ops:
  9.9 3.0 collective-permute-start.1
  20.4 4.0 collective-permute-done
  32.5 7.9 %collective-permute-done.5 = f32[24,288]{1,0:T(8,128)S(1)} collective-permute-done((f32[24,288]{1,0:T(8,128)S(1)}, f32[24,288]{1,0:T(8,128)S(1)}, u32[]{:S(2)}, u32[]{:S(2)}) %collective-permute-start.5) | collective-permute-done | bytes 27680 | tf_op jit(solution)/shard_map/ppermute | solution.py:66
  49.0 5.4 collective-permute-done.7
  56.9 12.7 %collective-permute-done.11 = f32[29,288]{1,0:T(8,128)S(1)} collective-permute-done((f32[29,288]{1,0:T(8,128)S(1)}, f32[29,288]{1,0:T(8,128)S(1)}, u32[]{:S(2)}, u32[]{:S(2)}) %collective-permute-start.11) | collective-permute-done | bytes 33440 | tf_op jit(solution)/shard_map/ppermute | solution.py:66
  77.2 4.4 lay_small.1
  81.5 6.2 %collective-permute-done.16 = bf16[144,1152]{1,0:T(8,128)(2,1)} collective-permute-done((bf16[144,1152]{1,0:T(8,128)(2,1)}, bf16[144,1152]{1,0:T(8,128)(2,1)}, u32[]{:S(2)}, u32[]{:S(2)}) %collective-permute-start.16) | collective-permute-done | bytes 331808 | tf_op jit(solution)/shard_map/ppermute | solution.py:66
  90.0 6.9 %prepare_tokens.1 = (bf16[1152,1024]{1,0:T(8,128)(2,1)}, bf16[1152,1024]{1,0:T(8,128)(2,1)}) custom-call(s32[8]{0:T(128)} %stack.196.at_ref, bf16[1,4,288,256]{3,2,1,0:T(8,128)(2,1)} %get-tuple-element.307.refs_0_, bf16[1,4,288,256]{3,2,1,0:T(8,128)(2,1)} %copy-done.14, bf16[1,4,288,256]{3,2,1,0:T(8,128)(2,1)} %get-tuple-element.311.refs_2_, ...), custom_call_target="tpu_custom_call" | custom-call | flops 400000000 | tf_op jit(solution)/shard_map/prepare_tokens/pallas_call | solution.py:366
  96.9 3.9 cut_tokens.1
  100.8 3.3 collective-permute-done.15.refs_3_
  114.3 15.1 %project_qkv.1.qkv_ref = bf16[4,896,1024]{2,1,0:T(8,128)(2,1)} custom-call(bf16[576,1152]{1,0:T(8,128)(2,1)} %copy-done.2, bf16[576,1152]{1,0:T(8,128)(2,1)} %collective-permute-done.14.refs_1_, bf16[576,1152]{1,0:T(8,128)(2,1)} %copy-done.1, bf16[576,1152]{1,0:T(8,128)(2,1)} %collective-permute-done.15.refs_3_, ...), custom_call_target="tpu_custom_call" | custom-call | flops 1500000000 | tf_op jit(solution)/shard_map/project_qkv/pallas_call | solution.py:366
  139.7 3.8 all-to-all-start
  144.1 17.5 %attention_forward.1 = (bf16[4,384,1024]{2,1,0:T(8,128)(2,1)}, bf16[8,4,4,128,128]{4,3,2,1,0:T(8,128)(2,1)}) custom-call(bf16[4,896,1024]{2,1,0:T(8,128)(2,1)} %project_qkv.1.qkv_ref, s32[1,1024]{1,0:T(1,128)} %bitcast.231, s32[1024,1]{1,0:T(8,128)} %bitcast.225), custom_call_target="tpu_custom_call" | custom-call | flops 2400000000 | tf_op jit(solution)/shard_map/attention_forward/pallas_call | solution.py:366
  161.6 10.4 %collective-permute-done.25.refs_3_ = bf16[576,1152]{1,0:T(8,128)(2,1)} collective-permute-done((bf16[576,1152]{1,0:T(8,128)(2,1)}, bf16[576,1152]{1,0:T(8,128)(2,1)}, u32[]{:S(2)}, u32[]{:S(2)}) %collective-permute-start.25) | collective-permute-done | bytes 1327136 | tf_op jit(solution)/shard_map/ppermute | solution.py:66
  172.0 6.8 %collective-permute-done.24.refs_1_ = bf16[576,1152]{1,0:T(8,128)(2,1)} collective-permute-done((bf16[576,1152]{1,0:T(8,128)(2,1)}, bf16[576,1152]{1,0:T(8,128)(2,1)}, u32[]{:S(2)}, u32[]{:S(2)}) %collective-permute-start.24) | collective-permute-done | bytes 1327136 | tf_op jit(solution)/shard_map/ppermute | solution.py:66
  180.6 11.6 %project_out.1 = (f32[1152,1024]{1,0:T(8,128)}, bf16[1152,1024]{1,0:T(8,128)(2,1)}, bf16[1152,1024]{1,0:T(8,128)(2,1)}) custom-call(bf16[576,1152]{1,0:T(8,128)(2,1)} %copy-done.2, bf16[576,1152]{1,0:T(8,128)(2,1)} %collective-permute-done.14.refs_1_, bf16[576,1152]{1,0:T(8,128)(2,1)} %copy-done.1, bf16[576,1152]{1,0:T(8,128)(2,1)} %collective-permute-done.15.refs_3_, ...), custom_call_target="tpu_custom_call" | custom-call | flops 1700000000 | tf_op jit(solution)/shard_map/project_out/pallas_call | solution.py:366
  192.2 28.6 %project_up.1 = (bf16[4,1152,1024]{2,1,0:T(8,128)(2,1)}, bf16[4,1152,1024]{2,1,0:T(8,128)(2,1)}) custom-call(bf16[576,1152]{1,0:T(8,128)(2,1)} %constant_dynamic-update-slice_fusion.12.refs_0_, bf16[576,1152]{1,0:T(8,128)(2,1)} %collective-permute-done.24.refs_1_, bf16[576,1152]{1,0:T(8,128)(2,1)} %constant_dynamic-update-slice_fusion.14.refs_2_, ...), custom_call_target="tpu_custom_call" | custom-call | flops 2800000000 | tf_op jit(solution)/shard_map/project_up/pallas_call | solution.py:366
  222.2 6.5 %prepare_upstream.1 = (bf16[1152,1024]{1,0:T(8,128)(2,1)}, bf16[1152,1024]{1,0:T(8,128)(2,1)}, f32[1152,1]{1,0:T(8,128)}) custom-call(s32[8]{0:T(128)} %stack.238.at_ref, bf16[4,4,288,256]{3,2,1,0:T(8,128)(2,1)} %copy-done.5, f32[1152,29]{1,0:T(8,128)} %get-tuple-element.179.refs_4_.refs_10_.table_ref.refs_5_.refs_12_.refs_11_), custom_call_target="tpu_custom_call" | custom-call | flops 400000000 | tf_op jit(solution)/shard_map/prepare_upstream/pallas_call | solution.py:366
  228.7 17.8 %down_weight_grad.1 = bf16[4,8,144,1152]{3,2,1,0:T(8,128)(2,1)} custom-call(s32[32]{0:T(128)} %stack.229.order_ref.refs_0_, bf16[1152,1024]{1,0:T(8,128)(2,1)} %get-tuple-element.224.source_ref.refs_2_, bf16[4,1152,1024]{2,1,0:T(8,128)(2,1)} %get-tuple-element.220.grad_ref.refs_2_), custom_call_target="tpu_custom_call" | custom-call | flops 1000000000 | tf_op jit(solution)/shard_map/down_weight_grad/pallas_call | solution.py:366
  246.5 21.8 %project_down.1 = (bf16[4,4,288,256]{3,2,1,0:T(8,128)(2,1)}, f32[1152,4]{1,0:T(8,128)}) custom-call(s32[8]{0:T(128)} %stack.238.at_ref, s32[32]{0:T(128)} %stack.229.order_ref.refs_0_, bf16[32,144,1152]{2,1,0:T(8,128)(2,1)} %bitcast.204, bf16[4,1152,1024]{2,1,0:T(8,128)(2,1)} %get-tuple-element.220.grad_ref.refs_2_, ...), custom_call_target="tpu_custom_call" | custom-call | flops 2500000000 | tf_op jit(solution)/shard_map/project_down/pallas_call | solution.py:366
  268.3 3.6 all-to-all-start.1
  272.0 21.3 %hidden_backward.1 = (bf16[4,1152,1024]{2,1,0:T(8,128)(2,1)}, f32[4,1152,1]{2,1,0:T(8,128)}) custom-call(s32[32]{0:T(128)} %stack.229.order_ref.refs_0_, bf16[32,144,1152]{2,1,0:T(8,128)(2,1)} %bitcast.205, bf16[1152,1024]{1,0:T(8,128)(2,1)} %get-tuple-element.224.source_ref.refs_2_, bf16[4,1152,1024]{2,1,0:T(8,128)(2,1)} %get-tuple-element.225.refs_3_), custom_call_target="tpu_custom_call" | custom-call | flops 2100000000 | tf_op jit(solution)/shard_map/hidden_backward/pallas_call | solution.py:366
  293.3 10.5 %up_weight_grad.2 = bf16[2,2,576,1152]{3,2,1,0:T(8,128)(2,1)} custom-call(bf16[1152,1024]{1,0:T(8,128)(2,1)} %get-tuple-element.230.refs_8_.source_ref, bf16[4,1152,1024]{2,1,0:T(8,128)(2,1)} %get-tuple-element.233.grad_ref.refs_8_), custom_call_target="tpu_custom_call" | custom-call | flops 1000000000 | tf_op jit(solution)/shard_map/up_weight_grad/pallas_call | solution.py:366
  304.2 10.8 %up_weight_grad.3 = bf16[2,2,576,1152]{3,2,1,0:T(8,128)(2,1)} custom-call(bf16[1152,1024]{1,0:T(8,128)(2,1)} %get-tuple-element.230.refs_8_.source_ref, bf16[4,1152,1024]{2,1,0:T(8,128)(2,1)} %get-tuple-element.233.grad_ref.refs_8_), custom_call_target="tpu_custom_call" | custom-call | flops 1000000000 | tf_op jit(solution)/shard_map/up_weight_grad/pallas_call | solution.py:366
  319.1 26.1 %middle_backward.1 = (f32[1152,1024]{1,0:T(8,128)}, bf16[1152,1024]{1,0:T(8,128)(2,1)}, f32[1152,12]{1,0:T(8,128)}) custom-call(bf16[576,1152]{1,0:T(8,128)(2,1)} %constant_dynamic-update-slice_fusion.12.refs_0_, bf16[576,1152]{1,0:T(8,128)(2,1)} %collective-permute-done.24.refs_1_, bf16[576,1152]{1,0:T(8,128)(2,1)} %constant_dynamic-update-slice_fusion.14.refs_2_, ...), custom_call_target="tpu_custom_call" | custom-call | flops 3000000000 | tf_op jit(solution)/shard_map/middle_backward/pallas_call | solution.py:366
  345.2 3.4 collective-permute-done.31
  348.6 3.7 fusion.1
  356.9 9.3 %attended_backward.1.grad_ref = bf16[4,384,1024]{2,1,0:T(8,128)(2,1)} custom-call(bf16[576,1152]{1,0:T(8,128)(2,1)} %copy-done.2, bf16[576,1152]{1,0:T(8,128)(2,1)} %collective-permute-done.14.refs_1_, bf16[576,1152]{1,0:T(8,128)(2,1)} %copy-done.1, bf16[576,1152]{1,0:T(8,128)(2,1)} %collective-permute-done.15.refs_3_, ...), custom_call_target="tpu_custom_call" | custom-call | flops 900000000 | tf_op jit(solution)/shard_map/attended_backward/pallas_call | solution.py:366
  366.2 28.8 %attention_backward.1.qkv_ref.refs_8_ = bf16[4,896,1024]{2,1,0:T(8,128)(2,1)} custom-call(bf16[4,896,1024]{2,1,0:T(8,128)(2,1)} %project_qkv.1.qkv_ref, bf16[8,4,4,128,128]{4,3,2,1,0:T(8,128)(2,1)} %get-tuple-element.241.probs_ref, bf16[4,384,1024]{2,1,0:T(8,128)(2,1)} %attended_backward.1.grad_ref), custom_call_target="tpu_custom_call" | custom-call | flops 3300000000 | tf_op jit(solution)/shard_map/attention_backward/pallas_call | solution.py:366
  398.9 12.5 %first_weight_grad.2 = bf16[2,2,576,1152]{3,2,1,0:T(8,128)(2,1)} custom-call(bf16[1152,1024]{1,0:T(8,128)(2,1)} %get-tuple-element.262.refs_8_.source_ref, bf16[4,896,1024]{2,1,0:T(8,128)(2,1)} %attention_backward.1.qkv_ref.refs_8_, bf16[1152,1024]{1,0:T(8,128)(2,1)} %get-tuple-element.243.refs_8_.branch_ref, ...), custom_call_target="tpu_custom_call" | custom-call | flops 1200000000 | tf_op jit(solution)/shard_map/first_weight_grad/pallas_call | solution.py:366
  411.4 11.5 %collective-permute-done.34 = bf16[2,144,1152]{2,1,0:T(8,128)(2,1)} collective-permute-done((bf16[2,144,1152]{2,1,0:T(8,128)(2,1)}, bf16[2,144,1152]{2,1,0:T(8,128)(2,1)}, u32[]{:S(2)}, u32[]{:S(2)}) %collective-permute-start.34) | collective-permute-done | bytes 663584 | tf_op jit(solution)/shard_map/ppermute | solution.py:66
  424.9 2.7 fusion.18
  427.7 12.5 %first_weight_grad.3 = bf16[2,2,576,1152]{3,2,1,0:T(8,128)(2,1)} custom-call(bf16[1152,1024]{1,0:T(8,128)(2,1)} %get-tuple-element.262.refs_8_.source_ref, bf16[4,896,1024]{2,1,0:T(8,128)(2,1)} %attention_backward.1.qkv_ref.refs_8_, bf16[1152,1024]{1,0:T(8,128)(2,1)} %get-tuple-element.243.refs_8_.branch_ref, ...), custom_call_target="tpu_custom_call" | custom-call | flops 1200000000 | tf_op jit(solution)/shard_map/first_weight_grad/pallas_call | solution.py:366
  440.1 3.1 fusion.3
  443.9 3.1 fusion.2
  450.3 3.6 collective-permute-start.38
  453.8 22.0 %input_backward.1 = (bf16[4,4,288,256]{3,2,1,0:T(8,128)(2,1)}, f32[1152,8]{1,0:T(8,128)}) custom-call(s32[8]{0:T(128)} %stack.238.at_ref, bf16[576,1152]{1,0:T(8,128)(2,1)} %copy-done.2, bf16[576,1152]{1,0:T(8,128)(2,1)} %collective-permute-done.14.refs_1_, bf16[576,1152]{1,0:T(8,128)(2,1)} %copy-done.1, bf16[576,1152]{1,0:T(8,128)(2,1)} %collective-permute-done.15.refs_3_, ...), custom_call_target="tpu_custom_call" | custom-call | flops 2500000000 | tf_op jit(solution)/shard_map/input_backward/pallas_call | solution.py:366
  475.9 5.0 collective-permute-done.36
  480.9 2.9 fusion.4
  489.1 3.6 all-to-all-start.2
  493.7 5.0 lay_small_grads.1
  502.0 8.6 %collective-permute-start.44 = (f32[2,29,288]{2,1,0:T(8,128)S(1)}, f32[2,29,288]{2,1,0:T(8,128)S(1)}, u32[]{:S(2)}, u32[]{:S(2)}) collective-permute-start(f32[2,29,288]{2,1,0:T(8,128)S(1)} %slice_add_fusion), channel_id=1, source_target_pairs={{0,8},{1,9},{2,10},{3,11},{4,12},{5,13},{6,14},{7,15},{8,16},{9,17... | collective-permute-start | bytes 200456 | tf_op jit(solution)/shard_map/ppermute | solution.py:66
  515.3 5.4 collective-permute-done.45
  528.1 3.9 join_tokens.2
  535.5 5.7 collective-permute-start.51
  541.9 4.4 join_tokens.3
  551.6 10.7 %collective-permute-done.51 = bf16[144,1152]{1,0:T(8,128)(2,1)} collective-permute-done((bf16[144,1152]{1,0:T(8,128)(2,1)}, bf16[144,1152]{1,0:T(8,128)(2,1)}, u32[]{:S(2)}, u32[]{:S(2)}) %collective-permute-start.51) | collective-permute-done | bytes 331808 | tf_op jit(solution)/shard_map/ppermute | solution.py:66
  570.7 3.6 collective-permute-done.54
  (255 shorter events, 127.0 us)
Async XLA Ops:
  7.2 239.3 %all-gather.3.cloned.1.call-start = ((), (), s32[]{:S(2)}) async-start(), calls=%async_computation.5 | async-start | bytes 10948608 | tf_op jit(solution)/shard_map/all_gather | solution.py:1404
  9.9 16.3 %collective-permute-start.1 = (bf16[1,4,288,256]{3,2,1,0:T(8,128)(2,1)S(1)}, bf16[1,4,288,256]{3,2,1,0:T(8,128)(2,1)S(1)}, u32[]{:S(2)}, u32[]{:S(2)}) collective-permute-start(bf16[1,4,288,256]{3,2,1,0:T(8,128)(2,1)S(1)} %get-tuple-element.309), channel_id=1, source_target_pairs={{0,2},{1,3},{2,0},{3,1},{4,6},{5,7},{6,4},{7,5},{8,10},{9,11},{10,... | collective-permute-start | bytes 1769480 | tf_op jit(solution)/shard_map/ppermute | solution.py:66
  13.2 11.2 %collective-permute-start = (bf16[144,1152]{1,0:T(8,128)(2,1)S(1)}, bf16[144,1152]{1,0:T(8,128)(2,1)S(1)}, u32[]{:S(2)}, u32[]{:S(2)}) collective-permute-start(bf16[144,1152]{1,0:T(8,128)(2,1)S(1)} %concatenate.40), channel_id=1, source_target_pairs={{0,8},{1,9},{2,10},{3,11},{4,12},{5,13},{6,14},{7,15},{8,16},{9,17... | collective-permute-start | bytes 995336 | tf_op jit(solution)/shard_map/ppermute | solution.py:66
  27.6 14.6 %collective-permute-start.4 = (bf16[1,4,288,256]{3,2,1,0:T(8,128)(2,1)S(1)}, bf16[1,4,288,256]{3,2,1,0:T(8,128)(2,1)S(1)}, u32[]{:S(2)}, u32[]{:S(2)}) collective-permute-start(bf16[1,4,288,256]{3,2,1,0:T(8,128)(2,1)S(1)} %dynamic-slice_bitcast_fusion.2), channel_id=1, source_target_pairs={{0,2},{1,3},{2,0},{3,1},{4,6},{5,7},{6,4},{7,5},{8,10},{9,11},{10,... | collective-permute-start | bytes 1769480 | tf_op jit(solution)/shard_map/ppermute | solution.py:66
  29.4 11.0 %collective-permute-start.3 = (bf16[144,1152]{1,0:T(8,128)(2,1)S(1)}, bf16[144,1152]{1,0:T(8,128)(2,1)S(1)}, u32[]{:S(2)}, u32[]{:S(2)}) collective-permute-start(bf16[144,1152]{1,0:T(8,128)(2,1)S(1)} %collective-permute-done), channel_id=1, source_target_pairs={{0,8},{1,9},{2,10},{3,11},{4,12},{5,13},{6,14},{7,15},{8,16},{9,17... | collective-permute-start | bytes 995336 | tf_op jit(solution)/shard_map/ppermute | solution.py:66
  42.1 12.4 %collective-permute-start.7 = (f32[24,288]{1,0:T(8,128)S(1)}, f32[24,288]{1,0:T(8,128)S(1)}, u32[]{:S(2)}, u32[]{:S(2)}) collective-permute-start(f32[24,288]{1,0:T(8,128)S(1)} %add.845), channel_id=1, source_target_pairs={{0,16},{1,17},{2,18},{3,19},{4,20},{5,21},{6,22},{7,23},{8,24},{9,... | collective-permute-start | bytes 82952 | tf_op jit(solution)/shard_map/ppermute | solution.py:66
  44.6 9.9 %collective-permute-start.6 = (bf16[144,1152]{1,0:T(8,128)(2,1)S(1)}, bf16[144,1152]{1,0:T(8,128)(2,1)S(1)}, u32[]{:S(2)}, u32[]{:S(2)}) collective-permute-start(bf16[144,1152]{1,0:T(8,128)(2,1)S(1)} %collective-permute-done.3), channel_id=1, source_target_pairs={{0,8},{1,9},{2,10},{3,11},{4,12},{5,13},{6,14},{7,15},{8,16},{9,17... | collective-permute-start | bytes 995336 | tf_op jit(solution)/shard_map/ppermute | solution.py:66
  47.3 25.2 %collective-permute-start.10 = (bf16[2,4,288,256]{3,2,1,0:T(8,128)(2,1)}, bf16[2,4,288,256]{3,2,1,0:T(8,128)(2,1)}, u32[]{:S(2)}, u32[]{:S(2)}) collective-permute-start(bf16[2,4,288,256]{3,2,1,0:T(8,128)(2,1)} %pad_maximum_fusion), channel_id=1, source_target_pairs={{0,1},{1,0},{2,3},{3,2},{4,5},{5,4},{6,7},{7,6},{8,9},{9,8},{10,11... | collective-permute-start | bytes 3538952 | tf_op jit(solution)/shard_map/ppermute | solution.py:66
  47.5 24.2 %collective-permute-start.9 = (bf16[288,1152]{1,0:T(8,128)(2,1)S(1)}, bf16[288,1152]{1,0:T(8,128)(2,1)S(1)}, u32[]{:S(2)}, u32[]{:S(2)}) collective-permute-start(bf16[288,1152]{1,0:T(8,128)(2,1)S(1)} %constant_dynamic-update-slice_fusion.2), channel_id=1, source_target_pairs={{0,4},{1,5},{2,6},{3,7},{4,0},{5,1},{6,2},{7,3},{8,12},{9,13},{10,... | collective-permute-start | bytes 1990664 | tf_op jit(solution)/shard_map/ppermute | solution.py:66
  54.6 17.1 %collective-permute-start.8 = (bf16[288,1152]{1,0:T(8,128)(2,1)S(1)}, bf16[288,1152]{1,0:T(8,128)(2,1)S(1)}, u32[]{:S(2)}, u32[]{:S(2)}) collective-permute-start(bf16[288,1152]{1,0:T(8,128)(2,1)S(1)} %constant_dynamic-update-slice_fusion), channel_id=1, source_target_pairs={{0,2},{1,3},{2,0},{3,1},{4,6},{5,7},{6,4},{7,5},{8,10},{9,11},{10,... | collective-permute-start | bytes 1990664 | tf_op jit(solution)/shard_map/ppermute | solution.py:66
  56.3 13.4 %collective-permute-start.11 = (f32[29,288]{1,0:T(8,128)S(1)}, f32[29,288]{1,0:T(8,128)S(1)}, u32[]{:S(2)}, u32[]{:S(2)}) collective-permute-start(f32[29,288]{1,0:T(8,128)S(1)} %get-tuple-element.317), channel_id=1, source_target_pairs={{0,2},{1,3},{2,0},{3,1},{4,6},{5,7},{6,4},{7,5},{8,10},{9,11},{10,... | collective-permute-start | bytes 100232 | tf_op jit(solution)/shard_map/ppermute | solution.py:66
  56.9 14.8 %collective-permute-start.13 = (bf16[144,1152]{1,0:T(8,128)(2,1)}, bf16[144,1152]{1,0:T(8,128)(2,1)}, u32[]{:S(2)}, u32[]{:S(2)}) collective-permute-start(bf16[144,1152]{1,0:T(8,128)(2,1)} %param.24), channel_id=1, source_target_pairs={{0,8},{1,9},{2,10},{3,11},{4,12},{5,13},{6,14},{7,15},{8,16},{9,17... | collective-permute-start | bytes 995336 | tf_op jit(solution)/shard_map/ppermute | solution.py:66
  72.7 31.4 %collective-permute-start.15 = (bf16[576,1152]{1,0:T(8,128)(2,1)S(1)}, bf16[576,1152]{1,0:T(8,128)(2,1)}, u32[]{:S(2)}, u32[]{:S(2)}) collective-permute-start(bf16[576,1152]{1,0:T(8,128)(2,1)S(1)} %constant_dynamic-update-slice_fusion.6.refs_2_), channel_id=1, source_target_pairs={{0,2},{1,3},{2,0},{3,1},{4,6},{5,7},{6,4},{7,5},{8,10},{9,11},{10,... | collective-permute-start | bytes 3981320 | tf_op jit(solution)/shard_map/ppermute | solution.py:66
  74.5 31.3 %collective-permute-start.14 = (bf16[576,1152]{1,0:T(8,128)(2,1)S(1)}, bf16[576,1152]{1,0:T(8,128)(2,1)}, u32[]{:S(2)}, u32[]{:S(2)}) collective-permute-start(bf16[576,1152]{1,0:T(8,128)(2,1)S(1)} %constant_dynamic-update-slice_fusion.4.refs_0_), channel_id=1, source_target_pairs={{0,4},{1,5},{2,6},{3,7},{4,0},{5,1},{6,2},{7,3},{8,12},{9,13},{10,... | collective-permute-start | bytes 3981320 | tf_op jit(solution)/shard_map/ppermute | solution.py:66
  76.0 11.6 %collective-permute-start.16 = (bf16[144,1152]{1,0:T(8,128)(2,1)}, bf16[144,1152]{1,0:T(8,128)(2,1)}, u32[]{:S(2)}, u32[]{:S(2)}) collective-permute-start(bf16[144,1152]{1,0:T(8,128)(2,1)} %collective-permute-done.13), channel_id=1, source_target_pairs={{0,8},{1,9},{2,10},{3,11},{4,12},{5,13},{6,14},{7,15},{8,16},{9,17... | collective-permute-start | bytes 995336 | tf_op jit(solution)/shard_map/ppermute | solution.py:66
  76.7 36.1 %collective-permute-start.20 = (bf16[576,1152]{1,0:T(8,128)(2,1)S(1)}, bf16[576,1152]{1,0:T(8,128)(2,1)}, u32[]{:S(2)}, u32[]{:S(2)}) collective-permute-start(bf16[576,1152]{1,0:T(8,128)(2,1)S(1)} %constant_dynamic-update-slice_fusion.6.refs_2_), channel_id=1, source_target_pairs={{0,1},{1,0},{2,3},{3,2},{4,5},{5,4},{6,7},{7,6},{8,9},{9,8},{10,11... | collective-permute-start | bytes 3981320 | tf_op jit(solution)/shard_map/ppermute | solution.py:66
  76.7 37.6 %collective-permute-start.18 = (bf16[576,1152]{1,0:T(8,128)(2,1)S(1)}, bf16[576,1152]{1,0:T(8,128)(2,1)}, u32[]{:S(2)}, u32[]{:S(2)}) collective-permute-start(bf16[576,1152]{1,0:T(8,128)(2,1)S(1)} %constant_dynamic-update-slice_fusion.4.refs_0_), channel_id=1, source_target_pairs={{0,1},{1,0},{2,3},{3,2},{4,5},{5,4},{6,7},{7,6},{8,9},{9,8},{10,11... | collective-permute-start | bytes 3981320 | tf_op jit(solution)/shard_map/ppermute | solution.py:66
  87.7 13.1 %collective-permute-start.17 = (bf16[144,1152]{1,0:T(8,128)(2,1)}, bf16[144,1152]{1,0:T(8,128)(2,1)S(1)}, u32[]{:S(2)}, u32[]{:S(2)}) collective-permute-start(bf16[144,1152]{1,0:T(8,128)(2,1)} %collective-permute-done.16), channel_id=1, source_target_pairs={{0,8},{1,9},{2,10},{3,11},{4,12},{5,13},{6,14},{7,15},{8,16},{9,17... | collective-permute-start | bytes 995336 | tf_op jit(solution)/shard_map/ppermute | solution.py:66
  108.8 20.6 %collective-permute-start.23 = (bf16[288,1152]{1,0:T(8,128)(2,1)}, bf16[288,1152]{1,0:T(8,128)(2,1)}, u32[]{:S(2)}, u32[]{:S(2)}) collective-permute-start(bf16[288,1152]{1,0:T(8,128)(2,1)} %constant_dynamic-update-slice_fusion.10), channel_id=1, source_target_pairs={{0,2},{1,3},{2,0},{3,1},{4,6},{5,7},{6,4},{7,5},{8,10},{9,11},{10,... | collective-permute-start | bytes 1990664 | tf_op jit(solution)/shard_map/ppermute | solution.py:66
  112.8 16.7 %collective-permute-start.22 = (bf16[288,1152]{1,0:T(8,128)(2,1)}, bf16[288,1152]{1,0:T(8,128)(2,1)S(1)}, u32[]{:S(2)}, u32[]{:S(2)}) collective-permute-start(bf16[288,1152]{1,0:T(8,128)(2,1)} %constant_dynamic-update-slice_fusion.8), channel_id=1, source_target_pairs={{0,4},{1,5},{2,6},{3,7},{4,0},{5,1},{6,2},{7,3},{8,12},{9,13},{10,... | collective-permute-start | bytes 1990664 | tf_op jit(solution)/shard_map/ppermute | solution.py:66
  132.5 39.5 %collective-permute-start.25 = (bf16[576,1152]{1,0:T(8,128)(2,1)}, bf16[576,1152]{1,0:T(8,128)(2,1)}, u32[]{:S(2)}, u32[]{:S(2)}) collective-permute-start(bf16[576,1152]{1,0:T(8,128)(2,1)} %constant_dynamic-update-slice_fusion.14.refs_2_), channel_id=1, source_target_pairs={{0,2},{1,3},{2,0},{3,1},{4,6},{5,7},{6,4},{7,5},{8,10},{9,11},{10,... | collective-permute-start | bytes 3981320 | tf_op jit(solution)/shard_map/ppermute | solution.py:66
  137.0 41.8 %collective-permute-start.24 = (bf16[576,1152]{1,0:T(8,128)(2,1)}, bf16[576,1152]{1,0:T(8,128)(2,1)}, u32[]{:S(2)}, u32[]{:S(2)}) collective-permute-start(bf16[576,1152]{1,0:T(8,128)(2,1)} %constant_dynamic-update-slice_fusion.12.refs_0_), channel_id=1, source_target_pairs={{0,4},{1,5},{2,6},{3,7},{4,0},{5,1},{6,2},{7,3},{8,12},{9,13},{10,... | collective-permute-start | bytes 3981320 | tf_op jit(solution)/shard_map/ppermute | solution.py:66
  139.7 81.1 %all-to-all-start = ((bf16[4,4,288,256]{3,2,1,0:T(8,128)(2,1)}), bf16[4,4,288,256]{3,2,1,0:T(8,128)(2,1)S(1)}, u32[]{:S(2)}, u32[]{:S(2)}) async-start(bf16[4,4,288,256]{3,2,1,0:T(8,128)(2,1)} %cut_tokens.1), calls=%async_computation | async-start | bytes 4718592 | tf_op jit(solution)/shard_map/all_to_all | solution.py:269
  143.5 48.7 %collective-permute-start.28 = (bf16[576,1152]{1,0:T(8,128)(2,1)}, bf16[576,1152]{1,0:T(8,128)(2,1)}, u32[]{:S(2)}, u32[]{:S(2)}) collective-permute-start(bf16[576,1152]{1,0:T(8,128)(2,1)} %constant_dynamic-update-slice_fusion.14.refs_2_), channel_id=1, source_target_pairs={{0,1},{1,0},{2,3},{3,2},{4,5},{5,4},{6,7},{7,6},{8,9},{9,8},{10,11... | collective-permute-start | bytes 3981320 | tf_op jit(solution)/shard_map/ppermute | solution.py:66
  144.0 48.1 %collective-permute-start.26 = (bf16[576,1152]{1,0:T(8,128)(2,1)}, bf16[576,1152]{1,0:T(8,128)(2,1)}, u32[]{:S(2)}, u32[]{:S(2)}) collective-permute-start(bf16[576,1152]{1,0:T(8,128)(2,1)} %constant_dynamic-update-slice_fusion.12.refs_0_), channel_id=1, source_target_pairs={{0,1},{1,0},{2,3},{3,2},{4,5},{5,4},{6,7},{7,6},{8,9},{9,8},{10,11... | collective-permute-start | bytes 3981320 | tf_op jit(solution)/shard_map/ppermute | solution.py:66
  178.8 13.4 %collective-permute-start.27 = (bf16[576,1152]{1,0:T(8,128)(2,1)}, bf16[576,1152]{1,0:T(8,128)(2,1)}, u32[]{:S(2)}, u32[]{:S(2)}) collective-permute-start(bf16[576,1152]{1,0:T(8,128)(2,1)} %collective-permute-done.24.refs_1_), channel_id=1, source_target_pairs={{0,1},{1,0},{2,3},{3,2},{4,5},{5,4},{6,7},{7,6},{8,9},{9,8},{10,11... | collective-permute-start | bytes 3981320 | tf_op jit(solution)/shard_map/ppermute | solution.py:66
  178.8 13.4 %collective-permute-start.29 = (bf16[576,1152]{1,0:T(8,128)(2,1)}, bf16[576,1152]{1,0:T(8,128)(2,1)}, u32[]{:S(2)}, u32[]{:S(2)}) collective-permute-start(bf16[576,1152]{1,0:T(8,128)(2,1)} %collective-permute-done.25.refs_3_), channel_id=1, source_target_pairs={{0,1},{1,0},{2,3},{3,2},{4,5},{5,4},{6,7},{7,6},{8,9},{9,8},{10,11... | collective-permute-start | bytes 3981320 | tf_op jit(solution)/shard_map/ppermute | solution.py:66
  268.3 35.5 %all-to-all-start.1 = ((bf16[4,4,288,256]{3,2,1,0:T(8,128)(2,1)}), bf16[4,4,288,256]{3,2,1,0:T(8,128)(2,1)S(1)}, u32[]{:S(2)}, u32[]{:S(2)}) async-start(bf16[4,4,288,256]{3,2,1,0:T(8,128)(2,1)} %get-tuple-element.227), calls=%async_computation.1 | async-start | bytes 4718592 | tf_op jit(solution)/shard_map/all_to_all | solution.py:269
  271.9 261.8 %reduce-scatter.2.cloned.1.call-start = ((), (), s32[]{:S(2)}) async-start(), calls=%async_computation.4 | async-start | bytes 10948608 | tf_op jit(solution)/shard_map/reduce_scatter | solution.py:1423
  303.7 11.3 %collective-permute-start.30 = (bf16[2,2,576,1152]{3,2,1,0:T(8,128)(2,1)}, bf16[2,2,576,1152]{3,2,1,0:T(8,128)(2,1)}, u32[]{:S(2)}, u32[]{:S(2)}) collective-permute-start(bf16[2,2,576,1152]{3,2,1,0:T(8,128)(2,1)} %up_weight_grad.2), channel_id=1, source_target_pairs={{0,1},{1,0},{2,3},{3,2},{4,5},{5,4},{6,7},{7,6},{8,9},{9,8},{10,11... | collective-permute-start | bytes 15925256 | tf_op jit(solution)/shard_map/ppermute | solution.py:66
  317.0 31.6 %collective-permute-start.31 = (bf16[2,2,144,1152]{3,2,1,0:T(8,128)(2,1)S(1)}, bf16[2,2,144,1152]{3,2,1,0:T(8,128)(2,1)S(1)}, u32[]{:S(2)}, u32[]{:S(2)}) collective-permute-start(bf16[2,2,144,1152]{3,2,1,0:T(8,128)(2,1)S(1)} %fusion), channel_id=1, source_target_pairs={{0,2},{1,3},{2,0},{3,1},{4,6},{5,7},{6,4},{7,5},{8,10},{9,11},{10,... | collective-permute-start | bytes 3981320 | tf_op jit(solution)/shard_map/ppermute | solution.py:66
  352.3 42.7 %collective-permute-start.33 = (bf16[2,2,144,1152]{3,2,1,0:T(8,128)(2,1)}, bf16[2,2,144,1152]{3,2,1,0:T(8,128)(2,1)S(1)}, u32[]{:S(2)}, u32[]{:S(2)}) collective-permute-start(bf16[2,2,144,1152]{3,2,1,0:T(8,128)(2,1)} %fusion.1), channel_id=1, source_target_pairs={{0,2},{1,3},{2,0},{3,1},{4,6},{5,7},{6,4},{7,5},{8,10},{9,11},{10,... | collective-permute-start | bytes 3981320 | tf_op jit(solution)/shard_map/ppermute | solution.py:66
  356.4 38.6 %collective-permute-start.32 = (bf16[2,144,1152]{2,1,0:T(8,128)(2,1)}, bf16[2,144,1152]{2,1,0:T(8,128)(2,1)}, u32[]{:S(2)}, u32[]{:S(2)}) collective-permute-start(bf16[2,144,1152]{2,1,0:T(8,128)(2,1)} %fusion.7), channel_id=1, source_target_pairs={{0,4},{1,5},{2,6},{3,7},{4,0},{5,1},{6,2},{7,3},{8,12},{9,13},{10,... | collective-permute-start | bytes 1990664 | tf_op jit(solution)/shard_map/ppermute | solution.py:66
  397.4 25.4 %collective-permute-start.34 = (bf16[2,144,1152]{2,1,0:T(8,128)(2,1)}, bf16[2,144,1152]{2,1,0:T(8,128)(2,1)}, u32[]{:S(2)}, u32[]{:S(2)}) collective-permute-start(bf16[2,144,1152]{2,1,0:T(8,128)(2,1)} %fusion.6), channel_id=1, source_target_pairs={{0,4},{1,5},{2,6},{3,7},{4,0},{5,1},{6,2},{7,3},{8,12},{9,13},{10,... | collective-permute-start | bytes 1990664 | tf_op jit(solution)/shard_map/ppermute | solution.py:66
  422.8 17.3 %collective-permute-start.35 = (bf16[2,2,576,1152]{3,2,1,0:T(8,128)(2,1)}, bf16[2,2,576,1152]{3,2,1,0:T(8,128)(2,1)}, u32[]{:S(2)}, u32[]{:S(2)}) collective-permute-start(bf16[2,2,576,1152]{3,2,1,0:T(8,128)(2,1)} %first_weight_grad.2), channel_id=1, source_target_pairs={{0,1},{1,0},{2,3},{3,2},{4,5},{5,4},{6,7},{7,6},{8,9},{9,8},{10,11... | collective-permute-start | bytes 15925256 | tf_op jit(solution)/shard_map/ppermute | solution.py:66
  443.2 32.6 %collective-permute-start.37 = (bf16[2,2,144,1152]{3,2,1,0:T(8,128)(2,1)}, bf16[2,2,144,1152]{3,2,1,0:T(8,128)(2,1)S(1)}, u32[]{:S(2)}, u32[]{:S(2)}) collective-permute-start(bf16[2,2,144,1152]{3,2,1,0:T(8,128)(2,1)} %fusion.3), channel_id=1, source_target_pairs={{0,2},{1,3},{2,0},{3,1},{4,6},{5,7},{6,4},{7,5},{8,10},{9,11},{10,... | collective-permute-start | bytes 3981320 | tf_op jit(solution)/shard_map/ppermute | solution.py:66
  447.1 33.8 %collective-permute-start.36 = (bf16[2,2,144,1152]{3,2,1,0:T(8,128)(2,1)}, bf16[2,2,144,1152]{3,2,1,0:T(8,128)(2,1)S(1)}, u32[]{:S(2)}, u32[]{:S(2)}) collective-permute-start(bf16[2,2,144,1152]{3,2,1,0:T(8,128)(2,1)} %fusion.2), channel_id=1, source_target_pairs={{0,4},{1,5},{2,6},{3,7},{4,0},{5,1},{6,2},{7,3},{8,12},{9,13},{10,... | collective-permute-start | bytes 3981320 | tf_op jit(solution)/shard_map/ppermute | solution.py:66
  448.7 27.1 %collective-permute-start.39 = (bf16[144,1152]{1,0:T(8,128)(2,1)}, bf16[144,1152]{1,0:T(8,128)(2,1)S(1)}, u32[]{:S(2)}, u32[]{:S(2)}) collective-permute-start(bf16[144,1152]{1,0:T(8,128)(2,1)} %get-tuple-element.306), channel_id=1, source_target_pairs={{0,16},{1,17},{2,18},{3,19},{4,20},{5,21},{6,22},{7,23},{8,24},{9,... | collective-permute-start | bytes 995336 | tf_op jit(solution)/shard_map/ppermute | solution.py:66
  450.0 25.8 %collective-permute-start.40 = (bf16[144,1152]{1,0:T(8,128)(2,1)}, bf16[144,1152]{1,0:T(8,128)(2,1)S(1)}, u32[]{:S(2)}, u32[]{:S(2)}) collective-permute-start(bf16[144,1152]{1,0:T(8,128)(2,1)} %get-tuple-element.305), channel_id=1, source_target_pairs={{0,8},{1,9},{2,10},{3,11},{4,12},{5,13},{6,14},{7,15},{8,16},{9,17... | collective-permute-start | bytes 995336 | tf_op jit(solution)/shard_map/ppermute | solution.py:66
  450.3 25.6 %collective-permute-start.38 = (bf16[144,1152]{1,0:T(8,128)(2,1)}, bf16[144,1152]{1,0:T(8,128)(2,1)}, u32[]{:S(2)}, u32[]{:S(2)}) collective-permute-start(bf16[144,1152]{1,0:T(8,128)(2,1)} %fusion.20), channel_id=1, source_target_pairs={{0,24},{1,25},{2,26},{3,27},{4,28},{5,29},{6,30},{7,31},{8,0},{9,1... | collective-permute-start | bytes 995336 | tf_op jit(solution)/shard_map/ppermute | solution.py:66
  483.8 37.0 %collective-permute-start.42 = (bf16[2,144,1152]{2,1,0:T(8,128)(2,1)}, bf16[2,144,1152]{2,1,0:T(8,128)(2,1)}, u32[]{:S(2)}, u32[]{:S(2)}) collective-permute-start(bf16[2,144,1152]{2,1,0:T(8,128)(2,1)} %fusion.4), channel_id=1, source_target_pairs={{0,4},{1,5},{2,6},{3,7},{4,0},{5,1},{6,2},{7,3},{8,12},{9,13},{10,... | collective-permute-start | bytes 1990664 | tf_op jit(solution)/shard_map/ppermute | solution.py:66
  487.8 32.9 %collective-permute-start.41 = (bf16[2,144,1152]{2,1,0:T(8,128)(2,1)}, bf16[2,144,1152]{2,1,0:T(8,128)(2,1)}, u32[]{:S(2)}, u32[]{:S(2)}) collective-permute-start(bf16[2,144,1152]{2,1,0:T(8,128)(2,1)} %fusion.5), channel_id=1, source_target_pairs={{0,2},{1,3},{2,0},{3,1},{4,6},{5,7},{6,4},{7,5},{8,10},{9,11},{10,... | collective-permute-start | bytes 1990664 | tf_op jit(solution)/shard_map/ppermute | solution.py:66
  489.1 43.0 %all-to-all-start.2 = ((bf16[4,4,288,256]{3,2,1,0:T(8,128)(2,1)}), bf16[4,4,288,256]{3,2,1,0:T(8,128)(2,1)S(1)}, u32[]{:S(2)}, u32[]{:S(2)}) async-start(bf16[4,4,288,256]{3,2,1,0:T(8,128)(2,1)} %get-tuple-element.282), calls=%async_computation.2 | async-start | bytes 4718592 | tf_op jit(solution)/shard_map/all_to_all | solution.py:269
  502.0 11.0 %collective-permute-start.44 = (f32[2,29,288]{2,1,0:T(8,128)S(1)}, f32[2,29,288]{2,1,0:T(8,128)S(1)}, u32[]{:S(2)}, u32[]{:S(2)}) collective-permute-start(f32[2,29,288]{2,1,0:T(8,128)S(1)} %slice_add_fusion), channel_id=1, source_target_pairs={{0,8},{1,9},{2,10},{3,11},{4,12},{5,13},{6,14},{7,15},{8,16},{9,17... | collective-permute-start | bytes 200456 | tf_op jit(solution)/shard_map/ppermute | solution.py:66
  526.2 20.1 %collective-permute-start.48 = (bf16[144,1152]{1,0:T(8,128)(2,1)}, bf16[144,1152]{1,0:T(8,128)(2,1)}, u32[]{:S(2)}, u32[]{:S(2)}) collective-permute-start(bf16[144,1152]{1,0:T(8,128)(2,1)} %fusion.17), channel_id=1, source_target_pairs={{0,24},{1,25},{2,26},{3,27},{4,28},{5,29},{6,30},{7,31},{8,0},{9,1... | collective-permute-start | bytes 995336 | tf_op jit(solution)/shard_map/ppermute | solution.py:66
  535.5 26.8 %collective-permute-start.51 = (bf16[144,1152]{1,0:T(8,128)(2,1)}, bf16[144,1152]{1,0:T(8,128)(2,1)}, u32[]{:S(2)}, u32[]{:S(2)}) collective-permute-start(bf16[144,1152]{1,0:T(8,128)(2,1)} %get-tuple-element.304), channel_id=1, source_target_pairs={{0,16},{1,17},{2,18},{3,19},{4,20},{5,21},{6,22},{7,23},{8,24},{9,... | collective-permute-start | bytes 995336 | tf_op jit(solution)/shard_map/ppermute | solution.py:66
  541.2 21.1 %collective-permute-start.52 = (bf16[144,1152]{1,0:T(8,128)(2,1)}, bf16[144,1152]{1,0:T(8,128)(2,1)}, u32[]{:S(2)}, u32[]{:S(2)}) collective-permute-start(bf16[144,1152]{1,0:T(8,128)(2,1)} %get-tuple-element.303), channel_id=1, source_target_pairs={{0,8},{1,9},{2,10},{3,11},{4,12},{5,13},{6,14},{7,15},{8,16},{9,17... | collective-permute-start | bytes 995336 | tf_op jit(solution)/shard_map/ppermute | solution.py:66
  550.2 14.0 %collective-permute-start.50 = (f32[4,144]{1,0:T(4,128)S(1)}, f32[4,144]{1,0:T(4,128)S(1)}, u32[]{:S(2)}, u32[]{:S(2)}) collective-permute-start(f32[4,144]{1,0:T(4,128)S(1)} %add.1025), channel_id=1, source_target_pairs={{0,2},{1,3},{2,0},{3,1},{4,6},{5,7},{6,4},{7,5},{8,10},{9,11},{10,... | collective-permute-start | bytes 6920 | tf_op jit(solution)/shard_map/ppermute | solution.py:66
  (47 other events, 401.9 us)
Sparse Core Ops, SparseCore 0:
  129.7 97.5 all-gather.2
  319.2 169.8 reduce-scatter.1

commit v2 on v1

--- a/solution.py
+++ b/solution.py
@@ -1512,7 +1512,6 @@
     sums = deep_sums(first_parts)
     first_got = along_deep(first_parts, sums)
     output = join_tokens(shape, after(output_got, small_grad), low)
-    small_grad = after(small_grad, *sums)
     small_grad = small_grad + send(small_grad, side_by=1)
     small_grad = after(small_grad, output, input_got)
     small_grad = sum(

time: 596 us -> 595 us (level)
    unnamed x78 -> x70, local copies, waits for them, and re-layouts: 10.6 us -> 12 us
  transfers between devices with their start and end apart: 61 -> 61, of which waited for: 24 -> 26; matrix products, arithmetic and copies ran while one was open for 11% -> 11% of each run, Pallas kernels for 48% -> 48%
where the time goes in v2:
time: 595 us; the launch traced here: 586 us
  Pallas kernels  301 us (51%)
  waiting for transfers between devices  113 us (19%)
  starting transfers between devices  80.4 us (14%)
  other arithmetic  41.7 us (7%)
  local copies, waits for them, and re-layouts  30.7 us (5%)
  between operations  15.1 us (3%)
    pallas_call x22, Pallas kernels, call(): pl.pallas_call(kernel, grid_spec=pltpu.PrefetchScalarGridSpec(num_scalar_...  301 us
    ppermute x56, waiting for transfers between devices, send(): return lax.ppermute(value, both, pairs)  113 us
    ppermute x56, starting transfers between devices, send(): return lax.ppermute(value, both, pairs)  69.3 us
    convert_element_type x8, other arithmetic, sums(): self.total(self.at(axis, k)).astype(low)  21.8 us
    unnamed x70, local copies, waits for them, and re-layouts  12 us
  transfers between devices with their start and end apart: 61, of which 26 were waited for; matrix products, arithmetic and copies ran while one was open for 11% of the time, Pallas kernels for 48%

profile of v2, /device:TPU:0, one launch (start us, length us, event | category | flops | bytes accessed | tf_op | source)
XLA Modules:
  0.0 586.3 jit_solution(11718211767415785138)
XLA Ops:
  9.9 3.0 collective-permute-start.1
  19.7 4.6 collective-permute-done
  32.5 7.9 %collective-permute-done.5 = f32[24,288]{1,0:T(8,128)S(1)} collective-permute-done((f32[24,288]{1,0:T(8,128)S(1)}, f32[24,288]{1,0:T(8,128)S(1)}, u32[]{:S(2)}, u32[]{:S(2)}) %collective-permute-start.5) | collective-permute-done | bytes 27680 | tf_op jit(solution)/shard_map/ppermute | solution.py:66
  49.0 5.4 collective-permute-done.7
  56.9 12.7 %collective-permute-done.11 = f32[29,288]{1,0:T(8,128)S(1)} collective-permute-done((f32[29,288]{1,0:T(8,128)S(1)}, f32[29,288]{1,0:T(8,128)S(1)}, u32[]{:S(2)}, u32[]{:S(2)}) %collective-permute-start.11) | collective-permute-done | bytes 33440 | tf_op jit(solution)/shard_map/ppermute | solution.py:66
  77.2 4.4 lay_small.1
  81.5 6.2 %collective-permute-done.16 = bf16[144,1152]{1,0:T(8,128)(2,1)} collective-permute-done((bf16[144,1152]{1,0:T(8,128)(2,1)}, bf16[144,1152]{1,0:T(8,128)(2,1)}, u32[]{:S(2)}, u32[]{:S(2)}) %collective-permute-start.16) | collective-permute-done | bytes 331808 | tf_op jit(solution)/shard_map/ppermute | solution.py:66
  90.0 6.9 %prepare_tokens.1 = (bf16[1152,1024]{1,0:T(8,128)(2,1)}, bf16[1152,1024]{1,0:T(8,128)(2,1)}) custom-call(s32[8]{0:T(128)} %stack.196.at_ref, bf16[1,4,288,256]{3,2,1,0:T(8,128)(2,1)} %get-tuple-element.305.refs_0_, bf16[1,4,288,256]{3,2,1,0:T(8,128)(2,1)} %copy-done.16, bf16[1,4,288,256]{3,2,1,0:T(8,128)(2,1)} %get-tuple-element.309.refs_2_, ...), custom_call_target="tpu_custom_call" | custom-call | flops 400000000 | tf_op jit(solution)/shard_map/prepare_tokens/pallas_call | solution.py:366
  96.9 3.9 cut_tokens.1
  100.8 3.3 collective-permute-done.15.refs_3_
  114.3 15.1 %project_qkv.1.qkv_ref = bf16[4,896,1024]{2,1,0:T(8,128)(2,1)} custom-call(bf16[576,1152]{1,0:T(8,128)(2,1)} %copy-done.2, bf16[576,1152]{1,0:T(8,128)(2,1)} %collective-permute-done.14.refs_1_, bf16[576,1152]{1,0:T(8,128)(2,1)} %copy-done.1, bf16[576,1152]{1,0:T(8,128)(2,1)} %collective-permute-done.15.refs_3_, ...), custom_call_target="tpu_custom_call" | custom-call | flops 1500000000 | tf_op jit(solution)/shard_map/project_qkv/pallas_call | solution.py:366
  139.7 3.8 all-to-all-start
  144.1 17.4 %attention_forward.1 = (bf16[4,384,1024]{2,1,0:T(8,128)(2,1)}, bf16[8,4,4,128,128]{4,3,2,1,0:T(8,128)(2,1)}) custom-call(bf16[4,896,1024]{2,1,0:T(8,128)(2,1)} %project_qkv.1.qkv_ref, s32[1,1024]{1,0:T(1,128)} %bitcast.231, s32[1024,1]{1,0:T(8,128)} %bitcast.225), custom_call_target="tpu_custom_call" | custom-call | flops 2400000000 | tf_op jit(solution)/shard_map/attention_forward/pallas_call | solution.py:366
  161.5 10.4 %collective-permute-done.25.refs_3_ = bf16[576,1152]{1,0:T(8,128)(2,1)} collective-permute-done((bf16[576,1152]{1,0:T(8,128)(2,1)}, bf16[576,1152]{1,0:T(8,128)(2,1)}, u32[]{:S(2)}, u32[]{:S(2)}) %collective-permute-start.25) | collective-permute-done | bytes 1327136 | tf_op jit(solution)/shard_map/ppermute | solution.py:66
  172.0 6.8 %collective-permute-done.24.refs_1_ = bf16[576,1152]{1,0:T(8,128)(2,1)} collective-permute-done((bf16[576,1152]{1,0:T(8,128)(2,1)}, bf16[576,1152]{1,0:T(8,128)(2,1)}, u32[]{:S(2)}, u32[]{:S(2)}) %collective-permute-start.24) | collective-permute-done | bytes 1327136 | tf_op jit(solution)/shard_map/ppermute | solution.py:66
  180.6 11.5 %project_out.1 = (f32[1152,1024]{1,0:T(8,128)}, bf16[1152,1024]{1,0:T(8,128)(2,1)}, bf16[1152,1024]{1,0:T(8,128)(2,1)}) custom-call(bf16[576,1152]{1,0:T(8,128)(2,1)} %copy-done.2, bf16[576,1152]{1,0:T(8,128)(2,1)} %collective-permute-done.14.refs_1_, bf16[576,1152]{1,0:T(8,128)(2,1)} %copy-done.1, bf16[576,1152]{1,0:T(8,128)(2,1)} %collective-permute-done.15.refs_3_, ...), custom_call_target="tpu_custom_call" | custom-call | flops 1700000000 | tf_op jit(solution)/shard_map/project_out/pallas_call | solution.py:366
  192.2 28.6 %project_up.1 = (bf16[4,1152,1024]{2,1,0:T(8,128)(2,1)}, bf16[4,1152,1024]{2,1,0:T(8,128)(2,1)}) custom-call(bf16[576,1152]{1,0:T(8,128)(2,1)} %constant_dynamic-update-slice_fusion.12.refs_0_, bf16[576,1152]{1,0:T(8,128)(2,1)} %collective-permute-done.24.refs_1_, bf16[576,1152]{1,0:T(8,128)(2,1)} %constant_dynamic-update-slice_fusion.14.refs_2_, ...), custom_call_target="tpu_custom_call" | custom-call | flops 2800000000 | tf_op jit(solution)/shard_map/project_up/pallas_call | solution.py:366
  222.2 6.5 %prepare_upstream.1 = (bf16[1152,1024]{1,0:T(8,128)(2,1)}, bf16[1152,1024]{1,0:T(8,128)(2,1)}, f32[1152,1]{1,0:T(8,128)}) custom-call(s32[8]{0:T(128)} %stack.238.at_ref, bf16[4,4,288,256]{3,2,1,0:T(8,128)(2,1)} %copy-done.5, f32[1152,29]{1,0:T(8,128)} %get-tuple-element.178.refs_4_.refs_10_.table_ref.refs_5_.refs_12_.refs_11_), custom_call_target="tpu_custom_call" | custom-call | flops 400000000 | tf_op jit(solution)/shard_map/prepare_upstream/pallas_call | solution.py:366
  228.7 17.8 %down_weight_grad.1 = bf16[4,8,144,1152]{3,2,1,0:T(8,128)(2,1)} custom-call(s32[32]{0:T(128)} %stack.229.order_ref.refs_0_, bf16[1152,1024]{1,0:T(8,128)(2,1)} %get-tuple-element.223.source_ref.refs_2_, bf16[4,1152,1024]{2,1,0:T(8,128)(2,1)} %get-tuple-element.219.grad_ref.refs_2_), custom_call_target="tpu_custom_call" | custom-call | flops 1000000000 | tf_op jit(solution)/shard_map/down_weight_grad/pallas_call | solution.py:366
  246.5 21.8 %project_down.1 = (bf16[4,4,288,256]{3,2,1,0:T(8,128)(2,1)}, f32[1152,4]{1,0:T(8,128)}) custom-call(s32[8]{0:T(128)} %stack.238.at_ref, s32[32]{0:T(128)} %stack.229.order_ref.refs_0_, bf16[32,144,1152]{2,1,0:T(8,128)(2,1)} %bitcast.204, bf16[4,1152,1024]{2,1,0:T(8,128)(2,1)} %get-tuple-element.219.grad_ref.refs_2_, ...), custom_call_target="tpu_custom_call" | custom-call | flops 2500000000 | tf_op jit(solution)/shard_map/project_down/pallas_call | solution.py:366
  268.3 3.6 all-to-all-start.1
  272.0 21.3 %hidden_backward.1 = (bf16[4,1152,1024]{2,1,0:T(8,128)(2,1)}, f32[4,1152,1]{2,1,0:T(8,128)}) custom-call(s32[32]{0:T(128)} %stack.229.order_ref.refs_0_, bf16[32,144,1152]{2,1,0:T(8,128)(2,1)} %bitcast.205, bf16[1152,1024]{1,0:T(8,128)(2,1)} %get-tuple-element.223.source_ref.refs_2_, bf16[4,1152,1024]{2,1,0:T(8,128)(2,1)} %get-tuple-element.224.refs_3_), custom_call_target="tpu_custom_call" | custom-call | flops 2100000000 | tf_op jit(solution)/shard_map/hidden_backward/pallas_call | solution.py:366
  293.3 10.5 %up_weight_grad.2 = bf16[2,2,576,1152]{3,2,1,0:T(8,128)(2,1)} custom-call(bf16[1152,1024]{1,0:T(8,128)(2,1)} %get-tuple-element.229.refs_8_.source_ref, bf16[4,1152,1024]{2,1,0:T(8,128)(2,1)} %get-tuple-element.232.grad_ref.refs_8_), custom_call_target="tpu_custom_call" | custom-call | flops 1000000000 | tf_op jit(solution)/shard_map/up_weight_grad/pallas_call | solution.py:366
  305.1 10.4 %up_weight_grad.3 = bf16[2,2,576,1152]{3,2,1,0:T(8,128)(2,1)} custom-call(bf16[1152,1024]{1,0:T(8,128)(2,1)} %get-tuple-element.229.refs_8_.source_ref, bf16[4,1152,1024]{2,1,0:T(8,128)(2,1)} %get-tuple-element.232.grad_ref.refs_8_), custom_call_target="tpu_custom_call" | custom-call | flops 1000000000 | tf_op jit(solution)/shard_map/up_weight_grad/pallas_call | solution.py:366
  319.7 26.4 %middle_backward.1 = (f32[1152,1024]{1,0:T(8,128)}, bf16[1152,1024]{1,0:T(8,128)(2,1)}, f32[1152,12]{1,0:T(8,128)}) custom-call(bf16[576,1152]{1,0:T(8,128)(2,1)} %constant_dynamic-update-slice_fusion.12.refs_0_, bf16[576,1152]{1,0:T(8,128)(2,1)} %collective-permute-done.24.refs_1_, bf16[576,1152]{1,0:T(8,128)(2,1)} %constant_dynamic-update-slice_fusion.14.refs_2_, ...), custom_call_target="tpu_custom_call" | custom-call | flops 3000000000 | tf_op jit(solution)/shard_map/middle_backward/pallas_call | solution.py:366
  346.2 3.1 collective-permute-done.31
  349.3 3.6 fusion.1
  357.5 9.4 %attended_backward.1.grad_ref = bf16[4,384,1024]{2,1,0:T(8,128)(2,1)} custom-call(bf16[576,1152]{1,0:T(8,128)(2,1)} %copy-done.2, bf16[576,1152]{1,0:T(8,128)(2,1)} %collective-permute-done.14.refs_1_, bf16[576,1152]{1,0:T(8,128)(2,1)} %copy-done.1, bf16[576,1152]{1,0:T(8,128)(2,1)} %collective-permute-done.15.refs_3_, ...), custom_call_target="tpu_custom_call" | custom-call | flops 900000000 | tf_op jit(solution)/shard_map/attended_backward/pallas_call | solution.py:366
  366.8 28.8 %attention_backward.1.qkv_ref.refs_8_ = bf16[4,896,1024]{2,1,0:T(8,128)(2,1)} custom-call(bf16[4,896,1024]{2,1,0:T(8,128)(2,1)} %project_qkv.1.qkv_ref, bf16[8,4,4,128,128]{4,3,2,1,0:T(8,128)(2,1)} %get-tuple-element.240.probs_ref, bf16[4,384,1024]{2,1,0:T(8,128)(2,1)} %attended_backward.1.grad_ref), custom_call_target="tpu_custom_call" | custom-call | flops 3300000000 | tf_op jit(solution)/shard_map/attention_backward/pallas_call | solution.py:366
  400.1 12.4 %first_weight_grad.2 = bf16[2,2,576,1152]{3,2,1,0:T(8,128)(2,1)} custom-call(bf16[1152,1024]{1,0:T(8,128)(2,1)} %get-tuple-element.261.refs_8_.source_ref, bf16[4,896,1024]{2,1,0:T(8,128)(2,1)} %attention_backward.1.qkv_ref.refs_8_, bf16[1152,1024]{1,0:T(8,128)(2,1)} %get-tuple-element.242.refs_8_.branch_ref, ...), custom_call_target="tpu_custom_call" | custom-call | flops 1200000000 | tf_op jit(solution)/shard_map/first_weight_grad/pallas_call | solution.py:366
  419.5 12.5 %first_weight_grad.3 = bf16[2,2,576,1152]{3,2,1,0:T(8,128)(2,1)} custom-call(bf16[1152,1024]{1,0:T(8,128)(2,1)} %get-tuple-element.261.refs_8_.source_ref, bf16[4,896,1024]{2,1,0:T(8,128)(2,1)} %attention_backward.1.qkv_ref.refs_8_, bf16[1152,1024]{1,0:T(8,128)(2,1)} %get-tuple-element.242.refs_8_.branch_ref, ...), custom_call_target="tpu_custom_call" | custom-call | flops 1200000000 | tf_op jit(solution)/shard_map/first_weight_grad/pallas_call | solution.py:366
  432.1 3.1 fusion.3
  436.0 3.1 fusion.2
  445.8 22.0 %input_backward.1 = (bf16[4,4,288,256]{3,2,1,0:T(8,128)(2,1)}, f32[1152,8]{1,0:T(8,128)}) custom-call(s32[8]{0:T(128)} %stack.238.at_ref, bf16[576,1152]{1,0:T(8,128)(2,1)} %copy-done.2, bf16[576,1152]{1,0:T(8,128)(2,1)} %collective-permute-done.14.refs_1_, bf16[576,1152]{1,0:T(8,128)(2,1)} %copy-done.1, bf16[576,1152]{1,0:T(8,128)(2,1)} %collective-permute-done.15.refs_3_, ...), custom_call_target="tpu_custom_call" | custom-call | flops 2500000000 | tf_op jit(solution)/shard_map/input_backward/pallas_call | solution.py:366
  467.8 4.4 collective-permute-done.39
  473.9 3.6 all-to-all-start.2
  477.5 2.7 fusion.4
  482.6 5.0 lay_small_grads.1
  492.5 7.7 %collective-permute-start.44 = (f32[2,29,288]{2,1,0:T(8,128)S(1)}, f32[2,29,288]{2,1,0:T(8,128)S(1)}, u32[]{:S(2)}, u32[]{:S(2)}) collective-permute-start(f32[2,29,288]{2,1,0:T(8,128)S(1)} %slice_add_fusion), channel_id=1, source_target_pairs={{0,8},{1,9},{2,10},{3,11},{4,12},{5,13},{6,14},{7,15},{8,16},{9,17... | collective-permute-start | bytes 200456 | tf_op jit(solution)/shard_map/ppermute | solution.py:66
  502.4 2.7 collective-permute-start.45
  507.0 3.0 collective-permute-done.45
  510.0 10.3 %collective-permute-done.41 = bf16[2,144,1152]{2,1,0:T(8,128)(2,1)} collective-permute-done((bf16[2,144,1152]{2,1,0:T(8,128)(2,1)}, bf16[2,144,1152]{2,1,0:T(8,128)(2,1)}, u32[]{:S(2)}, u32[]{:S(2)}) %collective-permute-start.41) | collective-permute-done | bytes 663584 | tf_op jit(solution)/shard_map/ppermute | solution.py:66
  525.8 3.9 join_tokens.2
  530.2 3.2 fusion.15
  533.5 6.7 %collective-permute-start.51 = (bf16[144,1152]{1,0:T(8,128)(2,1)}, bf16[144,1152]{1,0:T(8,128)(2,1)S(1)}, u32[]{:S(2)}, u32[]{:S(2)}) collective-permute-start(bf16[144,1152]{1,0:T(8,128)(2,1)} %get-tuple-element.302), channel_id=1, source_target_pairs={{0,16},{1,17},{2,18},{3,19},{4,20},{5,21},{6,22},{7,23},{8,24},{9,... | collective-permute-start | bytes 995336 | tf_op jit(solution)/shard_map/ppermute | solution.py:66
  541.0 4.4 join_tokens.3
  550.1 11.5 %collective-permute-done.51 = bf16[144,1152]{1,0:T(8,128)(2,1)S(1)} collective-permute-done((bf16[144,1152]{1,0:T(8,128)(2,1)}, bf16[144,1152]{1,0:T(8,128)(2,1)S(1)}, u32[]{:S(2)}, u32[]{:S(2)}) %collective-permute-start.51) | collective-permute-done | bytes 331808 | tf_op jit(solution)/shard_map/ppermute | solution.py:66
  569.7 3.6 collective-permute-done.54
  (247 shorter events, 130.3 us)
Async XLA Ops:
  7.2 239.3 %all-gather.3.cloned.1.call-start = ((), (), s32[]{:S(2)}) async-start(), calls=%async_computation.5 | async-start | bytes 10948608 | tf_op jit(solution)/shard_map/all_gather | solution.py:1404
  9.9 16.3 %collective-permute-start.1 = (bf16[1,4,288,256]{3,2,1,0:T(8,128)(2,1)S(1)}, bf16[1,4,288,256]{3,2,1,0:T(8,128)(2,1)S(1)}, u32[]{:S(2)}, u32[]{:S(2)}) collective-permute-start(bf16[1,4,288,256]{3,2,1,0:T(8,128)(2,1)S(1)} %get-tuple-element.307), channel_id=1, source_target_pairs={{0,2},{1,3},{2,0},{3,1},{4,6},{5,7},{6,4},{7,5},{8,10},{9,11},{10,... | collective-permute-start | bytes 1769480 | tf_op jit(solution)/shard_map/ppermute | solution.py:66
  13.2 11.2 %collective-permute-start = (bf16[144,1152]{1,0:T(8,128)(2,1)S(1)}, bf16[144,1152]{1,0:T(8,128)(2,1)S(1)}, u32[]{:S(2)}, u32[]{:S(2)}) collective-permute-start(bf16[144,1152]{1,0:T(8,128)(2,1)S(1)} %concatenate.40), channel_id=1, source_target_pairs={{0,8},{1,9},{2,10},{3,11},{4,12},{5,13},{6,14},{7,15},{8,16},{9,17... | collective-permute-start | bytes 995336 | tf_op jit(solution)/shard_map/ppermute | solution.py:66
  27.6 14.6 %collective-permute-start.4 = (bf16[1,4,288,256]{3,2,1,0:T(8,128)(2,1)S(1)}, bf16[1,4,288,256]{3,2,1,0:T(8,128)(2,1)S(1)}, u32[]{:S(2)}, u32[]{:S(2)}) collective-permute-start(bf16[1,4,288,256]{3,2,1,0:T(8,128)(2,1)S(1)} %dynamic-slice_bitcast_fusion.2), channel_id=1, source_target_pairs={{0,2},{1,3},{2,0},{3,1},{4,6},{5,7},{6,4},{7,5},{8,10},{9,11},{10,... | collective-permute-start | bytes 1769480 | tf_op jit(solution)/shard_map/ppermute | solution.py:66
  29.4 11.0 %collective-permute-start.3 = (bf16[144,1152]{1,0:T(8,128)(2,1)S(1)}, bf16[144,1152]{1,0:T(8,128)(2,1)S(1)}, u32[]{:S(2)}, u32[]{:S(2)}) collective-permute-start(bf16[144,1152]{1,0:T(8,128)(2,1)S(1)} %collective-permute-done), channel_id=1, source_target_pairs={{0,8},{1,9},{2,10},{3,11},{4,12},{5,13},{6,14},{7,15},{8,16},{9,17... | collective-permute-start | bytes 995336 | tf_op jit(solution)/shard_map/ppermute | solution.py:66
  42.1 12.4 %collective-permute-start.7 = (f32[24,288]{1,0:T(8,128)S(1)}, f32[24,288]{1,0:T(8,128)S(1)}, u32[]{:S(2)}, u32[]{:S(2)}) collective-permute-start(f32[24,288]{1,0:T(8,128)S(1)} %add.845), channel_id=1, source_target_pairs={{0,16},{1,17},{2,18},{3,19},{4,20},{5,21},{6,22},{7,23},{8,24},{9,... | collective-permute-start | bytes 82952 | tf_op jit(solution)/shard_map/ppermute | solution.py:66
  44.6 9.9 %collective-permute-start.6 = (bf16[144,1152]{1,0:T(8,128)(2,1)S(1)}, bf16[144,1152]{1,0:T(8,128)(2,1)S(1)}, u32[]{:S(2)}, u32[]{:S(2)}) collective-permute-start(bf16[144,1152]{1,0:T(8,128)(2,1)S(1)} %collective-permute-done.3), channel_id=1, source_target_pairs={{0,8},{1,9},{2,10},{3,11},{4,12},{5,13},{6,14},{7,15},{8,16},{9,17... | collective-permute-start | bytes 995336 | tf_op jit(solution)/shard_map/ppermute | solution.py:66
  47.3 25.2 %collective-permute-start.10 = (bf16[2,4,288,256]{3,2,1,0:T(8,128)(2,1)}, bf16[2,4,288,256]{3,2,1,0:T(8,128)(2,1)}, u32[]{:S(2)}, u32[]{:S(2)}) collective-permute-start(bf16[2,4,288,256]{3,2,1,0:T(8,128)(2,1)} %pad_maximum_fusion), channel_id=1, source_target_pairs={{0,1},{1,0},{2,3},{3,2},{4,5},{5,4},{6,7},{7,6},{8,9},{9,8},{10,11... | collective-permute-start | bytes 3538952 | tf_op jit(solution)/shard_map/ppermute | solution.py:66
  47.5 24.2 %collective-permute-start.9 = (bf16[288,1152]{1,0:T(8,128)(2,1)S(1)}, bf16[288,1152]{1,0:T(8,128)(2,1)S(1)}, u32[]{:S(2)}, u32[]{:S(2)}) collective-permute-start(bf16[288,1152]{1,0:T(8,128)(2,1)S(1)} %constant_dynamic-update-slice_fusion.2), channel_id=1, source_target_pairs={{0,4},{1,5},{2,6},{3,7},{4,0},{5,1},{6,2},{7,3},{8,12},{9,13},{10,... | collective-permute-start | bytes 1990664 | tf_op jit(solution)/shard_map/ppermute | solution.py:66
  54.6 17.1 %collective-permute-start.8 = (bf16[288,1152]{1,0:T(8,128)(2,1)S(1)}, bf16[288,1152]{1,0:T(8,128)(2,1)S(1)}, u32[]{:S(2)}, u32[]{:S(2)}) collective-permute-start(bf16[288,1152]{1,0:T(8,128)(2,1)S(1)} %constant_dynamic-update-slice_fusion), channel_id=1, source_target_pairs={{0,2},{1,3},{2,0},{3,1},{4,6},{5,7},{6,4},{7,5},{8,10},{9,11},{10,... | collective-permute-start | bytes 1990664 | tf_op jit(solution)/shard_map/ppermute | solution.py:66
  56.3 13.4 %collective-permute-start.11 = (f32[29,288]{1,0:T(8,128)S(1)}, f32[29,288]{1,0:T(8,128)S(1)}, u32[]{:S(2)}, u32[]{:S(2)}) collective-permute-start(f32[29,288]{1,0:T(8,128)S(1)} %get-tuple-element.315), channel_id=1, source_target_pairs={{0,2},{1,3},{2,0},{3,1},{4,6},{5,7},{6,4},{7,5},{8,10},{9,11},{10,... | collective-permute-start | bytes 100232 | tf_op jit(solution)/shard_map/ppermute | solution.py:66
  56.9 14.8 %collective-permute-start.13 = (bf16[144,1152]{1,0:T(8,128)(2,1)}, bf16[144,1152]{1,0:T(8,128)(2,1)}, u32[]{:S(2)}, u32[]{:S(2)}) collective-permute-start(bf16[144,1152]{1,0:T(8,128)(2,1)} %param.24), channel_id=1, source_target_pairs={{0,8},{1,9},{2,10},{3,11},{4,12},{5,13},{6,14},{7,15},{8,16},{9,17... | collective-permute-start | bytes 995336 | tf_op jit(solution)/shard_map/ppermute | solution.py:66
  72.7 31.4 %collective-permute-start.15 = (bf16[576,1152]{1,0:T(8,128)(2,1)S(1)}, bf16[576,1152]{1,0:T(8,128)(2,1)}, u32[]{:S(2)}, u32[]{:S(2)}) collective-permute-start(bf16[576,1152]{1,0:T(8,128)(2,1)S(1)} %constant_dynamic-update-slice_fusion.6.refs_2_), channel_id=1, source_target_pairs={{0,2},{1,3},{2,0},{3,1},{4,6},{5,7},{6,4},{7,5},{8,10},{9,11},{10,... | collective-permute-start | bytes 3981320 | tf_op jit(solution)/shard_map/ppermute | solution.py:66
  74.5 31.3 %collective-permute-start.14 = (bf16[576,1152]{1,0:T(8,128)(2,1)S(1)}, bf16[576,1152]{1,0:T(8,128)(2,1)}, u32[]{:S(2)}, u32[]{:S(2)}) collective-permute-start(bf16[576,1152]{1,0:T(8,128)(2,1)S(1)} %constant_dynamic-update-slice_fusion.4.refs_0_), channel_id=1, source_target_pairs={{0,4},{1,5},{2,6},{3,7},{4,0},{5,1},{6,2},{7,3},{8,12},{9,13},{10,... | collective-permute-start | bytes 3981320 | tf_op jit(solution)/shard_map/ppermute | solution.py:66
  76.0 11.6 %collective-permute-start.16 = (bf16[144,1152]{1,0:T(8,128)(2,1)}, bf16[144,1152]{1,0:T(8,128)(2,1)}, u32[]{:S(2)}, u32[]{:S(2)}) collective-permute-start(bf16[144,1152]{1,0:T(8,128)(2,1)} %collective-permute-done.13), channel_id=1, source_target_pairs={{0,8},{1,9},{2,10},{3,11},{4,12},{5,13},{6,14},{7,15},{8,16},{9,17... | collective-permute-start | bytes 995336 | tf_op jit(solution)/shard_map/ppermute | solution.py:66
  76.7 36.1 %collective-permute-start.20 = (bf16[576,1152]{1,0:T(8,128)(2,1)S(1)}, bf16[576,1152]{1,0:T(8,128)(2,1)}, u32[]{:S(2)}, u32[]{:S(2)}) collective-permute-start(bf16[576,1152]{1,0:T(8,128)(2,1)S(1)} %constant_dynamic-update-slice_fusion.6.refs_2_), channel_id=1, source_target_pairs={{0,1},{1,0},{2,3},{3,2},{4,5},{5,4},{6,7},{7,6},{8,9},{9,8},{10,11... | collective-permute-start | bytes 3981320 | tf_op jit(solution)/shard_map/ppermute | solution.py:66
  76.7 37.6 %collective-permute-start.18 = (bf16[576,1152]{1,0:T(8,128)(2,1)S(1)}, bf16[576,1152]{1,0:T(8,128)(2,1)}, u32[]{:S(2)}, u32[]{:S(2)}) collective-permute-start(bf16[576,1152]{1,0:T(8,128)(2,1)S(1)} %constant_dynamic-update-slice_fusion.4.refs_0_), channel_id=1, source_target_pairs={{0,1},{1,0},{2,3},{3,2},{4,5},{5,4},{6,7},{7,6},{8,9},{9,8},{10,11... | collective-permute-start | bytes 3981320 | tf_op jit(solution)/shard_map/ppermute | solution.py:66
  87.7 13.1 %collective-permute-start.17 = (bf16[144,1152]{1,0:T(8,128)(2,1)}, bf16[144,1152]{1,0:T(8,128)(2,1)S(1)}, u32[]{:S(2)}, u32[]{:S(2)}) collective-permute-start(bf16[144,1152]{1,0:T(8,128)(2,1)} %collective-permute-done.16), channel_id=1, source_target_pairs={{0,8},{1,9},{2,10},{3,11},{4,12},{5,13},{6,14},{7,15},{8,16},{9,17... | collective-permute-start | bytes 995336 | tf_op jit(solution)/shard_map/ppermute | solution.py:66
  108.8 20.6 %collective-permute-start.23 = (bf16[288,1152]{1,0:T(8,128)(2,1)}, bf16[288,1152]{1,0:T(8,128)(2,1)}, u32[]{:S(2)}, u32[]{:S(2)}) collective-permute-start(bf16[288,1152]{1,0:T(8,128)(2,1)} %constant_dynamic-update-slice_fusion.10), channel_id=1, source_target_pairs={{0,2},{1,3},{2,0},{3,1},{4,6},{5,7},{6,4},{7,5},{8,10},{9,11},{10,... | collective-permute-start | bytes 1990664 | tf_op jit(solution)/shard_map/ppermute | solution.py:66
  112.8 16.7 %collective-permute-start.22 = (bf16[288,1152]{1,0:T(8,128)(2,1)}, bf16[288,1152]{1,0:T(8,128)(2,1)S(1)}, u32[]{:S(2)}, u32[]{:S(2)}) collective-permute-start(bf16[288,1152]{1,0:T(8,128)(2,1)} %constant_dynamic-update-slice_fusion.8), channel_id=1, source_target_pairs={{0,4},{1,5},{2,6},{3,7},{4,0},{5,1},{6,2},{7,3},{8,12},{9,13},{10,... | collective-permute-start | bytes 1990664 | tf_op jit(solution)/shard_map/ppermute | solution.py:66
  132.5 39.5 %collective-permute-start.25 = (bf16[576,1152]{1,0:T(8,128)(2,1)}, bf16[576,1152]{1,0:T(8,128)(2,1)}, u32[]{:S(2)}, u32[]{:S(2)}) collective-permute-start(bf16[576,1152]{1,0:T(8,128)(2,1)} %constant_dynamic-update-slice_fusion.14.refs_2_), channel_id=1, source_target_pairs={{0,2},{1,3},{2,0},{3,1},{4,6},{5,7},{6,4},{7,5},{8,10},{9,11},{10,... | collective-permute-start | bytes 3981320 | tf_op jit(solution)/shard_map/ppermute | solution.py:66
  137.0 41.8 %collective-permute-start.24 = (bf16[576,1152]{1,0:T(8,128)(2,1)}, bf16[576,1152]{1,0:T(8,128)(2,1)}, u32[]{:S(2)}, u32[]{:S(2)}) collective-permute-start(bf16[576,1152]{1,0:T(8,128)(2,1)} %constant_dynamic-update-slice_fusion.12.refs_0_), channel_id=1, source_target_pairs={{0,4},{1,5},{2,6},{3,7},{4,0},{5,1},{6,2},{7,3},{8,12},{9,13},{10,... | collective-permute-start | bytes 3981320 | tf_op jit(solution)/shard_map/ppermute | solution.py:66
  139.7 81.2 %all-to-all-start = ((bf16[4,4,288,256]{3,2,1,0:T(8,128)(2,1)}), bf16[4,4,288,256]{3,2,1,0:T(8,128)(2,1)S(1)}, u32[]{:S(2)}, u32[]{:S(2)}) async-start(bf16[4,4,288,256]{3,2,1,0:T(8,128)(2,1)} %cut_tokens.1), calls=%async_computation | async-start | bytes 4718592 | tf_op jit(solution)/shard_map/all_to_all | solution.py:269
  143.5 48.7 %collective-permute-start.28 = (bf16[576,1152]{1,0:T(8,128)(2,1)}, bf16[576,1152]{1,0:T(8,128)(2,1)}, u32[]{:S(2)}, u32[]{:S(2)}) collective-permute-start(bf16[576,1152]{1,0:T(8,128)(2,1)} %constant_dynamic-update-slice_fusion.14.refs_2_), channel_id=1, source_target_pairs={{0,1},{1,0},{2,3},{3,2},{4,5},{5,4},{6,7},{7,6},{8,9},{9,8},{10,11... | collective-permute-start | bytes 3981320 | tf_op jit(solution)/shard_map/ppermute | solution.py:66
  144.0 48.1 %collective-permute-start.26 = (bf16[576,1152]{1,0:T(8,128)(2,1)}, bf16[576,1152]{1,0:T(8,128)(2,1)}, u32[]{:S(2)}, u32[]{:S(2)}) collective-permute-start(bf16[576,1152]{1,0:T(8,128)(2,1)} %constant_dynamic-update-slice_fusion.12.refs_0_), channel_id=1, source_target_pairs={{0,1},{1,0},{2,3},{3,2},{4,5},{5,4},{6,7},{7,6},{8,9},{9,8},{10,11... | collective-permute-start | bytes 3981320 | tf_op jit(solution)/shard_map/ppermute | solution.py:66
  178.8 13.4 %collective-permute-start.27 = (bf16[576,1152]{1,0:T(8,128)(2,1)}, bf16[576,1152]{1,0:T(8,128)(2,1)}, u32[]{:S(2)}, u32[]{:S(2)}) collective-permute-start(bf16[576,1152]{1,0:T(8,128)(2,1)} %collective-permute-done.24.refs_1_), channel_id=1, source_target_pairs={{0,1},{1,0},{2,3},{3,2},{4,5},{5,4},{6,7},{7,6},{8,9},{9,8},{10,11... | collective-permute-start | bytes 3981320 | tf_op jit(solution)/shard_map/ppermute | solution.py:66
  178.8 13.4 %collective-permute-start.29 = (bf16[576,1152]{1,0:T(8,128)(2,1)}, bf16[576,1152]{1,0:T(8,128)(2,1)}, u32[]{:S(2)}, u32[]{:S(2)}) collective-permute-start(bf16[576,1152]{1,0:T(8,128)(2,1)} %collective-permute-done.25.refs_3_), channel_id=1, source_target_pairs={{0,1},{1,0},{2,3},{3,2},{4,5},{5,4},{6,7},{7,6},{8,9},{9,8},{10,11... | collective-permute-start | bytes 3981320 | tf_op jit(solution)/shard_map/ppermute | solution.py:66
  268.3 35.5 %all-to-all-start.1 = ((bf16[4,4,288,256]{3,2,1,0:T(8,128)(2,1)}), bf16[4,4,288,256]{3,2,1,0:T(8,128)(2,1)S(1)}, u32[]{:S(2)}, u32[]{:S(2)}) async-start(bf16[4,4,288,256]{3,2,1,0:T(8,128)(2,1)} %get-tuple-element.226), calls=%async_computation.1 | async-start | bytes 4718592 | tf_op jit(solution)/shard_map/all_to_all | solution.py:269
  271.9 233.2 %reduce-scatter.2.cloned.1.call-start = ((), (), s32[]{:S(2)}) async-start(), calls=%async_computation.4 | async-start | bytes 10948608 | tf_op jit(solution)/shard_map/reduce_scatter | solution.py:1423
  303.7 11.8 %collective-permute-start.30 = (bf16[2,2,576,1152]{3,2,1,0:T(8,128)(2,1)}, bf16[2,2,576,1152]{3,2,1,0:T(8,128)(2,1)}, u32[]{:S(2)}, u32[]{:S(2)}) collective-permute-start(bf16[2,2,576,1152]{3,2,1,0:T(8,128)(2,1)} %up_weight_grad.2), channel_id=1, source_target_pairs={{0,1},{1,0},{2,3},{3,2},{4,5},{5,4},{6,7},{7,6},{8,9},{9,8},{10,11... | collective-permute-start | bytes 15925256 | tf_op jit(solution)/shard_map/ppermute | solution.py:66
  317.7 31.5 %collective-permute-start.31 = (bf16[2,2,144,1152]{3,2,1,0:T(8,128)(2,1)S(1)}, bf16[2,2,144,1152]{3,2,1,0:T(8,128)(2,1)S(1)}, u32[]{:S(2)}, u32[]{:S(2)}) collective-permute-start(bf16[2,2,144,1152]{3,2,1,0:T(8,128)(2,1)S(1)} %fusion), channel_id=1, source_target_pairs={{0,2},{1,3},{2,0},{3,1},{4,6},{5,7},{6,4},{7,5},{8,10},{9,11},{10,... | collective-permute-start | bytes 3981320 | tf_op jit(solution)/shard_map/ppermute | solution.py:66
  352.9 44.2 %collective-permute-start.33 = (bf16[2,2,144,1152]{3,2,1,0:T(8,128)(2,1)}, bf16[2,2,144,1152]{3,2,1,0:T(8,128)(2,1)S(1)}, u32[]{:S(2)}, u32[]{:S(2)}) collective-permute-start(bf16[2,2,144,1152]{3,2,1,0:T(8,128)(2,1)} %fusion.1), channel_id=1, source_target_pairs={{0,2},{1,3},{2,0},{3,1},{4,6},{5,7},{6,4},{7,5},{8,10},{9,11},{10,... | collective-permute-start | bytes 3981320 | tf_op jit(solution)/shard_map/ppermute | solution.py:66
  356.9 38.7 %collective-permute-start.32 = (bf16[2,144,1152]{2,1,0:T(8,128)(2,1)}, bf16[2,144,1152]{2,1,0:T(8,128)(2,1)S(1)}, u32[]{:S(2)}, u32[]{:S(2)}) collective-permute-start(bf16[2,144,1152]{2,1,0:T(8,128)(2,1)} %fusion.7), channel_id=1, source_target_pairs={{0,4},{1,5},{2,6},{3,7},{4,0},{5,1},{6,2},{7,3},{8,12},{9,13},{10,... | collective-permute-start | bytes 1990664 | tf_op jit(solution)/shard_map/ppermute | solution.py:66
  399.4 15.4 %collective-permute-start.34 = (bf16[2,144,1152]{2,1,0:T(8,128)(2,1)}, bf16[2,144,1152]{2,1,0:T(8,128)(2,1)}, u32[]{:S(2)}, u32[]{:S(2)}) collective-permute-start(bf16[2,144,1152]{2,1,0:T(8,128)(2,1)} %fusion.6), channel_id=1, source_target_pairs={{0,4},{1,5},{2,6},{3,7},{4,0},{5,1},{6,2},{7,3},{8,12},{9,13},{10,... | collective-permute-start | bytes 1990664 | tf_op jit(solution)/shard_map/ppermute | solution.py:66
  414.9 17.2 %collective-permute-start.35 = (bf16[2,2,576,1152]{3,2,1,0:T(8,128)(2,1)}, bf16[2,2,576,1152]{3,2,1,0:T(8,128)(2,1)}, u32[]{:S(2)}, u32[]{:S(2)}) collective-permute-start(bf16[2,2,576,1152]{3,2,1,0:T(8,128)(2,1)} %first_weight_grad.2), channel_id=1, source_target_pairs={{0,1},{1,0},{2,3},{3,2},{4,5},{5,4},{6,7},{7,6},{8,9},{9,8},{10,11... | collective-permute-start | bytes 15925256 | tf_op jit(solution)/shard_map/ppermute | solution.py:66
  435.2 37.0 %collective-permute-start.37 = (bf16[2,2,144,1152]{3,2,1,0:T(8,128)(2,1)}, bf16[2,2,144,1152]{3,2,1,0:T(8,128)(2,1)S(1)}, u32[]{:S(2)}, u32[]{:S(2)}) collective-permute-start(bf16[2,2,144,1152]{3,2,1,0:T(8,128)(2,1)} %fusion.3), channel_id=1, source_target_pairs={{0,2},{1,3},{2,0},{3,1},{4,6},{5,7},{6,4},{7,5},{8,10},{9,11},{10,... | collective-permute-start | bytes 3981320 | tf_op jit(solution)/shard_map/ppermute | solution.py:66
  439.1 33.7 %collective-permute-start.36 = (bf16[2,2,144,1152]{3,2,1,0:T(8,128)(2,1)}, bf16[2,2,144,1152]{3,2,1,0:T(8,128)(2,1)S(1)}, u32[]{:S(2)}, u32[]{:S(2)}) collective-permute-start(bf16[2,2,144,1152]{3,2,1,0:T(8,128)(2,1)} %fusion.2), channel_id=1, source_target_pairs={{0,4},{1,5},{2,6},{3,7},{4,0},{5,1},{6,2},{7,3},{8,12},{9,13},{10,... | collective-permute-start | bytes 3981320 | tf_op jit(solution)/shard_map/ppermute | solution.py:66
  440.6 31.6 %collective-permute-start.39 = (bf16[144,1152]{1,0:T(8,128)(2,1)}, bf16[144,1152]{1,0:T(8,128)(2,1)}, u32[]{:S(2)}, u32[]{:S(2)}) collective-permute-start(bf16[144,1152]{1,0:T(8,128)(2,1)} %get-tuple-element.304), channel_id=1, source_target_pairs={{0,16},{1,17},{2,18},{3,19},{4,20},{5,21},{6,22},{7,23},{8,24},{9,... | collective-permute-start | bytes 995336 | tf_op jit(solution)/shard_map/ppermute | solution.py:66
  441.4 30.8 %collective-permute-start.40 = (bf16[144,1152]{1,0:T(8,128)(2,1)}, bf16[144,1152]{1,0:T(8,128)(2,1)}, u32[]{:S(2)}, u32[]{:S(2)}) collective-permute-start(bf16[144,1152]{1,0:T(8,128)(2,1)} %get-tuple-element.303), channel_id=1, source_target_pairs={{0,8},{1,9},{2,10},{3,11},{4,12},{5,13},{6,14},{7,15},{8,16},{9,17... | collective-permute-start | bytes 995336 | tf_op jit(solution)/shard_map/ppermute | solution.py:66
  442.9 29.3 %collective-permute-start.38 = (bf16[144,1152]{1,0:T(8,128)(2,1)}, bf16[144,1152]{1,0:T(8,128)(2,1)}, u32[]{:S(2)}, u32[]{:S(2)}) collective-permute-start(bf16[144,1152]{1,0:T(8,128)(2,1)} %fusion.20), channel_id=1, source_target_pairs={{0,24},{1,25},{2,26},{3,27},{4,28},{5,29},{6,30},{7,31},{8,0},{9,1... | collective-permute-start | bytes 995336 | tf_op jit(solution)/shard_map/ppermute | solution.py:66
  473.9 55.9 %all-to-all-start.2 = ((bf16[4,4,288,256]{3,2,1,0:T(8,128)(2,1)}), bf16[4,4,288,256]{3,2,1,0:T(8,128)(2,1)S(1)}, u32[]{:S(2)}, u32[]{:S(2)}) async-start(bf16[4,4,288,256]{3,2,1,0:T(8,128)(2,1)} %get-tuple-element.281), calls=%async_computation.2 | async-start | bytes 4718592 | tf_op jit(solution)/shard_map/all_to_all | solution.py:269
  489.0 21.0 %collective-permute-start.42 = (bf16[2,144,1152]{2,1,0:T(8,128)(2,1)}, bf16[2,144,1152]{2,1,0:T(8,128)(2,1)}, u32[]{:S(2)}, u32[]{:S(2)}) collective-permute-start(bf16[2,144,1152]{2,1,0:T(8,128)(2,1)} %fusion.4), channel_id=1, source_target_pairs={{0,4},{1,5},{2,6},{3,7},{4,0},{5,1},{6,2},{7,3},{8,12},{9,13},{10,... | collective-permute-start | bytes 1990664 | tf_op jit(solution)/shard_map/ppermute | solution.py:66
  489.9 30.4 %collective-permute-start.41 = (bf16[2,144,1152]{2,1,0:T(8,128)(2,1)}, bf16[2,144,1152]{2,1,0:T(8,128)(2,1)}, u32[]{:S(2)}, u32[]{:S(2)}) collective-permute-start(bf16[2,144,1152]{2,1,0:T(8,128)(2,1)} %fusion.5), channel_id=1, source_target_pairs={{0,2},{1,3},{2,0},{3,1},{4,6},{5,7},{6,4},{7,5},{8,10},{9,11},{10,... | collective-permute-start | bytes 1990664 | tf_op jit(solution)/shard_map/ppermute | solution.py:66
  523.4 22.0 %collective-permute-start.48 = (bf16[144,1152]{1,0:T(8,128)(2,1)}, bf16[144,1152]{1,0:T(8,128)(2,1)S(1)}, u32[]{:S(2)}, u32[]{:S(2)}) collective-permute-start(bf16[144,1152]{1,0:T(8,128)(2,1)} %fusion.17), channel_id=1, source_target_pairs={{0,24},{1,25},{2,26},{3,27},{4,28},{5,29},{6,30},{7,31},{8,0},{9,1... | collective-permute-start | bytes 995336 | tf_op jit(solution)/shard_map/ppermute | solution.py:66
  529.8 11.1 %collective-permute-start.47 = (f32[29,288]{1,0:T(8,128)S(1)}, f32[29,288]{1,0:T(8,128)S(1)}, u32[]{:S(2)}, u32[]{:S(2)}) collective-permute-start(f32[29,288]{1,0:T(8,128)S(1)} %slice_bitcast_fusion.1), channel_id=1, source_target_pairs={{0,2},{1,3},{2,0},{3,1},{4,6},{5,7},{6,4},{7,5},{8,10},{9,11},{10,... | collective-permute-start | bytes 100232 | tf_op jit(solution)/shard_map/ppermute | solution.py:66
  533.5 28.1 %collective-permute-start.51 = (bf16[144,1152]{1,0:T(8,128)(2,1)}, bf16[144,1152]{1,0:T(8,128)(2,1)S(1)}, u32[]{:S(2)}, u32[]{:S(2)}) collective-permute-start(bf16[144,1152]{1,0:T(8,128)(2,1)} %get-tuple-element.302), channel_id=1, source_target_pairs={{0,16},{1,17},{2,18},{3,19},{4,20},{5,21},{6,22},{7,23},{8,24},{9,... | collective-permute-start | bytes 995336 | tf_op jit(solution)/shard_map/ppermute | solution.py:66
  540.1 21.5 %collective-permute-start.52 = (bf16[144,1152]{1,0:T(8,128)(2,1)}, bf16[144,1152]{1,0:T(8,128)(2,1)S(1)}, u32[]{:S(2)}, u32[]{:S(2)}) collective-permute-start(bf16[144,1152]{1,0:T(8,128)(2,1)} %get-tuple-element.301), channel_id=1, source_target_pairs={{0,8},{1,9},{2,10},{3,11},{4,12},{5,13},{6,14},{7,15},{8,16},{9,17... | collective-permute-start | bytes 995336 | tf_op jit(solution)/shard_map/ppermute | solution.py:66
  548.7 14.5 %collective-permute-start.50 = (f32[4,144]{1,0:T(4,128)S(1)}, f32[4,144]{1,0:T(4,128)S(1)}, u32[]{:S(2)}, u32[]{:S(2)}) collective-permute-start(f32[4,144]{1,0:T(4,128)S(1)} %add.1017), channel_id=1, source_target_pairs={{0,2},{1,3},{2,0},{3,1},{4,6},{5,7},{6,4},{7,5},{8,10},{9,11},{10,... | collective-permute-start | bytes 6920 | tf_op jit(solution)/shard_map/ppermute | solution.py:66
  (43 other events, 338.3 us)
Sparse Core Ops, SparseCore 0:
  129.7 97.5 all-gather.2
  304.3 165.4 reduce-scatter.1
